TPU v7x, 32 devices: a whole 2x2x4 slice. The times are simulated.
32 devices in a mesh: dp: 4 (over z), seq: 8 (over y, x, core).
Axes of the slice: x: 2, y: 2, z: 4, core: 2. Of those that a mesh axis runs over, the one named last changes fastest.
Arguments:
- block_in: bfloat16 [2, 4, 2048, 512], P(None, 'dp', 'seq'), may hold values from -14 to 14
- cotangent: bfloat16 [2, 4, 2048, 512], P(None, 'dp', 'seq'), may hold values from -6 to 6
- doc_lengths: int32 [2, 4, 4], P(None, 'dp'), may hold values from 1 to 1920, 2048 in all within a row
- norm_gain: float32 [2, 512], replicated, may hold values from 0.25 to 1.75
- norm_shift: float32 [2, 512], replicated, may hold values from -4 to 4
- log_step: float32 [2, 384], replicated, may hold values from -0.3 to 0.3
- lam_re: float32 [2, 384], replicated, may hold values from -1 to 0, as said below
- lam_im: float32 [2, 384], replicated, may hold values from -2048 to 2048
- b_proj: bfloat16 [2, 512, 768], replicated, may hold values from -0.25 to 0.25
- c_proj: bfloat16 [2, 768, 512], replicated, may hold values from -0.09375 to 0.09375
- d_skip: float32 [2, 512], replicated, may hold values from -3 to 3
- w_gate: bfloat16 [2, 512, 512], replicated, may hold values from -0.25 to 0.25
Outputs:
- block_out: bfloat16 [2, 4, 2048, 512], P(None, 'dp', 'seq')
- grad_input: float32 [2, 4, 2048, 512], P(None, 'dp', 'seq')
- grad_norm_gain: float32 [2, 512], replicated
- grad_norm_shift: float32 [2, 512], replicated
- grad_log_step: float32 [2, 384], replicated
- grad_lam_re: float32 [2, 384], replicated
- grad_lam_im: float32 [2, 384], replicated
- grad_b_proj: float32 [2, 512, 768], replicated
- grad_c_proj: float32 [2, 768, 512], replicated
- grad_d_skip: float32 [2, 512], replicated
- grad_w_gate: float32 [2, 512, 512], replicated
Inputs may be any that keep to these rules, and one draw needn't show every extreme that they name: `doc_lengths`: in every row the 4 lengths sum to 2048 and the largest is exactly 1920. `lam_re`: negative.
All inputs are finite; a program needn't handle non-finite values.
Results may differ from a plain program's by a relative error of at most 0.019.
Values sent between devices are 32-bit elements; how exact they have to be, the bound alone decides.
No kernel may reach another device: no remote copies, remote signals or barrier semaphores. Data moves between devices by JAX's collectives and lax.ppermute only.
A program may use at most 128 MiB of HBM per device.

v0:
```python
import functools

import jax
import jax.numpy as jnp
from jax import lax
from jax.experimental import pallas as pl
from jax.experimental.pallas import tpu as pltpu
from jax.sharding import PartitionSpec as P

f32, bf16 = jnp.float32, jnp.bfloat16
epsilon = 1e-05
tanh_scale = 0.7978845608028654
cubic_term = 0.044715
LANES = 128
CHUNKS = 8
ROWS = 32
VMEM_LIMIT = 16 * 1024 * 1024


def dot(left, right, contract=(1, 0)):
    return lax.dot_general(
        left, right, (((contract[0],), (contract[1],)), ((), ())), preferred_element_type=f32
    )


def reorder(span, inverse):
    shape = (span, span)
    kept, moved = (1, 0) if inverse else (0, 1)
    row = lax.broadcasted_iota(jnp.int32, shape, kept)
    position = lax.broadcasted_iota(jnp.int32, shape, moved)
    source = (row & (CHUNKS - 1)) * (span // CHUNKS) + (row >> 3)
    return jnp.where(position == source, 1.0, 0.0).astype(bf16)


def row_loop(count, body, init=0, step=ROWS):
    def one(index, carry):
        return body(pl.multiple_of(index * step, step), carry)

    return lax.fori_loop(0, count // step, one, init)


def documents(here, batches, span, count):
    mine = here[0]
    first = mine * span
    out = []
    for batch in range(batches):
        begins, ends, so_far = [], [], 0
        docs = (here.shape[0] - 2) // batches
        for doc in range(docs):
            begins.append(so_far)
            so_far = so_far + here[2 + batch * docs + doc]
            ends.append(so_far)
        before, after = 0, 2 * count * span
        for begin, end in zip(begins, ends):
            before = jnp.maximum(before, jnp.where(begin < first, begin, 0))
            after = jnp.minimum(after, jnp.where(end > first + span, end, 2 * count * span))
        after = jnp.where(mine == count - 1, 0, after)
        out.append(begins + ends + [before, after, first, mine])
    return out


def place_documents(cfg, place):
    layer, reverse, batches, span, groups, tokens, count = cfg
    return documents(place, batches, span, count)


def keep_of(meta, batch, base, step, backward):
    docs = (len(meta[batch]) - 4) // 2
    off = docs if backward else 0
    late = 1 if backward else 0
    stop = base == meta[batch][off] - step - late
    for doc in range(1, docs):
        stop = jnp.logical_or(stop, base == meta[batch][off + doc] - step - late)
    return jnp.where(stop, 0.0, 1.0)


def base_positions(meta, steps):
    return meta[0][-2] + lax.broadcasted_iota(jnp.int32, (CHUNKS, LANES), 0) * steps


def lanes_of(index, half=0):
    return slice(half + index * LANES, half + (index + 1) * LANES)


def coef_tiles(value, groups):
    return [
        tuple(jnp.broadcast_to(part[:, lanes_of(q)], (CHUNKS, LANES)) for part in value)
        for q in range(groups)
    ]


def constants(disc, layer):
    dec_re, dec_im, inj_re, inj_im = (part[layer : layer + 1, :] for part in disc)
    return (dec_re, dec_im), (inj_re, inj_im)


def times(a, b):
    return (a[0] * b[0] - a[1] * b[1], a[0] * b[1] + a[1] * b[0])


def power(value, exponent):
    for _ in range(exponent.bit_length() - 1):
        value = times(value, value)
    return value


def conj(value):
    return (value[0], -value[1])


def scan(meta, source, inject, dec, batches, span, groups, reverse, masks_reverse, init, extra, visit):
    steps = span // CHUNKS
    half = groups * LANES
    base = base_positions(meta, steps)

    def pair(index, carry):
        states, more = carry
        states = list(states)
        first = steps - 2 - 2 * index if reverse else 2 * index
        start = pl.multiple_of(first * CHUNKS, 2 * CHUNKS)
        order = (1, 0) if reverse else (0, 1)
        for batch in range(batches):
            keeps = [keep_of(meta, batch, base, first + j, masks_reverse) for j in (0, 1)]
            for q in range(groups):
                rows = pl.ds(batch * span + start, 2 * CHUNKS)
                src_re = source[rows, lanes_of(q)]
                src_im = source[rows, lanes_of(q, half)]
                state = states[batch * groups + q]
                found = [None, None]
                for j in order:
                    part = (
                        src_re[j * CHUNKS : (j + 1) * CHUNKS],
                        src_im[j * CHUNKS : (j + 1) * CHUNKS],
                    )
                    push = times(inject[q], part) if inject is not None else part
                    held = times((keeps[j] * dec[q][0], keeps[j] * dec[q][1]), state)
                    state = (held[0] + push[0], held[1] + push[1])
                    found[j] = state
                states[batch * groups + q] = state
                more = visit(more, batch, q, first, start, found, (src_re, src_im))
            more = visit(more, batch, None, first, start, keeps, None)
        return tuple(states), more

    return lax.fori_loop(0, steps // 2, pair, (tuple(init), extra), unroll=2)


def zero_states(batches, groups):
    zero = jnp.zeros((CHUNKS, LANES), f32)
    return [(zero, zero)] * (batches * groups)


def local_ends(meta, source, inject, dec, batches, span, groups, reverse, prefix, total):
    ones = tuple(jnp.ones((CHUNKS, LANES), f32) for _ in range(batches))

    def visit(more, batch, q, first, start, found, src):
        if q is not None:
            return more
        return tuple(
            value * found[0] * found[1] if at == batch else value for at, value in enumerate(more)
        )

    dec_chunk = coef_tiles(power(dec, span // CHUNKS), groups)
    ends, kept = scan(
        meta, source, inject, coef_tiles(dec, groups), batches, span, groups, reverse, reverse,
        zero_states(batches, groups), ones, visit,
    )
    half = groups * LANES
    row = lax.broadcasted_iota(jnp.int32, (CHUNKS, LANES), 0)
    for batch in range(batches):
        for q in range(groups):
            end = ends[batch * groups + q]
            decay = (kept[batch] * dec_chunk[q][0], kept[batch] * dec_chunk[q][1])
            for shift in (1, 2, 4):
                turn = CHUNKS - shift if reverse else shift
                valid = row < CHUNKS - shift if reverse else row >= shift
                before = [pltpu.roll(value, turn, 0) for value in (*end, *decay)]
                from_before = times(decay, (before[0], before[1]))
                end = (
                    end[0] + jnp.where(valid, from_before[0], 0.0),
                    end[1] + jnp.where(valid, from_before[1], 0.0),
                )
                longer = times(decay, (before[2], before[3]))
                decay = (
                    jnp.where(valid, longer[0], decay[0]),
                    jnp.where(valid, longer[1], decay[1]),
                )
            rows = slice(batch * CHUNKS, (batch + 1) * CHUNKS)
            prefix[0, rows, lanes_of(q)] = end[0]
            prefix[0, rows, lanes_of(q, half)] = end[1]
            prefix[1, rows, lanes_of(q)] = decay[0]
            prefix[1, rows, lanes_of(q, half)] = decay[1]
            last = 0 if reverse else CHUNKS - 1
            total[batch : batch + 1, lanes_of(q)] = end[0][last : last + 1]
            total[batch : batch + 1, lanes_of(q, half)] = end[1][last : last + 1]


def chunk_carries(meta, gathered, dec, prefix, batches, span, groups, reverse):
    count = gathered.shape[0]
    half = groups * LANES
    dec_span = power(dec, span)
    row = lax.broadcasted_iota(jnp.int32, (CHUNKS, LANES), 0)
    mine = meta[0][-1]
    out = []
    for batch in range(batches):

        def add(at, so_far, batch=batch):
            away = count - 2 - at
            if reverse:
                other = mine + 1 + away
                reaches = meta[batch][-3] > other * span
            else:
                other = mine - 1 - away
                reaches = meta[batch][-4] < (mine - away) * span
            other = jnp.clip(other, 0, count - 1)
            value = jnp.where(reaches, gathered[other, pl.ds(batch, 1), :], 0.0)
            moved = times(dec_span, so_far)
            return (moved[0] + value[:, :half], moved[1] + value[:, half:])

        zero = jnp.zeros((1, half), f32)
        enter = lax.fori_loop(0, count - 1, add, (zero, zero), unroll=count <= 8)
        rows = slice(batch * CHUNKS, (batch + 1) * CHUNKS)
        for q in range(groups):
            own = tuple(jnp.broadcast_to(part[:, lanes_of(q)], (CHUNKS, LANES)) for part in enter)
            end = (prefix[0, rows, lanes_of(q)], prefix[0, rows, lanes_of(q, half)])
            decay = (prefix[1, rows, lanes_of(q)], prefix[1, rows, lanes_of(q, half)])
            moved = times(decay, own)
            turn, first = (CHUNKS - 1, CHUNKS - 1) if reverse else (1, 0)
            out.append(
                tuple(
                    jnp.where(row == first, own[i], pltpu.roll(end[i] + moved[i], turn, 0))
                    for i in (0, 1)
                )
            )
    return out


def add_sums(target, batches, sums):
    for kind, per_batch in enumerate(sums):
        for batch in range(batches):
            target[kind * batches + batch : kind * batches + batch + 1, :] = jnp.sum(
                per_batch[batch], axis=0, keepdims=True
            )


def fold(value):
    return sum(value[i : i + CHUNKS] for i in range(CHUNKS, value.shape[0], CHUNKS)) + value[:CHUNKS]


def order_rows(batches, span, inverse, x, out):
    turn = reorder(span, inverse)
    for batch in range(batches):
        rows = slice(batch * span, (batch + 1) * span)
        out[rows, :] = dot(turn, x[rows, :]).astype(bf16)


def first_sums(batches, span, x, stats):
    width = x.shape[1]
    sums, squares = [], []
    for batch in range(batches):

        def body(start, carry, batch=batch):
            value = x[pl.ds(batch * span + start, ROWS), :].astype(f32)
            return carry[0] + fold(value), carry[1] + fold(value * value)

        zero = jnp.zeros((CHUNKS, width), f32)
        one, two = row_loop(span, body, (zero, zero))
        sums.append(one)
        squares.append(two)
    add_sums(stats, batches, (sums, squares))


def enter_layer(
    cfg, place, stats, hidden, norms, disc, b_proj, u, drive, prefix, total, norm
):
    layer, reverse, batches, span, groups, tokens, count = cfg
    sums = sum(part[...] for part in stats)
    average = sums[:batches] / tokens
    spread = sums[batches:] / tokens - average * average
    scale = lax.rsqrt(spread + epsilon)
    norm[:batches, :] = average
    norm[batches:, :] = scale
    gain_now, shift_now = norms[layer : layer + 1, :], norms[layer + 2 : layer + 3, :]
    for batch in range(batches):

        def body(start, carry, batch=batch):
            rows = pl.ds(batch * span + start, ROWS)
            normed = (hidden[rows, :].astype(f32) - average[batch : batch + 1]) * scale[
                batch : batch + 1
            ]
            u[rows, :] = (normed * gain_now + shift_now).astype(bf16)
            return carry

        row_loop(span, body)
    drive[...] = dot(u[...], b_proj[layer])
    meta = place_documents(cfg, place)
    dec, inj = constants(disc, layer)
    local_ends(
        meta, drive, coef_tiles(inj, groups), dec, batches, span, groups, reverse, prefix, total
    )


def finish_states(cfg, meta, ends, prefix, disc, drive, states, states_low):
    layer, reverse, batches, span, groups, tokens, count = cfg
    half = groups * LANES
    padded = span + CHUNKS
    dec, inj = constants(disc, layer)
    init = chunk_carries(meta, ends, dec, prefix, batches, span, groups, reverse)
    for batch in range(batches):
        edge = batch * padded + (span if reverse else 0)
        for q in range(groups):
            states[edge : edge + CHUNKS, lanes_of(q)] = init[batch * groups + q][0]
            states[edge : edge + CHUNKS, lanes_of(q, half)] = init[batch * groups + q][1]

    def visit(more, batch, q, first, start, found, src):
        if q is not None:
            for part, off in ((0, 0), (1, half)):
                both = jnp.concatenate([found[0][part], found[1][part]], axis=0)
                at = batch * padded + (0 if reverse else CHUNKS)
                states[pl.ds(at + start, 2 * CHUNKS), lanes_of(q, off)] = both
                states_low[pl.ds(batch * span + start, 2 * CHUNKS), lanes_of(q, off)] = both.astype(
                    bf16
                )
        return more

    scan(
        meta, drive, coef_tiles(inj, groups), coef_tiles(dec, groups), batches, span, groups,
        reverse, reverse, init, 0, visit,
    )


def forward_finish(
    cfg, meta, ends, prefix, disc, drive, u, hidden, c_proj, norms, w_gate,
    states, states_low, act, sig, slope, result, wide, emit,
):
    layer, reverse, batches, span, groups, tokens, count = cfg
    finish_states(cfg, meta, ends, prefix, disc, drive, states, states_low)
    wide[...] = dot(states_low[...], c_proj[layer])
    skip = norms[layer + 4 : layer + 5, :]

    def body(start, carry):
        rows = pl.ds(start, ROWS)
        mixed = wide[rows, :] + skip * u[rows, :].astype(f32)
        square = mixed * mixed
        th = jnp.tanh(tanh_scale * (mixed + cubic_term * square * mixed))
        half_one = 0.5 * (1.0 + th)
        act[rows, :] = (mixed * half_one).astype(bf16)
        slope[rows, :] = half_one + 0.5 * mixed * (1.0 - th * th) * tanh_scale * (
            1.0 + 3.0 * cubic_term * square
        )
        return carry

    row_loop(batches * span, body)
    wide[...] = dot(act[...], w_gate[layer])
    sums, squares = [], []
    for batch in range(batches):

        def gate(start, carry, batch=batch):
            rows = pl.ds(batch * span + start, ROWS)
            sig_now = 0.5 + 0.5 * jnp.tanh(0.5 * wide[rows, :])
            sig[rows, :] = sig_now
            value = hidden[rows, :].astype(f32) + act[rows, :].astype(f32) * sig_now
            result[rows, :] = value.astype(result.dtype)
            if emit is None:
                return carry
            return carry[0] + fold(value), carry[1] + fold(value * value)

        zero = jnp.zeros((CHUNKS, wide.shape[1]), f32)
        one, two = row_loop(span, gate, (zero, zero))
        sums.append(one)
        squares.append(two)
    if emit is not None:
        add_sums(emit, batches, (sums, squares))


def backward_start(
    cfg, meta, grad_out, disc, u, c_proj, w_gate, states_low, act, sig, slope,
    grad_gate, grad_mixed, grad_low, source, prefix, total, grad_d, wide,
):
    layer, reverse, batches, span, groups, tokens, count = cfg

    def body(start, carry):
        rows = pl.ds(start, ROWS)
        sig_now = sig[rows, :]
        grad_gate[rows, :] = (
            grad_out[rows, :].astype(f32) * act[rows, :].astype(f32) * sig_now * (1.0 - sig_now)
        ).astype(bf16)
        return carry

    row_loop(batches * span, body)
    wide[...] = dot(grad_gate[...], w_gate[layer], (1, 1))

    def mixed(start, carry):
        rows = pl.ds(start, ROWS)
        value = (grad_out[rows, :].astype(f32) * sig[rows, :] + wide[rows, :]) * slope[rows, :]
        grad_mixed[rows, :] = value
        grad_low[rows, :] = value.astype(bf16)
        return carry + fold(value * u[rows, :].astype(f32))

    gd = row_loop(batches * span, mixed, jnp.zeros((CHUNKS, wide.shape[1]), f32))
    grad_d[...] = jnp.sum(gd, axis=0, keepdims=True)
    source[...] = dot(grad_low[...], c_proj[layer], (1, 1))
    local_ends(
        meta, source, None, conj(constants(disc, layer)[0]), batches, span, groups, not reverse,
        prefix, total,
    )


def middle_forward(
    cfg, place, ends, prefix, disc, drive, u, hidden, c_proj, norms, w_gate,
    states, states_low, act, sig, slope, result, stats, wide,
):
    meta = place_documents(cfg, place)
    forward_finish(
        cfg, meta, ends, prefix, disc, drive, u, hidden, c_proj, norms, w_gate,
        states, states_low, act, sig, slope, result, wide, stats,
    )


def turn_around(
    cfg, place, ends, prefix, disc, drive, u, hidden, c_proj, norms, w_gate, ordered_cot,
    result, states, states_low, act, grad_gate, grad_mixed, grad_low, source,
    back_prefix, total, grad_d, sig, slope, wide,
):
    layer, reverse, batches, span, groups, tokens, count = cfg
    meta = place_documents(cfg, place)
    forward_finish(
        cfg, meta, ends, prefix, disc, drive, u, hidden, c_proj, norms, w_gate,
        states, states_low, act, sig, slope, result, wide, None,
    )
    backward_start(
        cfg, meta, ordered_cot, disc, u, c_proj, w_gate, states_low, act, sig, slope,
        grad_gate, grad_mixed, grad_low, source, back_prefix, total, grad_d, wide,
    )


def backward_finish(
    cfg, place, ends, prefix, disc, source, drive, states, u, grad_mixed, grad_d, hidden, norm,
    norms, b_proj, grad_proj, grad_u, stats, small,
):
    layer, reverse, batches, span, groups, tokens, count = cfg
    half = groups * LANES
    padded = span + CHUNKS
    steps = span // CHUNKS
    meta = place_documents(cfg, place)
    dec, inj = constants(disc, layer)
    dec = conj(dec)
    init = chunk_carries(meta, ends, dec, prefix, batches, span, groups, not reverse)
    inj = coef_tiles(inj, groups)
    base = base_positions(meta, steps)
    zero = jnp.zeros((CHUNKS, LANES), f32)

    def visit(more, batch, q, first, start, found, src):
        if q is None:
            return more
        more = list(more)
        rows = pl.ds(batch * span + start, 2 * CHUNKS)
        drive_re, drive_im = drive[rows, lanes_of(q)], drive[rows, lanes_of(q, half)]
        before = pl.ds(batch * padded + start + (CHUNKS if reverse else 0), 2 * CHUNKS)
        prior_re, prior_im = states[before, lanes_of(q)], states[before, lanes_of(q, half)]
        dec_re, dec_im, inj_re, inj_im = more[q]
        out_re, out_im = [], []
        for j in (0, 1):
            part = slice(j * CHUNKS, (j + 1) * CHUNKS)
            adj_re, adj_im = found[j]
            keep = keep_of(meta, batch, base, first + j, reverse)
            kept_re, kept_im = keep * adj_re, keep * adj_im
            dec_re = dec_re + kept_re * prior_re[part] + kept_im * prior_im[part]
            dec_im = dec_im + kept_im * prior_re[part] - kept_re * prior_im[part]
            inj_re = inj_re + adj_re * drive_re[part] + adj_im * drive_im[part]
            inj_im = inj_im + adj_im * drive_re[part] - adj_re * drive_im[part]
            out_re.append(inj[q][0] * adj_re + inj[q][1] * adj_im)
            out_im.append(inj[q][0] * adj_im - inj[q][1] * adj_re)
        grad_proj[rows, lanes_of(q)] = jnp.concatenate(out_re, axis=0).astype(bf16)
        grad_proj[rows, lanes_of(q, half)] = jnp.concatenate(out_im, axis=0).astype(bf16)
        more[q] = (dec_re, dec_im, inj_re, inj_im)
        return tuple(more)

    _, sums = scan(
        meta, source, None, coef_tiles(dec, groups), batches, span, groups,
        not reverse, not reverse, init, ((zero,) * 4,) * groups, visit,
    )
    small[...] = jnp.zeros_like(small)
    for q in range(groups):
        for kind in range(4):
            small[kind : kind + 1, lanes_of(q)] = jnp.sum(sums[q][kind], axis=0, keepdims=True)
    small[4:5, :] = grad_d[...]
    grad_u[...] = dot(grad_proj[...], b_proj[layer], (1, 1))
    skip = norms[layer + 4 : layer + 5, :]
    plain, times_normed = [], []
    for batch in range(batches):
        average = norm[batch : batch + 1, :]
        scale = norm[batches + batch : batches + batch + 1, :]

        def body(start, carry, batch=batch, average=average, scale=scale):
            rows = pl.ds(batch * span + start, ROWS)
            value = grad_u[rows, :] + grad_mixed[rows, :] * skip
            grad_u[rows, :] = value
            normed = (hidden[rows, :].astype(f32) - average) * scale
            return carry[0] + fold(value), carry[1] + fold(value * normed)

        zero_sum = jnp.zeros((CHUNKS, grad_u.shape[1]), f32)
        one, two = row_loop(span, body, (zero_sum, zero_sum))
        plain.append(one)
        times_normed.append(two)
    add_sums(stats, batches, (plain, times_normed))


def backward_finish_last(cfg, *refs):
    ins, before, (grad_proj, grad_u, sums) = refs[:-4], refs[-4], refs[-3:]
    sums[...] = jnp.zeros_like(sums)
    sums[2 * CHUNKS :, :] = before[...]
    backward_finish(
        cfg, *ins, grad_proj, grad_u, sums.at[pl.ds(0, CHUNKS)], sums.at[pl.ds(CHUNKS, CHUNKS)]
    )


def norm_backward(cfg, stats, grad_out, grad_u, hidden, norm, norms, store, shared):
    layer, reverse, batches, span, groups, tokens, count = cfg
    sums = sum(part[...] for part in stats)
    shared[0:1, :] = jnp.sum(sums[batches:], axis=0, keepdims=True)
    shared[1:2, :] = jnp.sum(sums[:batches], axis=0, keepdims=True)
    gain_now = norms[layer : layer + 1, :]
    for batch in range(batches):
        average = norm[batch : batch + 1, :]
        scale = norm[batches + batch : batches + batch + 1, :]
        plain = gain_now * sums[batch : batch + 1] / tokens
        slanted = gain_now * sums[batches + batch : batches + batch + 1] / tokens

        def body(start, carry, batch=batch, average=average, scale=scale, plain=plain, slanted=slanted):
            rows = pl.ds(batch * span + start, ROWS)
            normed = (hidden[rows, :].astype(f32) - average) * scale
            value = grad_out[rows, :].astype(f32) + scale * (
                grad_u[rows, :] * gain_now - plain - normed * slanted
            )
            store(rows, value)
            return carry

        row_loop(span, body)


def between_layers(
    cfg, lower, place, stats, upper_out, upper_u, upper_hidden, upper_norm, norms,
    disc, u, c_proj, w_gate, states_low, act, sig, slope,
    grad_out, shared, grad_gate, grad_mixed, grad_low, source, prefix, total, grad_d, wide,
):
    def store(rows, value):
        grad_out[rows, :] = value

    norm_backward(cfg, stats, upper_out, upper_u, upper_hidden, upper_norm, norms, store, shared)
    meta = place_documents(lower, place)
    backward_start(
        lower, meta, grad_out, disc, u, c_proj, w_gate, states_low, act, sig, slope,
        grad_gate, grad_mixed, grad_low, source, prefix, total, grad_d, wide,
    )


def last_step(cfg, stats, grad_out, grad_u, hidden, norm, norms, target, shared, ordered):
    layer, reverse, batches, span, groups, tokens, count = cfg
    planes = target.shape[1] // LANES

    def store(rows, value):
        for plane in range(planes):
            ordered[plane, rows, :] = value[:, lanes_of(plane)]

    norm_backward(cfg, stats, grad_out, grad_u, hidden, norm, norms, store, shared)
    steps = span // CHUNKS
    for batch in range(batches):
        for chunk in range(CHUNKS):
            at = batch * span
            for plane in range(planes):
                target[at + chunk * steps : at + (chunk + 1) * steps, lanes_of(plane)] = ordered[
                    plane, pl.ds(at + chunk, steps, stride=CHUNKS), :
                ]


def half_weights(core, refs, own, sent):
    for target, half in ((own, core), (sent, 1 - core)):
        at = 0
        for left, right in refs:
            rows = left.shape[1] // 2
            cols = pl.ds(pl.multiple_of(half * rows, LANES), rows)
            target[at : at + rows, :] = dot(left[:, cols], right[...], (0, 0))
            at += rows


def all_weights(here, act, grad_gate, states_low, grad_low, grad_proj, u, own, sent):
    refs = ((act, grad_gate), (states_low, grad_low), (grad_proj, u))
    half_weights(lax.rem(here[0], 2), refs, own, sent)


def gate_weights(here, act, grad_gate, states_low, grad_low, own, sent):
    half_weights(lax.rem(here[0], 2), ((act, grad_gate), (states_low, grad_low)), own, sent)


def input_weights(here, grad_proj, u, own, sent):
    half_weights(lax.rem(here[0], 2), ((grad_proj, u),), own, sent)


def run(body, name, args, outs, scratch=(), scalars=1):
    vmem, smem = pl.BlockSpec(memory_space=pltpu.VMEM), pl.BlockSpec(memory_space=pltpu.SMEM)
    specs = tuple(
        jax.tree.map(lambda _, at=at: smem if at < scalars else vmem, arg)
        for at, arg in enumerate(args)
    )
    return pl.pallas_call(
        body,
        name=name,
        out_shape=tuple(jax.ShapeDtypeStruct(*out) for out in outs),
        in_specs=specs,
        out_specs=(vmem,) * len(outs),
        scratch_shapes=[pltpu.VMEM(*entry) for entry in scratch],
        compiler_params=pltpu.CompilerParams(vmem_limit_bytes=VMEM_LIMIT),
    )(*args)


def put_in_place(layer, here, halves, outs, before, pieces=1):
    width, states = outs[0][0][1], outs[1][0][1]
    rows_w, rows_c = width // 2, states // 2
    vmem, count = pl.BlockSpec(memory_space=pltpu.VMEM), len(halves)

    def half(step, here):
        core = lax.rem(here[0], 2)
        spots = [1 - core if other else core for other, _ in halves]
        return spots[0] if count == 1 else jnp.where(step == 0, *spots)

    blocks = (
        pl.BlockSpec((1, rows_w, width), lambda i, here: (layer, half(i, here), 0)),
        pl.BlockSpec((1, rows_c, width), lambda i, here: (layer, half(i, here), 0)),
        pl.BlockSpec((1, width, rows_c), lambda i, here: (layer, 0, half(i, here))),
    )

    def body(here, *refs):
        grad_w, grad_c, grad_b = refs[-3:]
        for now in range(count):

            @pl.when(pl.program_id(0) == now)
            def _(source=refs[now]):
                gates, inputs = (rows_w + rows_c) // pieces, rows_c // pieces
                columns = []
                for piece in range(pieces):
                    at, row = piece * (gates + inputs), piece * gates
                    turn = min(max(rows_w - row, 0), gates)
                    if turn:
                        grad_w[0, row : row + turn, :] = source[at : at + turn, :]
                    if turn < gates:
                        to = row + turn - rows_w
                        grad_c[0, to : to + gates - turn, :] = source[at + turn : at + gates, :]
                    columns.append(source[at + gates : at + gates + inputs, :])
                grad_b[0] = jnp.concatenate(columns, axis=0).T

    return pl.pallas_call(
        body,
        name="put_in_place",
        out_shape=tuple(jax.ShapeDtypeStruct(*out) for out in outs),
        grid_spec=pltpu.PrefetchScalarGridSpec(
            num_scalar_prefetch=1,
            grid=(count,),
            in_specs=[vmem] * count + [pl.BlockSpec(memory_space=pl.ANY)] * len(before),
            out_specs=blocks,
        ),
        input_output_aliases={1 + count + i: i for i in range(len(before))},
        compiler_params=pltpu.CompilerParams(vmem_limit_bytes=VMEM_LIMIT),
    )(here, *(rows for _, rows in halves), *before)


def axis_parts():
    count, depth = lax.axis_size("seq"), lax.axis_size("dp")
    return (("seq", 2, 1, count), ("seq", count // 2, 2, count), ("dp", depth, 1, depth))


def shifted(value, part, away):
    name, size, stride, count = part
    pairs = []
    for i in range(count):
        place = (i // stride) % size
        pairs.append((i, i + ((place + away) % size - place) * stride))
    return lax.ppermute(value, name, pairs)


def add_by_shifts(value, parts, *earlier):
    for number, part in enumerate(parts):
        if number:
            value = sum(terms[1:], terms[0])
        if number == len(parts) - 1:
            value, *earlier = lax.optimization_barrier((value, *earlier))
        terms = [value] + [shifted(value, part, away) for away in range(1, part[1])]
    return terms, *earlier


def bits_of(size, stride=1):
    bits = []
    while size > 1:
        bits.append(stride)
        size, stride = size // 2, stride * 2
    return bits


def plane_bits():
    chip_bits = bits_of(lax.axis_size("seq") // 2, 2)
    middle = (len(chip_bits) + 1) // 2
    inner, outer = chip_bits[:middle], chip_bits[middle:]
    return list(zip(inner + outer, outer + inner))


def swap(value, axis, bit):
    return lax.ppermute(value, axis, [(i, i ^ bit) for i in range(lax.axis_size(axis))])


def bit_at(here, axis, bit):
    return lax.rem(lax.div(here[0 if axis == "seq" else 1], bit), 2)


def rows_at(half, rows):
    return pl.ds(pl.multiple_of(half * rows, CHUNKS), rows)


def fold_cores(bits, here, *refs):
    terms, targets = refs[:-4], refs[-4:]
    rows, cols = targets[0].shape
    for side in (0, 1):
        kept, sent = targets[2 * side : 2 * side + 2]
        where = slice(side * cols, (side + 1) * cols)
        bit = bit_at(here, "seq", bits[side])
        for half in (0, 1):

            @pl.when(bit == half)
            def _(half=half, kept=kept, sent=sent, where=where):
                start = 0
                for own, found in zip(terms[0::2], terms[1::2]):
                    for part, target in ((half, kept), (1 - half, sent)):
                        low = max(start, part * rows)
                        high = min(start + own.shape[0], (part + 1) * rows)
                        if low < high:
                            source = slice(low - start, high - start)
                            target[low - part * rows : high - part * rows, :] = (
                                own[source, where] + found[source, where]
                            )
                    start += own.shape[0]


def fold_sides(bits, here, *refs):
    targets, blocks = refs[-4:], refs[:-4]
    for side in (0, 1):
        kept, sent = targets[2 * side : 2 * side + 2]
        half, start = bit_at(here, "seq", bits[side]), 0
        for at in range(0, len(blocks), 4):
            own, found = blocks[at + 2 * side : at + 2 * side + 2]
            rows = own.shape[0] // 2
            to = slice(start, start + rows)
            kept[to, :] = own[rows_at(half, rows), :] + found[rows_at(half, rows), :]
            sent[to, :] = own[rows_at(1 - half, rows), :] + found[rows_at(1 - half, rows), :]
            start += rows


def fold_join(bit, here, left, found_left, right, found_right, kept, sent):
    rows, cols = kept.shape[0], left.shape[1]
    half = bit_at(here, "dp", bit)
    for side, (own, found) in enumerate(((left, found_left), (right, found_right))):
        where = slice(side * cols, (side + 1) * cols)
        kept[:, where] = own[rows_at(half, rows), :] + found[rows_at(half, rows), :]
        sent[:, where] = own[rows_at(1 - half, rows), :] + found[rows_at(1 - half, rows), :]


def fold_depth(bit, here, own, found, kept, sent):
    half, rows = bit_at(here, "dp", bit), kept.shape[0]
    kept[...] = own[rows_at(half, rows), :] + found[rows_at(half, rows), :]
    sent[...] = own[rows_at(1 - half, rows), :] + found[rows_at(1 - half, rows), :]


def add_two(own, found, out):
    out[...] = own[...] + found[...]


def unfold(bit, here, own, found, out):
    half, rows = bit_at(here, "dp", bit), own.shape[0]
    out[rows_at(half, rows), :] = own[...]
    out[rows_at(1 - half, rows), :] = found[...]


def unfold_split(bit, here, own, found, left, right):
    half, rows, cols = bit_at(here, "dp", bit), own.shape[0], left.shape[1]
    for side, out in enumerate((left, right)):
        where = slice(side * cols, (side + 1) * cols)
        out[rows_at(half, rows), :] = own[:, where]
        out[rows_at(1 - half, rows), :] = found[:, where]


def unfold_sides(bits, joined, here, *refs):
    for side in (0, 1):
        own, found = refs[2 * side : 2 * side + 2]
        half, (rows, cols) = bit_at(here, "seq", bits[side]), own.shape
        out = refs[4] if joined else refs[4 + side]
        where = slice(side * cols, (side + 1) * cols) if joined else slice(0, cols)
        out[rows_at(half, rows), where] = own[...]
        out[rows_at(1 - half, rows), where] = found[...]


def link_call(body, here, args, shapes):
    name = body.func.__name__
    return run(body, name, (here, *args), tuple((shape, f32) for shape in shapes))


class LinkSum:
    def __init__(self, here, terms):
        self.here, self.plane = here, plane_bits()
        self.depth = bits_of(lax.axis_size("dp"))
        rows = sum(term.shape[0] for term in terms[::2])
        self.shape = (rows // 2, terms[0].shape[1] // 2)
        self.parts = link_call(
            functools.partial(fold_cores, self.plane[0]), here, terms, (self.shape,) * 4
        )

    def swap_plane(self, stage):
        (left, right), pieces = self.plane[stage], self.parts
        self.parts = (
            pieces[0], swap(pieces[1], "seq", left), pieces[2], swap(pieces[3], "seq", right)
        )

    def down_plane(self, stage, *others):
        parts, rows, cols = list(self.parts), *self.shape
        for other in others:
            parts += other.parts
            rows += other.shape[0]
        self.shape = (rows // 2, cols)
        body = functools.partial(fold_sides, self.plane[stage])
        self.parts = link_call(body, self.here, parts, (self.shape,) * 4)

    def down_join(self):
        rows, cols = self.shape
        self.shape = (rows // 2, 2 * cols)
        body = functools.partial(fold_join, self.depth[0])
        self.parts = link_call(body, self.here, self.parts, (self.shape,) * 2)

    def swap_depth(self, stage):
        self.parts = (self.parts[0], swap(self.parts[1], "dp", self.depth[stage]))

    def down_depth(self, stage):
        rows, cols = self.shape
        self.shape = (rows // 2, cols)
        body = functools.partial(fold_depth, self.depth[stage])
        self.parts = link_call(body, self.here, self.parts, (self.shape,) * 2)

    def middle(self):
        (value,) = run(add_two, "add_two", self.parts, ((self.shape, f32),), scalars=0)
        self.parts = (value, value)

    def up_depth(self, stage):
        rows, cols = self.shape
        self.shape = (rows * 2, cols)
        body = functools.partial(unfold, self.depth[stage])
        (value,) = link_call(body, self.here, self.parts, (self.shape,))
        self.parts = (value, value)

    def up_split(self):
        rows, cols = self.shape
        self.shape = (rows * 2, cols // 2)
        body = functools.partial(unfold_split, self.depth[0])
        left, right = link_call(body, self.here, self.parts, (self.shape,) * 2)
        self.parts = (left, left, right, right)

    def up_plane(self, stage):
        rows, cols = self.shape
        if stage:
            self.shape = (rows * 2, cols)
            body = functools.partial(unfold_sides, self.plane[stage], False)
            left, right = link_call(body, self.here, self.parts, (self.shape,) * 2)
            self.parts = (left, left, right, right)
        else:
            self.shape = (rows * 2, cols * 2)
            body = functools.partial(unfold_sides, self.plane[stage], True)
            self.parts = link_call(body, self.here, self.parts, (self.shape,))

    def after(self, *values):
        self.parts, values = lax.optimization_barrier((self.parts, values))
        return values

    def to_depth(self):
        for stage in range(2, len(self.plane)):
            self.swap_plane(stage - 1)
            self.down_plane(stage)
        self.swap_plane(len(self.plane) - 1)

    def scatter_depth(self):
        for stage in range(len(self.depth) - 1):
            if stage:
                self.down_depth(stage)
            self.swap_depth(stage)

    def swap_whole(self):
        self.parts = (self.parts[0], swap(self.parts[0], "dp", self.depth[-1]))

    def gather_depth(self):
        for stage in range(len(self.depth) - 2, 0, -1):
            self.swap_depth(stage)
            self.up_depth(stage)
        self.swap_depth(0)


def wait_for(*things):
    sums = [thing for thing in things if isinstance(thing, LinkSum)]
    values = [thing for thing in things if not isinstance(thing, LinkSum)]
    parts, values = lax.optimization_barrier(([entry.parts for entry in sums], values))
    for entry, part in zip(sums, parts):
        entry.parts = part
    return values


def discretize(lam_re, lam_im, log_step):
    step_size = jnp.exp(log_step)
    decay_abs = jnp.exp(lam_re * step_size)
    rotation = lam_im * step_size
    dec_re = decay_abs * jnp.cos(rotation)
    dec_im = decay_abs * jnp.sin(rotation)
    denom_sq = lam_re * lam_re + lam_im * lam_im
    inj_re = ((dec_re - 1.0) * lam_re + dec_im * lam_im) / denom_sq
    inj_im = (dec_im * lam_re - (dec_re - 1.0) * lam_im) / denom_sq
    return (dec_re, dec_im, inj_re, inj_im)


def per_device(
    block_in, cotangent, doc_lengths, norm_gain, norm_shift, log_step, lam_re, lam_im,
    b_proj, c_proj, d_skip, w_gate,
):
    batches, seqs, span, width = block_in.shape
    assert seqs == 1 and span % (4 * CHUNKS) == 0 and span & (span - 1) == 0
    half = lam_re.shape[1]
    groups = half // LANES
    rows = batches * span
    count = lax.axis_size("seq")
    tokens = float(seqs * lax.axis_size("dp") * span * count)
    here = jnp.stack([lax.axis_index("seq"), lax.axis_index("dp")]).astype(jnp.int32)
    place = jnp.concatenate([here] + [doc_lengths[batch, 0] for batch in range(batches)])
    place, block_in = lax.optimization_barrier((place, block_in))
    here = place
    disc = discretize(lam_re, lam_im, log_step)

    x = block_in.reshape(rows, width)
    cot = cotangent.reshape(rows, width)
    lower = (0, False, batches, span, groups, tokens, count)
    upper = (1, True, batches, span, groups, tokens, count)
    part = functools.partial

    flat, low = ((rows, width), f32), ((rows, width), bf16)
    wide, wide_low = ((rows, 2 * half), f32), ((rows, 2 * half), bf16)
    padded = ((batches * (span + CHUNKS), 2 * half), f32)
    sums = ((2 * batches, width), f32)
    prefix = ((2, batches * CHUNKS, 2 * half), f32)
    total = ((batches, 2 * half), f32)
    line, shared = ((1, width), f32), ((2, width), f32)
    small = ((8, width), f32)

    def gather_row(value):
        return lax.all_gather(value, "seq")

    (stats,) = run(part(first_sums, batches, span), "first_sums", (x,), (sums,), scalars=0)

    def order(value, inverse):
        body = part(order_rows, batches, span, inverse)
        return run(body, "order_rows", (value,), (low,), scalars=0)[0]

    norms = jnp.concatenate([norm_gain, norm_shift, d_skip], axis=0)

    def forward(cfg, hidden, stats):
        return run(
            part(enter_layer, cfg),
            "enter_layer",
            (place, stats, hidden, norms, disc, b_proj),
            (low, wide, prefix, total, sums),
        )

    links, plane, depth = axis_parts()
    stats, ordered = lax.optimization_barrier(
        (add_by_shifts(stats, (links, plane, depth))[0], order(x, False))
    )
    u0, drive0, prefix0, total0, norm0 = forward(lower, ordered, stats)
    states0, states_low0, act0, sig0, slope0, hidden1, stats = run(
        part(middle_forward, lower),
        "middle_forward",
        (place, gather_row(total0), prefix0, disc, drive0, u0, ordered, c_proj, norms, w_gate),
        (padded, wide_low, low, flat, flat, flat, sums),
        (flat,),
    )
    cot, stats = lax.optimization_barrier((cot, stats))
    stats, ordered_cot = lax.optimization_barrier(
        (add_by_shifts(stats, (links, plane, depth))[0], order(cot, False))
    )
    u1, drive1, prefix1, total1, norm1 = forward(upper, hidden1, stats)
    (
        result1, states1, states_low1, act1, grad_gate1, grad_mixed1, grad_low1,
        source1, prefix1, total1, grad_d1,
    ) = run(
        part(turn_around, upper),
        "turn_around",
        (
            place, gather_row(total1), prefix1, disc, drive1, u1, hidden1, c_proj, norms, w_gate,
            ordered_cot,
        ),
        (low, padded, wide_low, low, low, flat, low, wide, prefix, total, line),
        (flat, flat, flat),
    )

    def halves(length):
        return (((length // 2, width), f32),) * 2

    grad_proj1, grad_u1, stats, small1 = run(
        part(backward_finish, upper),
        "backward_finish",
        (
            place, gather_row(total1), prefix1, disc, source1, drive1, states1, u1, grad_mixed1,
            grad_d1, hidden1, norm1, norms, b_proj,
        ),
        (wide_low, flat, sums, small),
    )
    sizes = (width + 2 * half, 2 * half)
    own1, sent1 = run(
        all_weights,
        "all_weights",
        (here, act1, grad_gate1, states_low1, grad_low1, grad_proj1, u1),
        halves(sum(sizes)),
    )
    stats = stats + swap(stats, "seq", 1)
    stats, sent1 = lax.optimization_barrier((stats, sent1))
    upper_sum = LinkSum(here, (own1, swap(sent1, "seq", 1)))
    stats, upper_sum.parts = add_by_shifts(stats, (plane, depth), upper_sum.parts)
    upper_sum.swap_plane(0)
    (
        grad_out0, shared1, grad_gate0, grad_mixed0, grad_low0, source0, prefix0, total0, grad_d0,
    ) = run(
        part(between_layers, upper, lower),
        "between_layers",
        (
            place, stats, ordered_cot, grad_u1, hidden1, norm1, norms,
            disc, u0, c_proj, w_gate, states_low0, act0, sig0, slope0,
        ),
        (flat, shared, low, flat, low, wide, prefix, total, line),
        (flat,),
    )
    (total0,) = upper_sum.after(total0)
    upper_sum.down_plane(1)
    (total0,) = upper_sum.after(total0)
    upper_sum.to_depth()
    ends, grad_gate0 = wait_for(upper_sum, gather_row(total0), grad_gate0)
    upper_sum.down_join()
    ends, grad_gate0 = wait_for(upper_sum, ends, grad_gate0)
    upper_sum.scatter_depth()
    own_gates, sent_gates = run(
        gate_weights, "gate_weights", (here, act0, grad_gate0, states_low0, grad_low0),
        halves(sizes[0]),
    )
    own_gates, ends = lax.optimization_barrier((own_gates, ends))
    grad_proj0, grad_u0, last_sums = run(
        part(backward_finish_last, lower),
        "backward_finish",
        (
            place, ends, prefix0, disc, source0, drive0, states0, u0, grad_mixed0, grad_d0,
            ordered, norm0, norms, b_proj, small1,
        ),
        (wide_low, flat, ((3 * CHUNKS, width), f32)),
    )
    lower_sum = LinkSum(here, (own_gates, swap(sent_gates, "seq", 1)))
    (grad_proj0,) = wait_for(upper_sum, lower_sum, grad_proj0)
    own_inputs, sent_inputs = run(
        input_weights, "input_weights", (here, grad_proj0, u0), halves(sizes[1])
    )
    inputs_sum = LinkSum(here, (own_inputs, swap(sent_inputs, "seq", 1)))
    upper_sum.middle()
    upper_sum.swap_whole()
    lower_sum.swap_plane(0)
    inputs_sum.swap_plane(0)
    wait_for(upper_sum, lower_sum, inputs_sum)

    lower_sum.down_plane(1, inputs_sum)
    upper_sum.middle()
    upper_sum.gather_depth()
    lower_sum.to_depth()
    wait_for(upper_sum, lower_sum)

    lower_sum.down_join()
    upper_sum.up_split()
    lower_sum.scatter_depth()
    upper_sum.swap_plane(len(upper_sum.plane) - 1)
    wait_for(upper_sum, lower_sum)

    lower_sum.middle()
    lower_sum.swap_whole()
    for stage in range(len(upper_sum.plane) - 1, 0, -1):
        upper_sum.up_plane(stage)
        upper_sum.swap_plane(stage - 1)
    (last_sums,) = wait_for(upper_sum, lower_sum, last_sums)

    lower_sum.middle()
    (last_sums,) = lower_sum.after(last_sums)
    lower_sum.gather_depth()
    last_sums = last_sums + swap(last_sums, "seq", 1)
    last_terms = [last_sums] + [shifted(last_sums, plane, away) for away in range(1, plane[1])]
    last_terms = wait_for(lower_sum, *last_terms)

    lower_sum.up_split()
    wait_for(upper_sum, lower_sum)
    lower_sum.swap_plane(len(lower_sum.plane) - 1)
    upper_sum.up_plane(0)
    own1, result1 = lax.optimization_barrier((upper_sum.parts[0], result1))
    other1 = swap(own1, "seq", 1)
    block_out = order(result1, True)
    final = (((2, width, width), f32), ((2, 2 * half, width), f32), ((2, width, 2 * half), f32))
    placed = put_in_place(1, here, ((False, own1), (True, other1)), final, ())
    last_sums, bits = sum(last_terms), bits_of(lax.axis_size("dp"))
    for bit in bits[:-1]:
        last_sums = last_sums + swap(last_sums, "dp", bit)
    last_sums, block_out, *placed = wait_for(lower_sum, last_sums, block_out, *placed)

    for stage in range(len(lower_sum.plane) - 1, 0, -1):
        lower_sum.up_plane(stage)
        if stage == 1:
            (last_sums,) = lower_sum.after(last_sums)
        lower_sum.swap_plane(stage - 1)
    summed = last_sums + swap(last_sums, "dp", bits[-1])
    grad_input, shared0 = run(
        part(last_step, lower),
        "last_step",
        ((summed[: 2 * batches],), grad_out0, grad_u0, ordered, norm0, norms),
        (flat, shared),
        (((width // LANES, rows, LANES), f32),),
        scalars=0,
    )
    small_sum = summed[CHUNKS:].reshape(2, CHUNKS, width)
    _, pullback = jax.vjp(discretize, lam_re, lam_im, log_step)
    grad_lr, grad_li, grad_ls = pullback(tuple(small_sum[:, kind, :half] for kind in range(4)))
    grad_input, grad_lr, grad_li, grad_ls = wait_for(
        lower_sum, grad_input, grad_lr, grad_li, grad_ls
    )

    lower_sum.up_plane(0)
    own0 = lower_sum.parts[0]
    other0 = swap(own0, "seq", 1)
    placed = put_in_place(0, here, ((False, own0),), final, placed, 4)
    grad_w, grad_c, grad_b = put_in_place(0, here, ((True, other0),), final, placed, 4)
    both = jnp.stack([shared0, shared1])
    shape = block_in.shape
    return (
        block_out.reshape(shape), grad_input.reshape(shape), both[:, 0], both[:, 1],
        grad_ls, grad_lr, grad_li, grad_b, grad_c, small_sum[:, 4], grad_w,
    )


def solution(mesh):
    split = P(None, "dp", "seq", None)
    return jax.shard_map(
        per_device,
        mesh=mesh,
        in_specs=(split, split, P(None, "dp", None)) + (P(),) * 9,
        out_specs=(split, split) + (P(),) * 9,
        check_vma=False,
    )
```

profile of v0, /device:TPU:0, one launch (start us, length us, event | category | flops | bytes accessed | tf_op | source)
XLA Modules:
  0.0 222.6 jit_solution(2438133937198374237)
XLA Ops:
  4.3 3.8 %collective-permute-start.3 = (f32[4,512]{1,0:T(4,128)S(1)}, f32[4,512]{1,0:T(4,128)S(1)}, u32[]{:S(2)}, u32[]{:S(2)}) collective-permute-start(f32[4,512]{1,0:T(4,128)S(1)} %add.63), channel_id=1, source_target_pairs={{0,6},{1,7},{2,0},{3,1},{4,2},{5,3},{6,4},{7,5},{8,14},{9,15},{10,... | collective-permute-start | bytes 24584 | tf_op jit(solution)/shard_map/ppermute | solution.py:677
  10.0 1.8 collective-permute-done.2
  13.1 3.6 %collective-permute-start.6 = (f32[4,512]{1,0:T(4,128)S(1)}, f32[4,512]{1,0:T(4,128)S(1)}, u32[]{:S(2)}, u32[]{:S(2)}) collective-permute-start(f32[4,512]{1,0:T(4,128)S(1)} %add_add_fusion.3.stats_0_), channel_id=1, source_target_pairs={{0,24},{8,0},{16,8},{24,16},{1,25},{9,1},{17,9},{25,17},{2,26},{10... | collective-permute-start | bytes 24584 | tf_op jit(solution)/shard_map/ppermute | solution.py:677
  18.8 2.5 %collective-permute-done.5.stats_2_ = f32[4,512]{1,0:T(4,128)S(1)} collective-permute-done((f32[4,512]{1,0:T(4,128)S(1)}, f32[4,512]{1,0:T(4,128)S(1)}, u32[]{:S(2)}, u32[]{:S(2)}) %collective-permute-start.5) | collective-permute-done | bytes 8224 | tf_op jit(solution)/shard_map/ppermute | solution.py:677
  22.2 2.0 enter_layer.2
  24.2 9.2 %all-gather.4.ends = f32[8,2,768]{2,1,0:T(2,128)S(1)} all-gather(f32[1,2,768]{2,1,0:T(2,128)S(1)} %bitcast.90), channel_id=2, replica_groups=mesh['dp'=4,'seq'=8] {'seq'}, dimensions={0}, use_global_device_ids=true | all-gather | bytes 55296 | tf_op jit(solution)/shard_map/all_gather | solution.py:953
  34.6 3.7 %middle_forward.1 = (f32[528,768]{1,0:T(8,128)S(1)}, bf16[512,768]{1,0:T(8,128)(2,1)S(1)}, bf16[512,512]{1,0:T(8,128)(2,1)S(1)}, f32[512,512]{1,0:T(8,128)S(1)},...) custom-call(s32[10]{0:T(128)S(1)} %pad_add_fusion.place.here.refs_0_, ...), custom_call_target="tpu_custom_call" | custom-call | tf_op jit(solution)/shard_map/middle_forward/pallas_call | solution.py:605
  39.6 1.5 collective-permute-start.10
  43.2 1.5 collective-permute-done.9
  47.3 2.0 collective-permute-start.11
  49.7 1.5 collective-permute-done.12.stats_2_
  51.2 1.5 collective-permute-done.11.stats_1_
  52.7 2.0 enter_layer.3
  54.8 9.2 %all-gather.5.ends = f32[8,2,768]{2,1,0:T(2,128)S(1)} all-gather(f32[1,2,768]{2,1,0:T(2,128)S(1)} %bitcast.91), channel_id=3, replica_groups=mesh['dp'=4,'seq'=8] {'seq'}, dimensions={0}, use_global_device_ids=true | all-gather | bytes 55296 | tf_op jit(solution)/shard_map/all_gather | solution.py:953
  63.9 6.1 %turn_around.1 = (bf16[512,512]{1,0:T(8,128)(2,1)S(1)}, f32[528,768]{1,0:T(8,128)S(1)}, bf16[512,768]{1,0:T(8,128)(2,1)S(1)}, bf16[512,512]{1,0:T(8,128)(2,1)S(1...) custom-call(s32[10]{0:T(128)S(1)} %pad_add_fusion.place.here.refs_0_, ...), custom_call_target="tpu_custom_call" | custom-call | tf_op jit(solution)/shard_map/turn_around/pallas_call | solution.py:605
  70.0 8.1 %all-gather.6.ends = f32[8,2,768]{2,1,0:T(2,128)S(1)} all-gather(f32[1,2,768]{2,1,0:T(2,128)S(1)} %bitcast.89), channel_id=4, replica_groups=mesh['dp'=4,'seq'=8] {'seq'}, dimensions={0}, use_global_device_ids=true | all-gather | bytes 55296 | tf_op jit(solution)/shard_map/all_gather | solution.py:953
  78.2 2.9 %backward_finish.2 = (bf16[512,768]{1,0:T(8,128)(2,1)S(1)}, f32[512,512]{1,0:T(8,128)S(1)}, f32[4,512]{1,0:T(4,128)S(1)}, f32[8,512]{1,0:T(8,128)S(1)}) custom-call(s32[10]{0:T(128)S(1)} %pad_add_fusion.place.here.refs_0_, f32[8,2,768]{2,1,0:T(2,128)S(1)} %all-gather.6.ends, f32[2,16,768]{2,1,0:T(8,128)S(1)} %get-tuple-element.249.prefix, ...), custom_call_target="tpu_custom_call" | custom-call | tf_op jit(solution)/shard_map/backward_finish/pallas_call | solution.py:605
  81.5 1.8 all_weights.1
  83.6 1.5 collective-permute-start.17
  85.0 1.5 collective-permute-start.16
  87.2 1.5 collective-permute-done.16
  88.7 2.4 %collective-permute-done.15 = f32[4,512]{1,0:T(4,128)S(1)} collective-permute-done((f32[4,512]{1,0:T(4,128)S(1)}, f32[4,512]{1,0:T(4,128)S(1)}, u32[]{:S(2)}, u32[]{:S(2)}) %collective-permute-start.15) | collective-permute-done | bytes 8224 | tf_op jit(solution)/shard_map/ppermute | solution.py:677
  96.3 2.3 %collective-permute-done.22.stats_2_ = f32[4,512]{1,0:T(4,128)S(1)} collective-permute-done((f32[4,512]{1,0:T(4,128)S(1)}, f32[4,512]{1,0:T(4,128)S(1)}, u32[]{:S(2)}, u32[]{:S(2)}) %collective-permute-start.22) | collective-permute-done | bytes 8224 | tf_op jit(solution)/shard_map/ppermute | solution.py:677
  99.7 3.4 %between_layers.1 = (f32[512,512]{1,0:T(8,128)S(1)}, f32[2,512]{1,0:T(2,128)S(1)}, bf16[512,512]{1,0:T(8,128)(2,1)S(1)}, f32[512,512]{1,0:T(8,128)S(1)}, bf16[51...) custom-call(s32[10]{0:T(128)S(1)} %pad_add_fusion.place.here.refs_0_, ...), custom_call_target="tpu_custom_call" | custom-call | tf_op jit(solution)/shard_map/between_layers/pallas_call | solution.py:605
  105.8 1.7 collective-permute-start.25
  107.5 9.2 %all-gather.7.refs_1_ = f32[8,2,768]{2,1,0:T(2,128)S(1)} all-gather(f32[1,2,768]{2,1,0:T(2,128)S(1)} %bitcast.88), channel_id=5, replica_groups=mesh['dp'=4,'seq'=8] {'seq'}, dimensions={0}, use_global_device_ids=true | all-gather | bytes 55296 | tf_op jit(solution)/shard_map/all_gather | solution.py:953
  119.2 3.0 %backward_finish.3 = (bf16[512,768]{1,0:T(8,128)(2,1)S(1)}, f32[512,512]{1,0:T(8,128)S(1)}, f32[24,512]{1,0:T(8,128)S(1)}) custom-call(s32[10]{0:T(128)S(1)} %pad_add_fusion.place.here.refs_0_, f32[8,2,768]{2,1,0:T(2,128)S(1)} %all-gather.7.refs_1_, f32[2,16,768]{2,1,0:T(8,128)S(1)} %get-tuple-element.316.refs_2_, ...), custom_call_target="tpu_custom_call" | custom-call | tf_op jit(solution)/shard_map/backward_finish/pallas_call | solution.py:605
  123.0 4.5 %collective-permute-done.26.found = f32[128,512]{1,0:T(8,128)S(1)} collective-permute-done((f32[128,512]{1,0:T(8,128)S(1)}, f32[128,512]{1,0:T(8,128)S(1)}, u32[]{:S(2)}, u32[]{:S(2)}) %collective-permute-start.26) | collective-permute-done | bytes 262176 | tf_op jit(solution)/shard_map/ppermute | solution.py:706
  128.7 1.6 collective-permute-start.29
  134.5 10.7 %collective-permute-done.28.found = f32[128,512]{1,0:T(8,128)S(1)} collective-permute-done((f32[128,512]{1,0:T(8,128)S(1)}, f32[128,512]{1,0:T(8,128)S(1)}, u32[]{:S(2)}, u32[]{:S(2)}) %collective-permute-start.28) | collective-permute-done | bytes 262176 | tf_op jit(solution)/shard_map/ppermute | solution.py:706
  146.0 1.6 collective-permute-start.35
  148.1 5.4 %collective-permute-done.34.found = f32[128,512]{1,0:T(8,128)S(1)} collective-permute-done((f32[128,512]{1,0:T(8,128)S(1)}, f32[128,512]{1,0:T(8,128)S(1)}, u32[]{:S(2)}, u32[]{:S(2)}) %collective-permute-start.34) | collective-permute-done | bytes 262176 | tf_op jit(solution)/shard_map/ppermute | solution.py:706
  156.7 1.6 collective-permute-start.38
  158.9 1.8 collective-permute-start.39
  160.7 2.6 %collective-permute-done.37.refs_1_ = f32[256,256]{1,0:T(8,128)S(1)} collective-permute-done((f32[256,256]{1,0:T(8,128)S(1)}, f32[256,256]{1,0:T(8,128)S(1)}, u32[]{:S(2)}, u32[]{:S(2)}) %collective-permute-start.37) | collective-permute-done | bytes 262176 | tf_op jit(solution)/shard_map/ppermute | solution.py:706
  163.6 1.9 collective-permute-done.39.found
  168.2 1.8 collective-permute-start.42
  170.0 9.8 %collective-permute-done.42.found = f32[128,512]{1,0:T(8,128)S(1)} collective-permute-done((f32[128,512]{1,0:T(8,128)S(1)}, f32[128,512]{1,0:T(8,128)S(1)}, u32[]{:S(2)}, u32[]{:S(2)}) %collective-permute-start.42) | collective-permute-done | bytes 262176 | tf_op jit(solution)/shard_map/ppermute | solution.py:706
  181.2 1.6 collective-permute-start.47
  185.4 2.0 collective-permute-done.46
  191.3 2.0 collective-permute-start.50
  195.5 2.9 %put_in_place.3 = (f32[2,512,512]{2,1,0:T(8,128)}, f32[2,768,512]{2,1,0:T(8,128)}, f32[2,512,768]{2,1,0:T(8,128)}) custom-call(s32[10]{0:T(128)S(1)} %pad_add_fusion.place.here.refs_0_, f32[1024,512]{1,0:T(8,128)S(1)} %unfold_sides.5.refs_0_, f32[1024,512]{1,0:T(8,128)S(1)} %collective-permute-done.51.refs_1_), custom_call_target="tpu_custom_call" | custom-call | tf_op jit(solution)/shard_map/put_in_place/pallas_call | solution.py:651
  200.3 2.1 collective-permute-start.54
  204.0 1.6 collective-permute-done.54
  205.6 1.6 last_step.1
  208.0 7.3 %collective-permute-done.52.refs_1_ = f32[512,256]{1,0:T(8,128)S(1)} collective-permute-done((f32[512,256]{1,0:T(8,128)S(1)}, f32[512,256]{1,0:T(8,128)S(1)}, u32[]{:S(2)}, u32[]{:S(2)}) %collective-permute-start.52) | collective-permute-done | bytes 524320 | tf_op jit(solution)/shard_map/ppermute | solution.py:706
  217.6 2.1 put_in_place.4
  220.6 2.1 put_in_place.5
  (143 shorter events, 61.9 us)
Async XLA Ops:
  4.3 5.7 %collective-permute-start.3 = (f32[4,512]{1,0:T(4,128)S(1)}, f32[4,512]{1,0:T(4,128)S(1)}, u32[]{:S(2)}, u32[]{:S(2)}) collective-permute-start(f32[4,512]{1,0:T(4,128)S(1)} %add.63), channel_id=1, source_target_pairs={{0,6},{1,7},{2,0},{3,1},{4,2},{5,3},{6,4},{7,5},{8,14},{9,15},{10,... | collective-permute-start | bytes 24584 | tf_op jit(solution)/shard_map/ppermute | solution.py:677
  8.1 3.7 %collective-permute-start.2 = (f32[4,512]{1,0:T(4,128)S(1)}, f32[4,512]{1,0:T(4,128)S(1)}, u32[]{:S(2)}, u32[]{:S(2)}) collective-permute-start(f32[4,512]{1,0:T(4,128)S(1)} %add.63), channel_id=1, source_target_pairs={{0,4},{1,5},{2,6},{3,7},{4,0},{5,1},{6,2},{7,3},{8,12},{9,13},{10,... | collective-permute-start | bytes 24584 | tf_op jit(solution)/shard_map/ppermute | solution.py:677
  8.6 4.5 %collective-permute-start.1 = (f32[4,512]{1,0:T(4,128)S(1)}, f32[4,512]{1,0:T(4,128)S(1)}, u32[]{:S(2)}, u32[]{:S(2)}) collective-permute-start(f32[4,512]{1,0:T(4,128)S(1)} %add.63), channel_id=1, source_target_pairs={{0,2},{1,3},{2,4},{3,5},{4,6},{5,7},{6,0},{7,1},{8,10},{9,11},{10,... | collective-permute-start | bytes 24584 | tf_op jit(solution)/shard_map/ppermute | solution.py:677
  13.1 5.7 %collective-permute-start.6 = (f32[4,512]{1,0:T(4,128)S(1)}, f32[4,512]{1,0:T(4,128)S(1)}, u32[]{:S(2)}, u32[]{:S(2)}) collective-permute-start(f32[4,512]{1,0:T(4,128)S(1)} %add_add_fusion.3.stats_0_), channel_id=1, source_target_pairs={{0,24},{8,0},{16,8},{24,16},{1,25},{9,1},{17,9},{25,17},{2,26},{10... | collective-permute-start | bytes 24584 | tf_op jit(solution)/shard_map/ppermute | solution.py:677
  16.7 4.5 %collective-permute-start.5 = (f32[4,512]{1,0:T(4,128)S(1)}, f32[4,512]{1,0:T(4,128)S(1)}, u32[]{:S(2)}, u32[]{:S(2)}) collective-permute-start(f32[4,512]{1,0:T(4,128)S(1)} %add_add_fusion.3.stats_0_), channel_id=1, source_target_pairs={{0,16},{8,24},{16,0},{24,8},{1,17},{9,25},{17,1},{25,9},{2,18},{10... | collective-permute-start | bytes 24584 | tf_op jit(solution)/shard_map/ppermute | solution.py:677
  16.7 5.4 %collective-permute-start.4 = (f32[4,512]{1,0:T(4,128)S(1)}, f32[4,512]{1,0:T(4,128)S(1)}, u32[]{:S(2)}, u32[]{:S(2)}) collective-permute-start(f32[4,512]{1,0:T(4,128)S(1)} %add_add_fusion.3.stats_0_), channel_id=1, source_target_pairs={{0,8},{8,16},{16,24},{24,0},{1,9},{9,17},{17,25},{25,1},{2,10},{10... | collective-permute-start | bytes 24584 | tf_op jit(solution)/shard_map/ppermute | solution.py:677
  39.6 3.7 %collective-permute-start.10 = (f32[4,512]{1,0:T(4,128)S(1)}, f32[4,512]{1,0:T(4,128)S(1)}, u32[]{:S(2)}, u32[]{:S(2)}) collective-permute-start(f32[4,512]{1,0:T(4,128)S(1)} %add.69), channel_id=1, source_target_pairs={{0,6},{1,7},{2,0},{3,1},{4,2},{5,3},{6,4},{7,5},{8,14},{9,15},{10,... | collective-permute-start | bytes 24584 | tf_op jit(solution)/shard_map/ppermute | solution.py:677
  41.0 3.7 %collective-permute-start.9 = (f32[4,512]{1,0:T(4,128)S(1)}, f32[4,512]{1,0:T(4,128)S(1)}, u32[]{:S(2)}, u32[]{:S(2)}) collective-permute-start(f32[4,512]{1,0:T(4,128)S(1)} %add.69), channel_id=1, source_target_pairs={{0,4},{1,5},{2,6},{3,7},{4,0},{5,1},{6,2},{7,3},{8,12},{9,13},{10,... | collective-permute-start | bytes 24584 | tf_op jit(solution)/shard_map/ppermute | solution.py:677
  41.5 4.5 %collective-permute-start.8 = (f32[4,512]{1,0:T(4,128)S(1)}, f32[4,512]{1,0:T(4,128)S(1)}, u32[]{:S(2)}, u32[]{:S(2)}) collective-permute-start(f32[4,512]{1,0:T(4,128)S(1)} %add.69), channel_id=1, source_target_pairs={{0,2},{1,3},{2,4},{3,5},{4,6},{5,7},{6,0},{7,1},{8,10},{9,11},{10,... | collective-permute-start | bytes 24584 | tf_op jit(solution)/shard_map/ppermute | solution.py:677
  46.6 4.5 %collective-permute-start.12 = (f32[4,512]{1,0:T(4,128)S(1)}, f32[4,512]{1,0:T(4,128)S(1)}, u32[]{:S(2)}, u32[]{:S(2)}) collective-permute-start(f32[4,512]{1,0:T(4,128)S(1)} %add_add_fusion.2.stats_0_), channel_id=1, source_target_pairs={{0,16},{8,24},{16,0},{24,8},{1,17},{9,25},{17,1},{25,9},{2,18},{10... | collective-permute-start | bytes 24584 | tf_op jit(solution)/shard_map/ppermute | solution.py:677
  47.3 5.4 %collective-permute-start.11 = (f32[4,512]{1,0:T(4,128)S(1)}, f32[4,512]{1,0:T(4,128)S(1)}, u32[]{:S(2)}, u32[]{:S(2)}) collective-permute-start(f32[4,512]{1,0:T(4,128)S(1)} %add_add_fusion.2.stats_0_), channel_id=1, source_target_pairs={{0,8},{8,16},{16,24},{24,0},{1,9},{9,17},{17,25},{25,1},{2,10},{10... | collective-permute-start | bytes 24584 | tf_op jit(solution)/shard_map/ppermute | solution.py:677
  83.3 7.8 %collective-permute-start.18 = (f32[1024,512]{1,0:T(8,128)S(1)}, f32[1024,512]{1,0:T(8,128)S(1)}, u32[]{:S(2)}, u32[]{:S(2)}) collective-permute-start(f32[1024,512]{1,0:T(8,128)S(1)} %get-tuple-element.264), channel_id=1, source_target_pairs={{0,1},{1,0},{2,3},{3,2},{4,5},{5,4},{6,7},{7,6},{8,9},{9,8},{10,11... | collective-permute-start | bytes 6291464 | tf_op jit(solution)/shard_map/ppermute | solution.py:706
  83.6 3.7 %collective-permute-start.17 = (f32[4,512]{1,0:T(4,128)S(1)}, f32[4,512]{1,0:T(4,128)S(1)}, u32[]{:S(2)}, u32[]{:S(2)}) collective-permute-start(f32[4,512]{1,0:T(4,128)S(1)} %add.73), channel_id=1, source_target_pairs={{0,6},{1,7},{2,0},{3,1},{4,2},{5,3},{6,4},{7,5},{8,14},{9,15},{10,... | collective-permute-start | bytes 24584 | tf_op jit(solution)/shard_map/ppermute | solution.py:677
  86.6 4.5 %collective-permute-start.15 = (f32[4,512]{1,0:T(4,128)S(1)}, f32[4,512]{1,0:T(4,128)S(1)}, u32[]{:S(2)}, u32[]{:S(2)}) collective-permute-start(f32[4,512]{1,0:T(4,128)S(1)} %add.73), channel_id=1, source_target_pairs={{0,2},{1,3},{2,4},{3,5},{4,6},{5,7},{6,0},{7,1},{8,10},{9,11},{10,... | collective-permute-start | bytes 24584 | tf_op jit(solution)/shard_map/ppermute | solution.py:677
  92.0 12.5 %collective-permute-start.19 = (f32[512,256]{1,0:T(8,128)S(1)}, f32[512,256]{1,0:T(8,128)S(1)}, u32[]{:S(2)}, u32[]{:S(2)}) collective-permute-start(f32[512,256]{1,0:T(8,128)S(1)} %get-tuple-element.270), channel_id=1, source_target_pairs={{0,2},{1,3},{2,0},{3,1},{4,6},{5,7},{6,4},{7,5},{8,10},{9,11},{10,... | collective-permute-start | bytes 1572872 | tf_op jit(solution)/shard_map/ppermute | solution.py:706
  92.1 12.5 %collective-permute-start.20 = (f32[512,256]{1,0:T(8,128)S(1)}, f32[512,256]{1,0:T(8,128)S(1)}, u32[]{:S(2)}, u32[]{:S(2)}) collective-permute-start(f32[512,256]{1,0:T(8,128)S(1)} %get-tuple-element.272), channel_id=1, source_target_pairs={{0,4},{1,5},{2,6},{3,7},{4,0},{5,1},{6,2},{7,3},{8,12},{9,13},{10,... | collective-permute-start | bytes 1572872 | tf_op jit(solution)/shard_map/ppermute | solution.py:706
  92.6 3.7 %collective-permute-start.23 = (f32[4,512]{1,0:T(4,128)S(1)}, f32[4,512]{1,0:T(4,128)S(1)}, u32[]{:S(2)}, u32[]{:S(2)}) collective-permute-start(f32[4,512]{1,0:T(4,128)S(1)} %add_add_fusion.1.stats_0_), channel_id=1, source_target_pairs={{0,24},{8,0},{16,8},{24,16},{1,25},{9,1},{17,9},{25,17},{2,26},{10... | collective-permute-start | bytes 24584 | tf_op jit(solution)/shard_map/ppermute | solution.py:677
  94.0 4.6 %collective-permute-start.22 = (f32[4,512]{1,0:T(4,128)S(1)}, f32[4,512]{1,0:T(4,128)S(1)}, u32[]{:S(2)}, u32[]{:S(2)}) collective-permute-start(f32[4,512]{1,0:T(4,128)S(1)} %add_add_fusion.1.stats_0_), channel_id=1, source_target_pairs={{0,16},{8,24},{16,0},{24,8},{1,17},{9,25},{17,1},{25,9},{2,18},{10... | collective-permute-start | bytes 24584 | tf_op jit(solution)/shard_map/ppermute | solution.py:677
  94.2 5.4 %collective-permute-start.21 = (f32[4,512]{1,0:T(4,128)S(1)}, f32[4,512]{1,0:T(4,128)S(1)}, u32[]{:S(2)}, u32[]{:S(2)}) collective-permute-start(f32[4,512]{1,0:T(4,128)S(1)} %add_add_fusion.1.stats_0_), channel_id=1, source_target_pairs={{0,8},{8,16},{16,24},{24,0},{1,9},{9,17},{17,25},{25,1},{2,10},{10... | collective-permute-start | bytes 24584 | tf_op jit(solution)/shard_map/ppermute | solution.py:677
  105.2 11.4 %collective-permute-start.24 = (f32[256,256]{1,0:T(8,128)S(1)}, f32[256,256]{1,0:T(8,128)S(1)}, u32[]{:S(2)}, u32[]{:S(2)}) collective-permute-start(f32[256,256]{1,0:T(8,128)S(1)} %get-tuple-element.290), channel_id=1, source_target_pairs={{0,4},{1,5},{2,6},{3,7},{4,0},{5,1},{6,2},{7,3},{8,12},{9,13},{10,... | collective-permute-start | bytes 786440 | tf_op jit(solution)/shard_map/ppermute | solution.py:706
  105.8 10.8 %collective-permute-start.25 = (f32[256,256]{1,0:T(8,128)S(1)}, f32[256,256]{1,0:T(8,128)S(1)}, u32[]{:S(2)}, u32[]{:S(2)}) collective-permute-start(f32[256,256]{1,0:T(8,128)S(1)} %get-tuple-element.292), channel_id=1, source_target_pairs={{0,2},{1,3},{2,0},{3,1},{4,6},{5,7},{6,4},{7,5},{8,10},{9,11},{10,... | collective-permute-start | bytes 786440 | tf_op jit(solution)/shard_map/ppermute | solution.py:706
  119.1 8.4 %collective-permute-start.26 = (f32[128,512]{1,0:T(8,128)S(1)}, f32[128,512]{1,0:T(8,128)S(1)}, u32[]{:S(2)}, u32[]{:S(2)}) collective-permute-start(f32[128,512]{1,0:T(8,128)S(1)} %get-tuple-element.304), channel_id=1, source_target_pairs={{0,8},{8,0},{16,24},{24,16},{1,9},{9,1},{17,25},{25,17},{2,10},{10... | collective-permute-start | bytes 786440 | tf_op jit(solution)/shard_map/ppermute | solution.py:706
  128.7 16.5 %collective-permute-start.29 = (f32[320,256]{1,0:T(8,128)S(1)}, f32[320,256]{1,0:T(8,128)S(1)}, u32[]{:S(2)}, u32[]{:S(2)}) collective-permute-start(f32[320,256]{1,0:T(8,128)S(1)} %get-tuple-element.327), channel_id=1, source_target_pairs={{0,2},{1,3},{2,0},{3,1},{4,6},{5,7},{6,4},{7,5},{8,10},{9,11},{10,... | collective-permute-start | bytes 983048 | tf_op jit(solution)/shard_map/ppermute | solution.py:706
  130.3 14.9 %collective-permute-start.30 = (f32[320,256]{1,0:T(8,128)S(1)}, f32[320,256]{1,0:T(8,128)S(1)}, u32[]{:S(2)}, u32[]{:S(2)}) collective-permute-start(f32[320,256]{1,0:T(8,128)S(1)} %get-tuple-element.329), channel_id=1, source_target_pairs={{0,4},{1,5},{2,6},{3,7},{4,0},{5,1},{6,2},{7,3},{8,12},{9,13},{10,... | collective-permute-start | bytes 983048 | tf_op jit(solution)/shard_map/ppermute | solution.py:706
  130.8 14.4 %collective-permute-start.28 = (f32[128,512]{1,0:T(8,128)S(1)}, f32[128,512]{1,0:T(8,128)S(1)}, u32[]{:S(2)}, u32[]{:S(2)}) collective-permute-start(f32[128,512]{1,0:T(8,128)S(1)} %add_two.4.own), channel_id=1, source_target_pairs={{0,16},{8,24},{16,0},{24,8},{1,17},{9,25},{17,1},{25,9},{2,18},{10... | collective-permute-start | bytes 786440 | tf_op jit(solution)/shard_map/ppermute | solution.py:706
  132.3 12.9 %collective-permute-start.32 = (f32[192,256]{1,0:T(8,128)S(1)}, f32[192,256]{1,0:T(8,128)S(1)}, u32[]{:S(2)}, u32[]{:S(2)}) collective-permute-start(f32[192,256]{1,0:T(8,128)S(1)} %get-tuple-element.334), channel_id=1, source_target_pairs={{0,2},{1,3},{2,0},{3,1},{4,6},{5,7},{6,4},{7,5},{8,10},{9,11},{10,... | collective-permute-start | bytes 589832 | tf_op jit(solution)/shard_map/ppermute | solution.py:706
  133.6 11.6 %collective-permute-start.33 = (f32[192,256]{1,0:T(8,128)S(1)}, f32[192,256]{1,0:T(8,128)S(1)}, u32[]{:S(2)}, u32[]{:S(2)}) collective-permute-start(f32[192,256]{1,0:T(8,128)S(1)} %get-tuple-element.336), channel_id=1, source_target_pairs={{0,4},{1,5},{2,6},{3,7},{4,0},{5,1},{6,2},{7,3},{8,12},{9,13},{10,... | collective-permute-start | bytes 589832 | tf_op jit(solution)/shard_map/ppermute | solution.py:706
  145.3 8.3 %collective-permute-start.34 = (f32[128,512]{1,0:T(8,128)S(1)}, f32[128,512]{1,0:T(8,128)S(1)}, u32[]{:S(2)}, u32[]{:S(2)}) collective-permute-start(f32[128,512]{1,0:T(8,128)S(1)} %add_two.5.own), channel_id=1, source_target_pairs={{0,8},{8,0},{16,24},{24,16},{1,9},{9,1},{17,25},{25,17},{2,10},{10... | collective-permute-start | bytes 786440 | tf_op jit(solution)/shard_map/ppermute | solution.py:706
  146.0 8.3 %collective-permute-start.35 = (f32[256,256]{1,0:T(8,128)S(1)}, f32[256,256]{1,0:T(8,128)S(1)}, u32[]{:S(2)}, u32[]{:S(2)}) collective-permute-start(f32[256,256]{1,0:T(8,128)S(1)} %get-tuple-element.348), channel_id=1, source_target_pairs={{0,4},{1,5},{2,6},{3,7},{4,0},{5,1},{6,2},{7,3},{8,12},{9,13},{10,... | collective-permute-start | bytes 786440 | tf_op jit(solution)/shard_map/ppermute | solution.py:706
  147.6 7.9 %collective-permute-start.36 = (f32[256,256]{1,0:T(8,128)S(1)}, f32[256,256]{1,0:T(8,128)S(1)}, u32[]{:S(2)}, u32[]{:S(2)}) collective-permute-start(f32[256,256]{1,0:T(8,128)S(1)} %get-tuple-element.350), channel_id=1, source_target_pairs={{0,2},{1,3},{2,0},{3,1},{4,6},{5,7},{6,4},{7,5},{8,10},{9,11},{10,... | collective-permute-start | bytes 786440 | tf_op jit(solution)/shard_map/ppermute | solution.py:706
  156.2 7.1 %collective-permute-start.37 = (f32[256,256]{1,0:T(8,128)S(1)}, f32[256,256]{1,0:T(8,128)S(1)}, u32[]{:S(2)}, u32[]{:S(2)}) collective-permute-start(f32[256,256]{1,0:T(8,128)S(1)} %get-tuple-element.361.refs_0_), channel_id=1, source_target_pairs={{0,4},{1,5},{2,6},{3,7},{4,0},{5,1},{6,2},{7,3},{8,12},{9,13},{10,... | collective-permute-start | bytes 786440 | tf_op jit(solution)/shard_map/ppermute | solution.py:706
  156.7 6.9 %collective-permute-start.38 = (f32[256,256]{1,0:T(8,128)S(1)}, f32[256,256]{1,0:T(8,128)S(1)}, u32[]{:S(2)}, u32[]{:S(2)}) collective-permute-start(f32[256,256]{1,0:T(8,128)S(1)} %get-tuple-element.363.refs_2_), channel_id=1, source_target_pairs={{0,2},{1,3},{2,0},{3,1},{4,6},{5,7},{6,4},{7,5},{8,10},{9,11},{10,... | collective-permute-start | bytes 786440 | tf_op jit(solution)/shard_map/ppermute | solution.py:706
  158.9 6.6 %collective-permute-start.39 = (f32[128,512]{1,0:T(8,128)S(1)}, f32[128,512]{1,0:T(8,128)S(1)}, u32[]{:S(2)}, u32[]{:S(2)}) collective-permute-start(f32[128,512]{1,0:T(8,128)S(1)} %get-tuple-element.360), channel_id=1, source_target_pairs={{0,8},{8,0},{16,24},{24,16},{1,9},{9,1},{17,25},{25,17},{2,10},{10... | collective-permute-start | bytes 786440 | tf_op jit(solution)/shard_map/ppermute | solution.py:706
  166.1 13.7 %collective-permute-start.40 = (f32[512,256]{1,0:T(8,128)S(1)}, f32[512,256]{1,0:T(8,128)S(1)}, u32[]{:S(2)}, u32[]{:S(2)}) collective-permute-start(f32[512,256]{1,0:T(8,128)S(1)} %get-tuple-element.392.refs_0_), channel_id=1, source_target_pairs={{0,2},{1,3},{2,0},{3,1},{4,6},{5,7},{6,4},{7,5},{8,10},{9,11},{10,... | collective-permute-start | bytes 1572872 | tf_op jit(solution)/shard_map/ppermute | solution.py:706
  166.7 13.1 %collective-permute-start.41 = (f32[512,256]{1,0:T(8,128)S(1)}, f32[512,256]{1,0:T(8,128)S(1)}, u32[]{:S(2)}, u32[]{:S(2)}) collective-permute-start(f32[512,256]{1,0:T(8,128)S(1)} %get-tuple-element.394.refs_2_), channel_id=1, source_target_pairs={{0,4},{1,5},{2,6},{3,7},{4,0},{5,1},{6,2},{7,3},{8,12},{9,13},{10,... | collective-permute-start | bytes 1572872 | tf_op jit(solution)/shard_map/ppermute | solution.py:706
  168.2 11.6 %collective-permute-start.42 = (f32[128,512]{1,0:T(8,128)S(1)}, f32[128,512]{1,0:T(8,128)S(1)}, u32[]{:S(2)}, u32[]{:S(2)}) collective-permute-start(f32[128,512]{1,0:T(8,128)S(1)} %add_two.6.own), channel_id=1, source_target_pairs={{0,16},{8,24},{16,0},{24,8},{1,17},{9,25},{17,1},{25,9},{2,18},{10... | collective-permute-start | bytes 786440 | tf_op jit(solution)/shard_map/ppermute | solution.py:706
  179.8 8.7 %collective-permute-start.43 = (f32[128,512]{1,0:T(8,128)S(1)}, f32[128,512]{1,0:T(8,128)S(1)}, u32[]{:S(2)}, u32[]{:S(2)}) collective-permute-start(f32[128,512]{1,0:T(8,128)S(1)} %add_two.7.own), channel_id=1, source_target_pairs={{0,8},{8,0},{16,24},{24,16},{1,9},{9,1},{17,25},{25,17},{2,10},{10... | collective-permute-start | bytes 786440 | tf_op jit(solution)/shard_map/ppermute | solution.py:706
  181.2 4.1 %collective-permute-start.47 = (f32[24,512]{1,0:T(8,128)S(1)}, f32[24,512]{1,0:T(8,128)S(1)}, u32[]{:S(2)}, u32[]{:S(2)}) collective-permute-start(f32[24,512]{1,0:T(8,128)S(1)} %add.77), channel_id=1, source_target_pairs={{0,6},{1,7},{2,0},{3,1},{4,2},{5,3},{6,4},{7,5},{8,14},{9,15},{10,... | collective-permute-start | bytes 147464 | tf_op jit(solution)/shard_map/ppermute | solution.py:677
  182.8 4.6 %collective-permute-start.46 = (f32[24,512]{1,0:T(8,128)S(1)}, f32[24,512]{1,0:T(8,128)S(1)}, u32[]{:S(2)}, u32[]{:S(2)}) collective-permute-start(f32[24,512]{1,0:T(8,128)S(1)} %add.77), channel_id=1, source_target_pairs={{0,4},{1,5},{2,6},{3,7},{4,0},{5,1},{6,2},{7,3},{8,12},{9,13},{10,... | collective-permute-start | bytes 147464 | tf_op jit(solution)/shard_map/ppermute | solution.py:677
  183.6 5.0 %collective-permute-start.45 = (f32[24,512]{1,0:T(8,128)S(1)}, f32[24,512]{1,0:T(8,128)S(1)}, u32[]{:S(2)}, u32[]{:S(2)}) collective-permute-start(f32[24,512]{1,0:T(8,128)S(1)} %add.77), channel_id=1, source_target_pairs={{0,2},{1,3},{2,4},{3,5},{4,6},{5,7},{6,0},{7,1},{8,10},{9,11},{10,... | collective-permute-start | bytes 147464 | tf_op jit(solution)/shard_map/ppermute | solution.py:677
  189.9 5.6 %collective-permute-start.51 = (f32[1024,512]{1,0:T(8,128)S(1)}, f32[1024,512]{1,0:T(8,128)S(1)}, u32[]{:S(2)}, u32[]{:S(2)}) collective-permute-start(f32[1024,512]{1,0:T(8,128)S(1)} %unfold_sides.5.refs_0_), channel_id=1, source_target_pairs={{0,1},{1,0},{2,3},{3,2},{4,5},{5,4},{6,7},{7,6},{8,9},{9,8},{10,11... | collective-permute-start | bytes 6291464 | tf_op jit(solution)/shard_map/ppermute | solution.py:706
  190.0 8.7 %collective-permute-start.48 = (f32[256,256]{1,0:T(8,128)S(1)}, f32[256,256]{1,0:T(8,128)S(1)}, u32[]{:S(2)}, u32[]{:S(2)}) collective-permute-start(f32[256,256]{1,0:T(8,128)S(1)} %get-tuple-element.403.refs_0_), channel_id=1, source_target_pairs={{0,4},{1,5},{2,6},{3,7},{4,0},{5,1},{6,2},{7,3},{8,12},{9,13},{10,... | collective-permute-start | bytes 786440 | tf_op jit(solution)/shard_map/ppermute | solution.py:706
  191.3 8.4 %collective-permute-start.49 = (f32[256,256]{1,0:T(8,128)S(1)}, f32[256,256]{1,0:T(8,128)S(1)}, u32[]{:S(2)}, u32[]{:S(2)}) collective-permute-start(f32[256,256]{1,0:T(8,128)S(1)} %get-tuple-element.405.refs_2_), channel_id=1, source_target_pairs={{0,2},{1,3},{2,0},{3,1},{4,6},{5,7},{6,4},{7,5},{8,10},{9,11},{10,... | collective-permute-start | bytes 786440 | tf_op jit(solution)/shard_map/ppermute | solution.py:706
  191.3 4.2 %collective-permute-start.50 = (f32[24,512]{1,0:T(8,128)S(1)}, f32[24,512]{1,0:T(8,128)S(1)}, u32[]{:S(2)}, u32[]{:S(2)}) collective-permute-start(f32[24,512]{1,0:T(8,128)S(1)} %add_add_fusion), channel_id=1, source_target_pairs={{0,8},{8,0},{16,24},{24,16},{1,9},{9,1},{17,25},{25,17},{2,10},{10... | collective-permute-start | bytes 147464 | tf_op jit(solution)/shard_map/ppermute | solution.py:706
  200.3 5.3 %collective-permute-start.54 = (f32[24,512]{1,0:T(8,128)S(1)}, f32[24,512]{1,0:T(8,128)S(1)}, u32[]{:S(2)}, u32[]{:S(2)}) collective-permute-start(f32[24,512]{1,0:T(8,128)S(1)} %add.81), channel_id=1, source_target_pairs={{0,16},{8,24},{16,0},{24,8},{1,17},{9,25},{17,1},{25,9},{2,18},{10... | collective-permute-start | bytes 147464 | tf_op jit(solution)/shard_map/ppermute | solution.py:706
  202.4 12.9 %collective-permute-start.52 = (f32[512,256]{1,0:T(8,128)S(1)}, f32[512,256]{1,0:T(8,128)S(1)}, u32[]{:S(2)}, u32[]{:S(2)}) collective-permute-start(f32[512,256]{1,0:T(8,128)S(1)} %get-tuple-element.424.refs_0_), channel_id=1, source_target_pairs={{0,2},{1,3},{2,0},{3,1},{4,6},{5,7},{6,4},{7,5},{8,10},{9,11},{10,... | collective-permute-start | bytes 1572872 | tf_op jit(solution)/shard_map/ppermute | solution.py:706
  203.2 12.5 %collective-permute-start.53 = (f32[512,256]{1,0:T(8,128)S(1)}, f32[512,256]{1,0:T(8,128)S(1)}, u32[]{:S(2)}, u32[]{:S(2)}) collective-permute-start(f32[512,256]{1,0:T(8,128)S(1)} %get-tuple-element.426.refs_2_), channel_id=1, source_target_pairs={{0,4},{1,5},{2,6},{3,7},{4,0},{5,1},{6,2},{7,3},{8,12},{9,13},{10,... | collective-permute-start | bytes 1572872 | tf_op jit(solution)/shard_map/ppermute | solution.py:706
  216.3 4.2 %collective-permute-start.55 = (f32[1024,512]{1,0:T(8,128)S(1)}, f32[1024,512]{1,0:T(8,128)S(1)}, u32[]{:S(2)}, u32[]{:S(2)}) collective-permute-start(f32[1024,512]{1,0:T(8,128)S(1)} %unfold_sides.7.refs_0_), channel_id=1, source_target_pairs={{0,1},{1,0},{2,3},{3,2},{4,5},{5,4},{6,7},{7,6},{8,9},{9,8},{10,11... | collective-permute-start | bytes 6291464 | tf_op jit(solution)/shard_map/ppermute | solution.py:706
  (17 other events, 143.6 us)
where the time goes:
time: 223 us
  waiting for transfers between devices  80.8 us (36%)
  starting transfers between devices  51.5 us (23%)
  Pallas kernels  46.9 us (21%)
  blocking collectives  35.6 us (16%)
  local copies, waits for them, and re-layouts  4.39 us (2%)
  other arithmetic  2.35 us (1%)
    ppermute x33, waiting for transfers between devices, swap(): lax.ppermute(value, axis, [(i, i ^ bit) for i in range(lax.axis_size(axis...  52.3 us
    pallas_call x32, Pallas kernels, run(): pl.pallas_call(body, name=name, out_shape=tuple((jax.ShapeDtypeStruct(*ou...  39.9 us
    all_gather x4, blocking collectives, gather_row(): return lax.all_gather(value, 'seq')  35.6 us
    ppermute x23, waiting for transfers between devices, shifted(): return lax.ppermute(value, name, pairs)  28.5 us
    ppermute x33, starting transfers between devices, swap(): lax.ppermute(value, axis, [(i, i ^ bit) for i in range(lax.axis_size(axis...  26.5 us
    ppermute x23, starting transfers between devices, shifted(): return lax.ppermute(value, name, pairs)  25 us
    pallas_call x3, Pallas kernels, put_in_place(): pl.pallas_call(body, name='put_in_place', out_shape=tuple((jax.ShapeDtype...  7.06 us
  transfers between devices with their start and end apart: 56, of which 40 were waited for; matrix products, arithmetic and copies ran while one was open for 2% of the time, Pallas kernels for 9%

commit v1 on v0

--- a/solution.py
+++ b/solution.py
@@ -36,7 +36,7 @@
     def one(index, carry):
         return body(pl.multiple_of(index * step, step), carry)
 
-    return lax.fori_loop(0, count // step, one, init)
+    return lax.fori_loop(0, count // step, one, init, unroll=2)
 
 
 def documents(here, batches, span, count):
@@ -141,7 +141,7 @@
             more = visit(more, batch, None, first, start, keeps, None)
         return tuple(states), more
 
-    return lax.fori_loop(0, steps // 2, pair, (tuple(init), extra), unroll=2)
+    return lax.fori_loop(0, steps // 2, pair, (tuple(init), extra), unroll=4)
 
 
 def zero_states(batches, groups):
@@ -1104,17 +1104,16 @@
     block_out = order(result1, True)
     final = (((2, width, width), f32), ((2, 2 * half, width), f32), ((2, width, 2 * half), f32))
     placed = put_in_place(1, here, ((False, own1), (True, other1)), final, ())
-    last_sums, bits = sum(last_terms), bits_of(lax.axis_size("dp"))
-    for bit in bits[:-1]:
-        last_sums = last_sums + swap(last_sums, "dp", bit)
-    last_sums, block_out, *placed = wait_for(lower_sum, last_sums, block_out, *placed)
+    summed = sum(last_terms)
+    for bit in bits_of(lax.axis_size("dp")):
+        summed = summed + swap(summed, "dp", bit)
+    summed, block_out = wait_for(lower_sum, summed, block_out)
 
     for stage in range(len(lower_sum.plane) - 1, 0, -1):
         lower_sum.up_plane(stage)
         if stage == 1:
-            (last_sums,) = lower_sum.after(last_sums)
+            (summed,) = lower_sum.after(summed)
         lower_sum.swap_plane(stage - 1)
-    summed = last_sums + swap(last_sums, "dp", bits[-1])
     grad_input, shared0 = run(
         part(last_step, lower),
         "last_step",
@@ -1126,8 +1125,8 @@
     small_sum = summed[CHUNKS:].reshape(2, CHUNKS, width)
     _, pullback = jax.vjp(discretize, lam_re, lam_im, log_step)
     grad_lr, grad_li, grad_ls = pullback(tuple(small_sum[:, kind, :half] for kind in range(4)))
-    grad_input, grad_lr, grad_li, grad_ls = wait_for(
-        lower_sum, grad_input, grad_lr, grad_li, grad_ls
+    grad_input, grad_lr, grad_li, grad_ls, *placed = wait_for(
+        lower_sum, grad_input, grad_lr, grad_li, grad_ls, *placed
     )
 
     lower_sum.up_plane(0)

time: 223 us -> 222 us (level)
  transfers between devices with their start and end apart: 56 -> 56, of which waited for: 40 -> 38; matrix products, arithmetic and copies ran while one was open for 2% -> 2% of each run, Pallas kernels for 9% -> 9%
where the time goes in v1:
time: 222 us; the launch traced here: 221 us
  waiting for transfers between devices  79.5 us (36%)
  starting transfers between devices  52.3 us (24%)
  Pallas kernels  46 us (21%)
  blocking collectives  35.6 us (16%)
  local copies, waits for them, and re-layouts  4.39 us (2%)
  other arithmetic  2.35 us (1%)
    ppermute x33, waiting for transfers between devices, swap(): lax.ppermute(value, axis, [(i, i ^ bit) for i in range(lax.axis_size(axis...  51.1 us
    pallas_call x32, Pallas kernels, run(): pl.pallas_call(body, name=name, out_shape=tuple((jax.ShapeDtypeStruct(*ou...  38.9 us
    all_gather x4, blocking collectives, gather_row(): return lax.all_gather(value, 'seq')  35.6 us
    ppermute x23, waiting for transfers between devices, shifted(): return lax.ppermute(value, name, pairs)  28.4 us
    ppermute x33, starting transfers between devices, swap(): lax.ppermute(value, axis, [(i, i ^ bit) for i in range(lax.axis_size(axis...  27.4 us
    ppermute x23, starting transfers between devices, shifted(): return lax.ppermute(value, name, pairs)  25 us
    pallas_call x3, Pallas kernels, put_in_place(): pl.pallas_call(body, name='put_in_place', out_shape=tuple((jax.ShapeDtype...  7.06 us
  transfers between devices with their start and end apart: 56, of which 38 were waited for; matrix products, arithmetic and copies ran while one was open for 2% of the time, Pallas kernels for 9%

profile of v1, /device:TPU:0, one launch (start us, length us, event | category | flops | bytes accessed | tf_op | source)
XLA Modules:
  0.0 221.3 jit_solution(7425246818758980540)
XLA Ops:
  4.2 3.8 %collective-permute-start.3 = (f32[4,512]{1,0:T(4,128)S(1)}, f32[4,512]{1,0:T(4,128)S(1)}, u32[]{:S(2)}, u32[]{:S(2)}) collective-permute-start(f32[4,512]{1,0:T(4,128)S(1)} %add.63), channel_id=1, source_target_pairs={{0,6},{1,7},{2,0},{3,1},{4,2},{5,3},{6,4},{7,5},{8,14},{9,15},{10,... | collective-permute-start | bytes 24584 | tf_op jit(solution)/shard_map/ppermute | solution.py:677
  9.9 1.8 collective-permute-done.2
  13.1 3.6 %collective-permute-start.6 = (f32[4,512]{1,0:T(4,128)S(1)}, f32[4,512]{1,0:T(4,128)S(1)}, u32[]{:S(2)}, u32[]{:S(2)}) collective-permute-start(f32[4,512]{1,0:T(4,128)S(1)} %add_add_fusion.3.stats_0_), channel_id=1, source_target_pairs={{0,24},{8,0},{16,8},{24,16},{1,25},{9,1},{17,9},{25,17},{2,26},{10... | collective-permute-start | bytes 24584 | tf_op jit(solution)/shard_map/ppermute | solution.py:677
  18.7 2.5 %collective-permute-done.5.stats_2_ = f32[4,512]{1,0:T(4,128)S(1)} collective-permute-done((f32[4,512]{1,0:T(4,128)S(1)}, f32[4,512]{1,0:T(4,128)S(1)}, u32[]{:S(2)}, u32[]{:S(2)}) %collective-permute-start.5) | collective-permute-done | bytes 8224 | tf_op jit(solution)/shard_map/ppermute | solution.py:677
  22.1 1.9 enter_layer.2
  24.1 9.2 %all-gather.4.ends = f32[8,2,768]{2,1,0:T(2,128)S(1)} all-gather(f32[1,2,768]{2,1,0:T(2,128)S(1)} %bitcast.90), channel_id=2, replica_groups=mesh['dp'=4,'seq'=8] {'seq'}, dimensions={0}, use_global_device_ids=true | all-gather | bytes 55296 | tf_op jit(solution)/shard_map/all_gather | solution.py:953
  34.5 3.6 %middle_forward.1 = (f32[528,768]{1,0:T(8,128)S(1)}, bf16[512,768]{1,0:T(8,128)(2,1)S(1)}, bf16[512,512]{1,0:T(8,128)(2,1)S(1)}, f32[512,512]{1,0:T(8,128)S(1)},...) custom-call(s32[10]{0:T(128)S(1)} %pad_add_fusion.place.here.refs_0_, ...), custom_call_target="tpu_custom_call" | custom-call | tf_op jit(solution)/shard_map/middle_forward/pallas_call | solution.py:605
  47.0 2.0 collective-permute-start.11
  49.5 1.5 collective-permute-done.12.stats_2_
  51.0 1.5 collective-permute-done.11.stats_1_
  52.5 1.9 enter_layer.3
  54.4 9.2 %all-gather.5.ends = f32[8,2,768]{2,1,0:T(2,128)S(1)} all-gather(f32[1,2,768]{2,1,0:T(2,128)S(1)} %bitcast.91), channel_id=3, replica_groups=mesh['dp'=4,'seq'=8] {'seq'}, dimensions={0}, use_global_device_ids=true | all-gather | bytes 55296 | tf_op jit(solution)/shard_map/all_gather | solution.py:953
  63.6 5.9 %turn_around.1 = (bf16[512,512]{1,0:T(8,128)(2,1)S(1)}, f32[528,768]{1,0:T(8,128)S(1)}, bf16[512,768]{1,0:T(8,128)(2,1)S(1)}, bf16[512,512]{1,0:T(8,128)(2,1)S(1...) custom-call(s32[10]{0:T(128)S(1)} %pad_add_fusion.place.here.refs_0_, ...), custom_call_target="tpu_custom_call" | custom-call | tf_op jit(solution)/shard_map/turn_around/pallas_call | solution.py:605
  69.5 8.1 %all-gather.6.ends = f32[8,2,768]{2,1,0:T(2,128)S(1)} all-gather(f32[1,2,768]{2,1,0:T(2,128)S(1)} %bitcast.89), channel_id=4, replica_groups=mesh['dp'=4,'seq'=8] {'seq'}, dimensions={0}, use_global_device_ids=true | all-gather | bytes 55296 | tf_op jit(solution)/shard_map/all_gather | solution.py:953
  77.6 2.8 %backward_finish.2 = (bf16[512,768]{1,0:T(8,128)(2,1)S(1)}, f32[512,512]{1,0:T(8,128)S(1)}, f32[4,512]{1,0:T(4,128)S(1)}, f32[8,512]{1,0:T(8,128)S(1)}) custom-call(s32[10]{0:T(128)S(1)} %pad_add_fusion.place.here.refs_0_, f32[8,2,768]{2,1,0:T(2,128)S(1)} %all-gather.6.ends, f32[2,16,768]{2,1,0:T(8,128)S(1)} %get-tuple-element.249.prefix, ...), custom_call_target="tpu_custom_call" | custom-call | tf_op jit(solution)/shard_map/backward_finish/pallas_call | solution.py:605
  80.8 1.8 all_weights.1
  82.9 1.5 collective-permute-start.17
  84.4 1.5 collective-permute-start.16
  88.1 2.4 %collective-permute-done.15 = f32[4,512]{1,0:T(4,128)S(1)} collective-permute-done((f32[4,512]{1,0:T(4,128)S(1)}, f32[4,512]{1,0:T(4,128)S(1)}, u32[]{:S(2)}, u32[]{:S(2)}) %collective-permute-start.15) | collective-permute-done | bytes 8224 | tf_op jit(solution)/shard_map/ppermute | solution.py:677
  95.6 2.3 %collective-permute-done.22.stats_2_ = f32[4,512]{1,0:T(4,128)S(1)} collective-permute-done((f32[4,512]{1,0:T(4,128)S(1)}, f32[4,512]{1,0:T(4,128)S(1)}, u32[]{:S(2)}, u32[]{:S(2)}) %collective-permute-start.22) | collective-permute-done | bytes 8224 | tf_op jit(solution)/shard_map/ppermute | solution.py:677
  99.1 3.3 %between_layers.1 = (f32[512,512]{1,0:T(8,128)S(1)}, f32[2,512]{1,0:T(2,128)S(1)}, bf16[512,512]{1,0:T(8,128)(2,1)S(1)}, f32[512,512]{1,0:T(8,128)S(1)}, bf16[51...) custom-call(s32[10]{0:T(128)S(1)} %pad_add_fusion.place.here.refs_0_, ...), custom_call_target="tpu_custom_call" | custom-call | tf_op jit(solution)/shard_map/between_layers/pallas_call | solution.py:605
  102.4 1.5 collective-permute-done.19.refs_1_
  105.2 1.7 collective-permute-start.25
  106.8 9.2 %all-gather.7.refs_1_ = f32[8,2,768]{2,1,0:T(2,128)S(1)} all-gather(f32[1,2,768]{2,1,0:T(2,128)S(1)} %bitcast.88), channel_id=5, replica_groups=mesh['dp'=4,'seq'=8] {'seq'}, dimensions={0}, use_global_device_ids=true | all-gather | bytes 55296 | tf_op jit(solution)/shard_map/all_gather | solution.py:953
  118.6 2.8 %backward_finish.3 = (bf16[512,768]{1,0:T(8,128)(2,1)S(1)}, f32[512,512]{1,0:T(8,128)S(1)}, f32[24,512]{1,0:T(8,128)S(1)}) custom-call(s32[10]{0:T(128)S(1)} %pad_add_fusion.place.here.refs_0_, f32[8,2,768]{2,1,0:T(2,128)S(1)} %all-gather.7.refs_1_, f32[2,16,768]{2,1,0:T(8,128)S(1)} %get-tuple-element.316.refs_2_, ...), custom_call_target="tpu_custom_call" | custom-call | tf_op jit(solution)/shard_map/backward_finish/pallas_call | solution.py:605
  122.2 4.6 %collective-permute-done.26.found = f32[128,512]{1,0:T(8,128)S(1)} collective-permute-done((f32[128,512]{1,0:T(8,128)S(1)}, f32[128,512]{1,0:T(8,128)S(1)}, u32[]{:S(2)}, u32[]{:S(2)}) %collective-permute-start.26) | collective-permute-done | bytes 262176 | tf_op jit(solution)/shard_map/ppermute | solution.py:706
  128.1 1.6 collective-permute-start.29
  133.7 10.9 %collective-permute-done.28.found = f32[128,512]{1,0:T(8,128)S(1)} collective-permute-done((f32[128,512]{1,0:T(8,128)S(1)}, f32[128,512]{1,0:T(8,128)S(1)}, u32[]{:S(2)}, u32[]{:S(2)}) %collective-permute-start.28) | collective-permute-done | bytes 262176 | tf_op jit(solution)/shard_map/ppermute | solution.py:706
  145.4 1.6 collective-permute-start.35
  147.5 5.4 %collective-permute-done.34.found = f32[128,512]{1,0:T(8,128)S(1)} collective-permute-done((f32[128,512]{1,0:T(8,128)S(1)}, f32[128,512]{1,0:T(8,128)S(1)}, u32[]{:S(2)}, u32[]{:S(2)}) %collective-permute-start.34) | collective-permute-done | bytes 262176 | tf_op jit(solution)/shard_map/ppermute | solution.py:706
  156.1 1.6 collective-permute-start.38
  158.3 1.8 collective-permute-start.39
  160.1 2.6 %collective-permute-done.37.refs_1_ = f32[256,256]{1,0:T(8,128)S(1)} collective-permute-done((f32[256,256]{1,0:T(8,128)S(1)}, f32[256,256]{1,0:T(8,128)S(1)}, u32[]{:S(2)}, u32[]{:S(2)}) %collective-permute-start.37) | collective-permute-done | bytes 262176 | tf_op jit(solution)/shard_map/ppermute | solution.py:706
  163.0 1.9 collective-permute-done.39.found
  167.6 1.8 collective-permute-start.42
  169.4 9.8 %collective-permute-done.42.found = f32[128,512]{1,0:T(8,128)S(1)} collective-permute-done((f32[128,512]{1,0:T(8,128)S(1)}, f32[128,512]{1,0:T(8,128)S(1)}, u32[]{:S(2)}, u32[]{:S(2)}) %collective-permute-start.42) | collective-permute-done | bytes 262176 | tf_op jit(solution)/shard_map/ppermute | solution.py:706
  180.6 1.6 collective-permute-start.47
  184.7 2.0 collective-permute-done.46
  190.7 2.0 collective-permute-start.50
  192.7 2.1 collective-permute-done.50
  194.8 2.1 collective-permute-start.51
  198.1 2.1 collective-permute-done.51
  200.8 1.8 collective-permute-start.52
  203.4 1.6 last_step.1
  205.7 2.9 %put_in_place.3 = (f32[2,512,512]{2,1,0:T(8,128)}, f32[2,768,512]{2,1,0:T(8,128)}, f32[2,512,768]{2,1,0:T(8,128)}) custom-call(s32[10]{0:T(128)S(1)} %pad_add_fusion.place.here.refs_0_, f32[1024,512]{1,0:T(8,128)S(1)} %unfold_sides.5.refs_0_, f32[1024,512]{1,0:T(8,128)S(1)} %collective-permute-done.54.refs_1_), custom_call_target="tpu_custom_call" | custom-call | tf_op jit(solution)/shard_map/put_in_place/pallas_call | solution.py:651
  208.6 4.3 %collective-permute-done.52.refs_1_ = f32[512,256]{1,0:T(8,128)S(1)} collective-permute-done((f32[512,256]{1,0:T(8,128)S(1)}, f32[512,256]{1,0:T(8,128)S(1)}, u32[]{:S(2)}, u32[]{:S(2)}) %collective-permute-start.52) | collective-permute-done | bytes 524320 | tf_op jit(solution)/shard_map/ppermute | solution.py:706
  216.3 2.1 put_in_place.4
  219.2 2.1 put_in_place.5
  (143 shorter events, 62.7 us)
Async XLA Ops:
  4.2 5.7 %collective-permute-start.3 = (f32[4,512]{1,0:T(4,128)S(1)}, f32[4,512]{1,0:T(4,128)S(1)}, u32[]{:S(2)}, u32[]{:S(2)}) collective-permute-start(f32[4,512]{1,0:T(4,128)S(1)} %add.63), channel_id=1, source_target_pairs={{0,6},{1,7},{2,0},{3,1},{4,2},{5,3},{6,4},{7,5},{8,14},{9,15},{10,... | collective-permute-start | bytes 24584 | tf_op jit(solution)/shard_map/ppermute | solution.py:677
  8.0 3.7 %collective-permute-start.2 = (f32[4,512]{1,0:T(4,128)S(1)}, f32[4,512]{1,0:T(4,128)S(1)}, u32[]{:S(2)}, u32[]{:S(2)}) collective-permute-start(f32[4,512]{1,0:T(4,128)S(1)} %add.63), channel_id=1, source_target_pairs={{0,4},{1,5},{2,6},{3,7},{4,0},{5,1},{6,2},{7,3},{8,12},{9,13},{10,... | collective-permute-start | bytes 24584 | tf_op jit(solution)/shard_map/ppermute | solution.py:677
  8.5 4.5 %collective-permute-start.1 = (f32[4,512]{1,0:T(4,128)S(1)}, f32[4,512]{1,0:T(4,128)S(1)}, u32[]{:S(2)}, u32[]{:S(2)}) collective-permute-start(f32[4,512]{1,0:T(4,128)S(1)} %add.63), channel_id=1, source_target_pairs={{0,2},{1,3},{2,4},{3,5},{4,6},{5,7},{6,0},{7,1},{8,10},{9,11},{10,... | collective-permute-start | bytes 24584 | tf_op jit(solution)/shard_map/ppermute | solution.py:677
  13.1 5.7 %collective-permute-start.6 = (f32[4,512]{1,0:T(4,128)S(1)}, f32[4,512]{1,0:T(4,128)S(1)}, u32[]{:S(2)}, u32[]{:S(2)}) collective-permute-start(f32[4,512]{1,0:T(4,128)S(1)} %add_add_fusion.3.stats_0_), channel_id=1, source_target_pairs={{0,24},{8,0},{16,8},{24,16},{1,25},{9,1},{17,9},{25,17},{2,26},{10... | collective-permute-start | bytes 24584 | tf_op jit(solution)/shard_map/ppermute | solution.py:677
  16.7 4.5 %collective-permute-start.5 = (f32[4,512]{1,0:T(4,128)S(1)}, f32[4,512]{1,0:T(4,128)S(1)}, u32[]{:S(2)}, u32[]{:S(2)}) collective-permute-start(f32[4,512]{1,0:T(4,128)S(1)} %add_add_fusion.3.stats_0_), channel_id=1, source_target_pairs={{0,16},{8,24},{16,0},{24,8},{1,17},{9,25},{17,1},{25,9},{2,18},{10... | collective-permute-start | bytes 24584 | tf_op jit(solution)/shard_map/ppermute | solution.py:677
  16.7 5.4 %collective-permute-start.4 = (f32[4,512]{1,0:T(4,128)S(1)}, f32[4,512]{1,0:T(4,128)S(1)}, u32[]{:S(2)}, u32[]{:S(2)}) collective-permute-start(f32[4,512]{1,0:T(4,128)S(1)} %add_add_fusion.3.stats_0_), channel_id=1, source_target_pairs={{0,8},{8,16},{16,24},{24,0},{1,9},{9,17},{17,25},{25,1},{2,10},{10... | collective-permute-start | bytes 24584 | tf_op jit(solution)/shard_map/ppermute | solution.py:677
  39.3 3.7 %collective-permute-start.10 = (f32[4,512]{1,0:T(4,128)S(1)}, f32[4,512]{1,0:T(4,128)S(1)}, u32[]{:S(2)}, u32[]{:S(2)}) collective-permute-start(f32[4,512]{1,0:T(4,128)S(1)} %add.69), channel_id=1, source_target_pairs={{0,6},{1,7},{2,0},{3,1},{4,2},{5,3},{6,4},{7,5},{8,14},{9,15},{10,... | collective-permute-start | bytes 24584 | tf_op jit(solution)/shard_map/ppermute | solution.py:677
  40.8 3.7 %collective-permute-start.9 = (f32[4,512]{1,0:T(4,128)S(1)}, f32[4,512]{1,0:T(4,128)S(1)}, u32[]{:S(2)}, u32[]{:S(2)}) collective-permute-start(f32[4,512]{1,0:T(4,128)S(1)} %add.69), channel_id=1, source_target_pairs={{0,4},{1,5},{2,6},{3,7},{4,0},{5,1},{6,2},{7,3},{8,12},{9,13},{10,... | collective-permute-start | bytes 24584 | tf_op jit(solution)/shard_map/ppermute | solution.py:677
  41.3 4.5 %collective-permute-start.8 = (f32[4,512]{1,0:T(4,128)S(1)}, f32[4,512]{1,0:T(4,128)S(1)}, u32[]{:S(2)}, u32[]{:S(2)}) collective-permute-start(f32[4,512]{1,0:T(4,128)S(1)} %add.69), channel_id=1, source_target_pairs={{0,2},{1,3},{2,4},{3,5},{4,6},{5,7},{6,0},{7,1},{8,10},{9,11},{10,... | collective-permute-start | bytes 24584 | tf_op jit(solution)/shard_map/ppermute | solution.py:677
  46.4 4.5 %collective-permute-start.12 = (f32[4,512]{1,0:T(4,128)S(1)}, f32[4,512]{1,0:T(4,128)S(1)}, u32[]{:S(2)}, u32[]{:S(2)}) collective-permute-start(f32[4,512]{1,0:T(4,128)S(1)} %add_add_fusion.2.stats_0_), channel_id=1, source_target_pairs={{0,16},{8,24},{16,0},{24,8},{1,17},{9,25},{17,1},{25,9},{2,18},{10... | collective-permute-start | bytes 24584 | tf_op jit(solution)/shard_map/ppermute | solution.py:677
  47.0 5.4 %collective-permute-start.11 = (f32[4,512]{1,0:T(4,128)S(1)}, f32[4,512]{1,0:T(4,128)S(1)}, u32[]{:S(2)}, u32[]{:S(2)}) collective-permute-start(f32[4,512]{1,0:T(4,128)S(1)} %add_add_fusion.2.stats_0_), channel_id=1, source_target_pairs={{0,8},{8,16},{16,24},{24,0},{1,9},{9,17},{17,25},{25,1},{2,10},{10... | collective-permute-start | bytes 24584 | tf_op jit(solution)/shard_map/ppermute | solution.py:677
  82.7 7.8 %collective-permute-start.18 = (f32[1024,512]{1,0:T(8,128)S(1)}, f32[1024,512]{1,0:T(8,128)S(1)}, u32[]{:S(2)}, u32[]{:S(2)}) collective-permute-start(f32[1024,512]{1,0:T(8,128)S(1)} %get-tuple-element.264), channel_id=1, source_target_pairs={{0,1},{1,0},{2,3},{3,2},{4,5},{5,4},{6,7},{7,6},{8,9},{9,8},{10,11... | collective-permute-start | bytes 6291464 | tf_op jit(solution)/shard_map/ppermute | solution.py:706
  82.9 3.7 %collective-permute-start.17 = (f32[4,512]{1,0:T(4,128)S(1)}, f32[4,512]{1,0:T(4,128)S(1)}, u32[]{:S(2)}, u32[]{:S(2)}) collective-permute-start(f32[4,512]{1,0:T(4,128)S(1)} %add.73), channel_id=1, source_target_pairs={{0,6},{1,7},{2,0},{3,1},{4,2},{5,3},{6,4},{7,5},{8,14},{9,15},{10,... | collective-permute-start | bytes 24584 | tf_op jit(solution)/shard_map/ppermute | solution.py:677
  84.4 3.7 %collective-permute-start.16 = (f32[4,512]{1,0:T(4,128)S(1)}, f32[4,512]{1,0:T(4,128)S(1)}, u32[]{:S(2)}, u32[]{:S(2)}) collective-permute-start(f32[4,512]{1,0:T(4,128)S(1)} %add.73), channel_id=1, source_target_pairs={{0,4},{1,5},{2,6},{3,7},{4,0},{5,1},{6,2},{7,3},{8,12},{9,13},{10,... | collective-permute-start | bytes 24584 | tf_op jit(solution)/shard_map/ppermute | solution.py:677
  85.9 4.5 %collective-permute-start.15 = (f32[4,512]{1,0:T(4,128)S(1)}, f32[4,512]{1,0:T(4,128)S(1)}, u32[]{:S(2)}, u32[]{:S(2)}) collective-permute-start(f32[4,512]{1,0:T(4,128)S(1)} %add.73), channel_id=1, source_target_pairs={{0,2},{1,3},{2,4},{3,5},{4,6},{5,7},{6,0},{7,1},{8,10},{9,11},{10,... | collective-permute-start | bytes 24584 | tf_op jit(solution)/shard_map/ppermute | solution.py:677
  91.3 12.5 %collective-permute-start.19 = (f32[512,256]{1,0:T(8,128)S(1)}, f32[512,256]{1,0:T(8,128)S(1)}, u32[]{:S(2)}, u32[]{:S(2)}) collective-permute-start(f32[512,256]{1,0:T(8,128)S(1)} %get-tuple-element.270), channel_id=1, source_target_pairs={{0,2},{1,3},{2,0},{3,1},{4,6},{5,7},{6,4},{7,5},{8,10},{9,11},{10,... | collective-permute-start | bytes 1572872 | tf_op jit(solution)/shard_map/ppermute | solution.py:706
  91.4 12.5 %collective-permute-start.20 = (f32[512,256]{1,0:T(8,128)S(1)}, f32[512,256]{1,0:T(8,128)S(1)}, u32[]{:S(2)}, u32[]{:S(2)}) collective-permute-start(f32[512,256]{1,0:T(8,128)S(1)} %get-tuple-element.272), channel_id=1, source_target_pairs={{0,4},{1,5},{2,6},{3,7},{4,0},{5,1},{6,2},{7,3},{8,12},{9,13},{10,... | collective-permute-start | bytes 1572872 | tf_op jit(solution)/shard_map/ppermute | solution.py:706
  93.4 4.6 %collective-permute-start.22 = (f32[4,512]{1,0:T(4,128)S(1)}, f32[4,512]{1,0:T(4,128)S(1)}, u32[]{:S(2)}, u32[]{:S(2)}) collective-permute-start(f32[4,512]{1,0:T(4,128)S(1)} %add_add_fusion.1.stats_0_), channel_id=1, source_target_pairs={{0,16},{8,24},{16,0},{24,8},{1,17},{9,25},{17,1},{25,9},{2,18},{10... | collective-permute-start | bytes 24584 | tf_op jit(solution)/shard_map/ppermute | solution.py:677
  93.6 5.4 %collective-permute-start.21 = (f32[4,512]{1,0:T(4,128)S(1)}, f32[4,512]{1,0:T(4,128)S(1)}, u32[]{:S(2)}, u32[]{:S(2)}) collective-permute-start(f32[4,512]{1,0:T(4,128)S(1)} %add_add_fusion.1.stats_0_), channel_id=1, source_target_pairs={{0,8},{8,16},{16,24},{24,0},{1,9},{9,17},{17,25},{25,1},{2,10},{10... | collective-permute-start | bytes 24584 | tf_op jit(solution)/shard_map/ppermute | solution.py:677
  104.6 11.4 %collective-permute-start.24 = (f32[256,256]{1,0:T(8,128)S(1)}, f32[256,256]{1,0:T(8,128)S(1)}, u32[]{:S(2)}, u32[]{:S(2)}) collective-permute-start(f32[256,256]{1,0:T(8,128)S(1)} %get-tuple-element.290), channel_id=1, source_target_pairs={{0,4},{1,5},{2,6},{3,7},{4,0},{5,1},{6,2},{7,3},{8,12},{9,13},{10,... | collective-permute-start | bytes 786440 | tf_op jit(solution)/shard_map/ppermute | solution.py:706
  105.2 10.8 %collective-permute-start.25 = (f32[256,256]{1,0:T(8,128)S(1)}, f32[256,256]{1,0:T(8,128)S(1)}, u32[]{:S(2)}, u32[]{:S(2)}) collective-permute-start(f32[256,256]{1,0:T(8,128)S(1)} %get-tuple-element.292), channel_id=1, source_target_pairs={{0,2},{1,3},{2,0},{3,1},{4,6},{5,7},{6,4},{7,5},{8,10},{9,11},{10,... | collective-permute-start | bytes 786440 | tf_op jit(solution)/shard_map/ppermute | solution.py:706
  118.4 8.4 %collective-permute-start.26 = (f32[128,512]{1,0:T(8,128)S(1)}, f32[128,512]{1,0:T(8,128)S(1)}, u32[]{:S(2)}, u32[]{:S(2)}) collective-permute-start(f32[128,512]{1,0:T(8,128)S(1)} %get-tuple-element.304), channel_id=1, source_target_pairs={{0,8},{8,0},{16,24},{24,16},{1,9},{9,1},{17,25},{25,17},{2,10},{10... | collective-permute-start | bytes 786440 | tf_op jit(solution)/shard_map/ppermute | solution.py:706
  128.1 16.5 %collective-permute-start.29 = (f32[320,256]{1,0:T(8,128)S(1)}, f32[320,256]{1,0:T(8,128)S(1)}, u32[]{:S(2)}, u32[]{:S(2)}) collective-permute-start(f32[320,256]{1,0:T(8,128)S(1)} %get-tuple-element.327), channel_id=1, source_target_pairs={{0,2},{1,3},{2,0},{3,1},{4,6},{5,7},{6,4},{7,5},{8,10},{9,11},{10,... | collective-permute-start | bytes 983048 | tf_op jit(solution)/shard_map/ppermute | solution.py:706
  129.6 14.9 %collective-permute-start.30 = (f32[320,256]{1,0:T(8,128)S(1)}, f32[320,256]{1,0:T(8,128)S(1)}, u32[]{:S(2)}, u32[]{:S(2)}) collective-permute-start(f32[320,256]{1,0:T(8,128)S(1)} %get-tuple-element.329), channel_id=1, source_target_pairs={{0,4},{1,5},{2,6},{3,7},{4,0},{5,1},{6,2},{7,3},{8,12},{9,13},{10,... | collective-permute-start | bytes 983048 | tf_op jit(solution)/shard_map/ppermute | solution.py:706
  130.2 14.4 %collective-permute-start.28 = (f32[128,512]{1,0:T(8,128)S(1)}, f32[128,512]{1,0:T(8,128)S(1)}, u32[]{:S(2)}, u32[]{:S(2)}) collective-permute-start(f32[128,512]{1,0:T(8,128)S(1)} %add_two.4.own), channel_id=1, source_target_pairs={{0,16},{8,24},{16,0},{24,8},{1,17},{9,25},{17,1},{25,9},{2,18},{10... | collective-permute-start | bytes 786440 | tf_op jit(solution)/shard_map/ppermute | solution.py:706
  131.5 13.0 %collective-permute-start.32 = (f32[192,256]{1,0:T(8,128)S(1)}, f32[192,256]{1,0:T(8,128)S(1)}, u32[]{:S(2)}, u32[]{:S(2)}) collective-permute-start(f32[192,256]{1,0:T(8,128)S(1)} %get-tuple-element.334), channel_id=1, source_target_pairs={{0,2},{1,3},{2,0},{3,1},{4,6},{5,7},{6,4},{7,5},{8,10},{9,11},{10,... | collective-permute-start | bytes 589832 | tf_op jit(solution)/shard_map/ppermute | solution.py:706
  133.0 11.6 %collective-permute-start.33 = (f32[192,256]{1,0:T(8,128)S(1)}, f32[192,256]{1,0:T(8,128)S(1)}, u32[]{:S(2)}, u32[]{:S(2)}) collective-permute-start(f32[192,256]{1,0:T(8,128)S(1)} %get-tuple-element.336), channel_id=1, source_target_pairs={{0,4},{1,5},{2,6},{3,7},{4,0},{5,1},{6,2},{7,3},{8,12},{9,13},{10,... | collective-permute-start | bytes 589832 | tf_op jit(solution)/shard_map/ppermute | solution.py:706
  144.6 8.3 %collective-permute-start.34 = (f32[128,512]{1,0:T(8,128)S(1)}, f32[128,512]{1,0:T(8,128)S(1)}, u32[]{:S(2)}, u32[]{:S(2)}) collective-permute-start(f32[128,512]{1,0:T(8,128)S(1)} %add_two.5.own), channel_id=1, source_target_pairs={{0,8},{8,0},{16,24},{24,16},{1,9},{9,1},{17,25},{25,17},{2,10},{10... | collective-permute-start | bytes 786440 | tf_op jit(solution)/shard_map/ppermute | solution.py:706
  145.4 8.3 %collective-permute-start.35 = (f32[256,256]{1,0:T(8,128)S(1)}, f32[256,256]{1,0:T(8,128)S(1)}, u32[]{:S(2)}, u32[]{:S(2)}) collective-permute-start(f32[256,256]{1,0:T(8,128)S(1)} %get-tuple-element.348), channel_id=1, source_target_pairs={{0,4},{1,5},{2,6},{3,7},{4,0},{5,1},{6,2},{7,3},{8,12},{9,13},{10,... | collective-permute-start | bytes 786440 | tf_op jit(solution)/shard_map/ppermute | solution.py:706
  147.0 7.9 %collective-permute-start.36 = (f32[256,256]{1,0:T(8,128)S(1)}, f32[256,256]{1,0:T(8,128)S(1)}, u32[]{:S(2)}, u32[]{:S(2)}) collective-permute-start(f32[256,256]{1,0:T(8,128)S(1)} %get-tuple-element.350), channel_id=1, source_target_pairs={{0,2},{1,3},{2,0},{3,1},{4,6},{5,7},{6,4},{7,5},{8,10},{9,11},{10,... | collective-permute-start | bytes 786440 | tf_op jit(solution)/shard_map/ppermute | solution.py:706
  155.5 7.1 %collective-permute-start.37 = (f32[256,256]{1,0:T(8,128)S(1)}, f32[256,256]{1,0:T(8,128)S(1)}, u32[]{:S(2)}, u32[]{:S(2)}) collective-permute-start(f32[256,256]{1,0:T(8,128)S(1)} %get-tuple-element.361.refs_0_), channel_id=1, source_target_pairs={{0,4},{1,5},{2,6},{3,7},{4,0},{5,1},{6,2},{7,3},{8,12},{9,13},{10,... | collective-permute-start | bytes 786440 | tf_op jit(solution)/shard_map/ppermute | solution.py:706
  156.1 6.9 %collective-permute-start.38 = (f32[256,256]{1,0:T(8,128)S(1)}, f32[256,256]{1,0:T(8,128)S(1)}, u32[]{:S(2)}, u32[]{:S(2)}) collective-permute-start(f32[256,256]{1,0:T(8,128)S(1)} %get-tuple-element.363.refs_2_), channel_id=1, source_target_pairs={{0,2},{1,3},{2,0},{3,1},{4,6},{5,7},{6,4},{7,5},{8,10},{9,11},{10,... | collective-permute-start | bytes 786440 | tf_op jit(solution)/shard_map/ppermute | solution.py:706
  158.3 6.6 %collective-permute-start.39 = (f32[128,512]{1,0:T(8,128)S(1)}, f32[128,512]{1,0:T(8,128)S(1)}, u32[]{:S(2)}, u32[]{:S(2)}) collective-permute-start(f32[128,512]{1,0:T(8,128)S(1)} %get-tuple-element.360), channel_id=1, source_target_pairs={{0,8},{8,0},{16,24},{24,16},{1,9},{9,1},{17,25},{25,17},{2,10},{10... | collective-permute-start | bytes 786440 | tf_op jit(solution)/shard_map/ppermute | solution.py:706
  165.5 13.7 %collective-permute-start.40 = (f32[512,256]{1,0:T(8,128)S(1)}, f32[512,256]{1,0:T(8,128)S(1)}, u32[]{:S(2)}, u32[]{:S(2)}) collective-permute-start(f32[512,256]{1,0:T(8,128)S(1)} %get-tuple-element.392.refs_0_), channel_id=1, source_target_pairs={{0,2},{1,3},{2,0},{3,1},{4,6},{5,7},{6,4},{7,5},{8,10},{9,11},{10,... | collective-permute-start | bytes 1572872 | tf_op jit(solution)/shard_map/ppermute | solution.py:706
  166.1 13.1 %collective-permute-start.41 = (f32[512,256]{1,0:T(8,128)S(1)}, f32[512,256]{1,0:T(8,128)S(1)}, u32[]{:S(2)}, u32[]{:S(2)}) collective-permute-start(f32[512,256]{1,0:T(8,128)S(1)} %get-tuple-element.394.refs_2_), channel_id=1, source_target_pairs={{0,4},{1,5},{2,6},{3,7},{4,0},{5,1},{6,2},{7,3},{8,12},{9,13},{10,... | collective-permute-start | bytes 1572872 | tf_op jit(solution)/shard_map/ppermute | solution.py:706
  167.6 11.6 %collective-permute-start.42 = (f32[128,512]{1,0:T(8,128)S(1)}, f32[128,512]{1,0:T(8,128)S(1)}, u32[]{:S(2)}, u32[]{:S(2)}) collective-permute-start(f32[128,512]{1,0:T(8,128)S(1)} %add_two.6.own), channel_id=1, source_target_pairs={{0,16},{8,24},{16,0},{24,8},{1,17},{9,25},{17,1},{25,9},{2,18},{10... | collective-permute-start | bytes 786440 | tf_op jit(solution)/shard_map/ppermute | solution.py:706
  179.2 8.7 %collective-permute-start.43 = (f32[128,512]{1,0:T(8,128)S(1)}, f32[128,512]{1,0:T(8,128)S(1)}, u32[]{:S(2)}, u32[]{:S(2)}) collective-permute-start(f32[128,512]{1,0:T(8,128)S(1)} %add_two.7.own), channel_id=1, source_target_pairs={{0,8},{8,0},{16,24},{24,16},{1,9},{9,1},{17,25},{25,17},{2,10},{10... | collective-permute-start | bytes 786440 | tf_op jit(solution)/shard_map/ppermute | solution.py:706
  180.6 4.1 %collective-permute-start.47 = (f32[24,512]{1,0:T(8,128)S(1)}, f32[24,512]{1,0:T(8,128)S(1)}, u32[]{:S(2)}, u32[]{:S(2)}) collective-permute-start(f32[24,512]{1,0:T(8,128)S(1)} %add.77), channel_id=1, source_target_pairs={{0,6},{1,7},{2,0},{3,1},{4,2},{5,3},{6,4},{7,5},{8,14},{9,15},{10,... | collective-permute-start | bytes 147464 | tf_op jit(solution)/shard_map/ppermute | solution.py:677
  182.2 4.6 %collective-permute-start.46 = (f32[24,512]{1,0:T(8,128)S(1)}, f32[24,512]{1,0:T(8,128)S(1)}, u32[]{:S(2)}, u32[]{:S(2)}) collective-permute-start(f32[24,512]{1,0:T(8,128)S(1)} %add.77), channel_id=1, source_target_pairs={{0,4},{1,5},{2,6},{3,7},{4,0},{5,1},{6,2},{7,3},{8,12},{9,13},{10,... | collective-permute-start | bytes 147464 | tf_op jit(solution)/shard_map/ppermute | solution.py:677
  182.9 5.0 %collective-permute-start.45 = (f32[24,512]{1,0:T(8,128)S(1)}, f32[24,512]{1,0:T(8,128)S(1)}, u32[]{:S(2)}, u32[]{:S(2)}) collective-permute-start(f32[24,512]{1,0:T(8,128)S(1)} %add.77), channel_id=1, source_target_pairs={{0,2},{1,3},{2,4},{3,5},{4,6},{5,7},{6,0},{7,1},{8,10},{9,11},{10,... | collective-permute-start | bytes 147464 | tf_op jit(solution)/shard_map/ppermute | solution.py:677
  189.2 16.5 %collective-permute-start.54 = (f32[1024,512]{1,0:T(8,128)S(1)}, f32[1024,512]{1,0:T(8,128)S(1)}, u32[]{:S(2)}, u32[]{:S(2)}) collective-permute-start(f32[1024,512]{1,0:T(8,128)S(1)} %unfold_sides.5.refs_0_), channel_id=1, source_target_pairs={{0,1},{1,0},{2,3},{3,2},{4,5},{5,4},{6,7},{7,6},{8,9},{9,8},{10,11... | collective-permute-start | bytes 6291464 | tf_op jit(solution)/shard_map/ppermute | solution.py:706
  189.3 10.8 %collective-permute-start.48 = (f32[256,256]{1,0:T(8,128)S(1)}, f32[256,256]{1,0:T(8,128)S(1)}, u32[]{:S(2)}, u32[]{:S(2)}) collective-permute-start(f32[256,256]{1,0:T(8,128)S(1)} %get-tuple-element.399.refs_0_), channel_id=1, source_target_pairs={{0,4},{1,5},{2,6},{3,7},{4,0},{5,1},{6,2},{7,3},{8,12},{9,13},{10,... | collective-permute-start | bytes 786440 | tf_op jit(solution)/shard_map/ppermute | solution.py:706
  190.6 9.5 %collective-permute-start.49 = (f32[256,256]{1,0:T(8,128)S(1)}, f32[256,256]{1,0:T(8,128)S(1)}, u32[]{:S(2)}, u32[]{:S(2)}) collective-permute-start(f32[256,256]{1,0:T(8,128)S(1)} %get-tuple-element.401.refs_2_), channel_id=1, source_target_pairs={{0,2},{1,3},{2,0},{3,1},{4,6},{5,7},{6,4},{7,5},{8,10},{9,11},{10,... | collective-permute-start | bytes 786440 | tf_op jit(solution)/shard_map/ppermute | solution.py:706
  190.7 4.2 %collective-permute-start.50 = (f32[24,512]{1,0:T(8,128)S(1)}, f32[24,512]{1,0:T(8,128)S(1)}, u32[]{:S(2)}, u32[]{:S(2)}) collective-permute-start(f32[24,512]{1,0:T(8,128)S(1)} %add_add_fusion), channel_id=1, source_target_pairs={{0,8},{8,0},{16,24},{24,16},{1,9},{9,1},{17,25},{25,17},{2,10},{10... | collective-permute-start | bytes 147464 | tf_op jit(solution)/shard_map/ppermute | solution.py:706
  194.8 5.3 %collective-permute-start.51 = (f32[24,512]{1,0:T(8,128)S(1)}, f32[24,512]{1,0:T(8,128)S(1)}, u32[]{:S(2)}, u32[]{:S(2)}) collective-permute-start(f32[24,512]{1,0:T(8,128)S(1)} %add.81), channel_id=1, source_target_pairs={{0,16},{8,24},{16,0},{24,8},{1,17},{9,25},{17,1},{25,9},{2,18},{10... | collective-permute-start | bytes 147464 | tf_op jit(solution)/shard_map/ppermute | solution.py:706
  200.8 12.1 %collective-permute-start.52 = (f32[512,256]{1,0:T(8,128)S(1)}, f32[512,256]{1,0:T(8,128)S(1)}, u32[]{:S(2)}, u32[]{:S(2)}) collective-permute-start(f32[512,256]{1,0:T(8,128)S(1)} %get-tuple-element.424.refs_0_), channel_id=1, source_target_pairs={{0,2},{1,3},{2,0},{3,1},{4,6},{5,7},{6,4},{7,5},{8,10},{9,11},{10,... | collective-permute-start | bytes 1572872 | tf_op jit(solution)/shard_map/ppermute | solution.py:706
  202.6 11.6 %collective-permute-start.53 = (f32[512,256]{1,0:T(8,128)S(1)}, f32[512,256]{1,0:T(8,128)S(1)}, u32[]{:S(2)}, u32[]{:S(2)}) collective-permute-start(f32[512,256]{1,0:T(8,128)S(1)} %get-tuple-element.426.refs_2_), channel_id=1, source_target_pairs={{0,4},{1,5},{2,6},{3,7},{4,0},{5,1},{6,2},{7,3},{8,12},{9,13},{10,... | collective-permute-start | bytes 1572872 | tf_op jit(solution)/shard_map/ppermute | solution.py:706
  215.0 4.2 %collective-permute-start.55 = (f32[1024,512]{1,0:T(8,128)S(1)}, f32[1024,512]{1,0:T(8,128)S(1)}, u32[]{:S(2)}, u32[]{:S(2)}) collective-permute-start(f32[1024,512]{1,0:T(8,128)S(1)} %unfold_sides.7.refs_0_), channel_id=1, source_target_pairs={{0,1},{1,0},{2,3},{3,2},{4,5},{5,4},{6,7},{7,6},{8,9},{9,8},{10,11... | collective-permute-start | bytes 6291464 | tf_op jit(solution)/shard_map/ppermute | solution.py:706
  (17 other events, 136.9 us)

commit v2 on v1

--- a/solution.py
+++ b/solution.py
@@ -195,29 +195,32 @@
 
 
 def chunk_carries(meta, gathered, dec, prefix, batches, span, groups, reverse):
-    count = gathered.shape[0]
     half = groups * LANES
     dec_span = power(dec, span)
     row = lax.broadcasted_iota(jnp.int32, (CHUNKS, LANES), 0)
     mine = meta[0][-1]
+    core = lax.rem(mine, 2)
     out = []
     for batch in range(batches):
-
-        def add(at, so_far, batch=batch):
-            away = count - 2 - at
-            if reverse:
-                other = mine + 1 + away
-                reaches = meta[batch][-3] > other * span
-            else:
-                other = mine - 1 - away
-                reaches = meta[batch][-4] < (mine - away) * span
-            other = jnp.clip(other, 0, count - 1)
-            value = jnp.where(reaches, gathered[other, pl.ds(batch, 1), :], 0.0)
-            moved = times(dec_span, so_far)
-            return (moved[0] + value[:, :half], moved[1] + value[:, half:])
-
-        zero = jnp.zeros((1, half), f32)
-        enter = lax.fori_loop(0, count - 1, add, (zero, zero), unroll=count <= 8)
+        enter = (jnp.zeros((1, half), f32), jnp.zeros((1, half), f32))
+        for away in range(len(gathered) - 1, -1, -1):
+            for kind in (1, 0) if reverse else (0, 1):
+                if away == 0 and kind == (0 if reverse else 1):
+                    continue
+                if reverse:
+                    other = mine - core + 2 * away + kind
+                    reaches = meta[batch][-3] > other * span
+                else:
+                    other = mine - core - 2 * away + kind
+                    reaches = meta[batch][-4] < (other + 1) * span
+                same = gathered[away][batch : batch + 1, :]
+                unlike = gathered[away][batches + batch : batches + batch + 1, :]
+                value = jnp.where(reaches, jnp.where(core == kind, same, unlike), 0.0)
+                moved = times(dec_span, enter)
+                after = (moved[0] + value[:, :half], moved[1] + value[:, half:])
+                if away == 0:
+                    after = tuple(jnp.where(core == kind, old, new) for old, new in zip(enter, after))
+                enter = after
         rows = slice(batch * CHUNKS, (batch + 1) * CHUNKS)
         for q in range(groups):
             own = tuple(jnp.broadcast_to(part[:, lanes_of(q)], (CHUNKS, LANES)) for part in enter)
@@ -949,8 +952,12 @@
     line, shared = ((1, width), f32), ((2, width), f32)
     small = ((8, width), f32)
 
-    def gather_row(value):
-        return lax.all_gather(value, "seq")
+    def gather_row(value, reverse):
+        both = jnp.concatenate([value, swap(value, "seq", 1)], axis=0)
+        chips = count // 2
+        return [both] + [
+            shifted(both, plane, chips - away if reverse else away) for away in range(1, chips)
+        ]
 
     (stats,) = run(part(first_sums, batches, span), "first_sums", (x,), (sums,), scalars=0)
 
@@ -976,7 +983,7 @@
     states0, states_low0, act0, sig0, slope0, hidden1, stats = run(
         part(middle_forward, lower),
         "middle_forward",
-        (place, gather_row(total0), prefix0, disc, drive0, u0, ordered, c_proj, norms, w_gate),
+        (place, gather_row(total0, False), prefix0, disc, drive0, u0, ordered, c_proj, norms, w_gate),
         (padded, wide_low, low, flat, flat, flat, sums),
         (flat,),
     )
@@ -992,7 +999,7 @@
         part(turn_around, upper),
         "turn_around",
         (
-            place, gather_row(total1), prefix1, disc, drive1, u1, hidden1, c_proj, norms, w_gate,
+            place, gather_row(total1, True), prefix1, disc, drive1, u1, hidden1, c_proj, norms, w_gate,
             ordered_cot,
         ),
         (low, padded, wide_low, low, low, flat, low, wide, prefix, total, line),
@@ -1006,7 +1013,7 @@
         part(backward_finish, upper),
         "backward_finish",
         (
-            place, gather_row(total1), prefix1, disc, source1, drive1, states1, u1, grad_mixed1,
+            place, gather_row(total1, False), prefix1, disc, source1, drive1, states1, u1, grad_mixed1,
             grad_d1, hidden1, norm1, norms, b_proj,
         ),
         (wide_low, flat, sums, small),
@@ -1039,7 +1046,7 @@
     upper_sum.down_plane(1)
     (total0,) = upper_sum.after(total0)
     upper_sum.to_depth()
-    ends, grad_gate0 = wait_for(upper_sum, gather_row(total0), grad_gate0)
+    ends, grad_gate0 = wait_for(upper_sum, gather_row(total0, True), grad_gate0)
     upper_sum.down_join()
     ends, grad_gate0 = wait_for(upper_sum, ends, grad_gate0)
     upper_sum.scatter_depth()

time: 222 us -> 216 us (0.973)
  blocking collectives: 35.6 us -> 0 us
  starting transfers between devices: 52.3 us -> 69.9 us
  waiting for transfers between devices: 79.5 us -> 92.2 us
    all_gather x4 -> x0, blocking collectives: 35.6 us -> none  [gather_row(): return lax.all_gather(value, 'seq')]
    ppermute x23 -> x35, starting transfers between devices: 25 us -> 39.1 us  [shifted(): return lax.ppermute(value, name, pairs)]
    ppermute x23 -> x35, waiting for transfers between devices: 28.4 us -> 37.7 us  [shifted(): return lax.ppermute(value, name, pairs)]
    ppermute x33 -> x37, waiting for transfers between devices: 51.1 us -> 54.5 us  [swap(): lax.ppermute(value, axis, [(i, i ^ bit) for i in range(lax.axis_size(axis...]
    ppermute x33 -> x37, starting transfers between devices: 27.4 us -> 30.8 us  [swap(): lax.ppermute(value, axis, [(i, i ^ bit) for i in range(lax.axis_size(axis...]
  transfers between devices with their start and end apart: 56 -> 72, of which waited for: 38 -> 50; matrix products, arithmetic and copies ran while one was open for 2% -> 2% of each run, Pallas kernels for 9% -> 9%
where the time goes in v2:
time: 216 us
  waiting for transfers between devices  92.2 us (43%)
  starting transfers between devices  69.9 us (32%)
  Pallas kernels  45.9 us (21%)
  local copies, waits for them, and re-layouts  4.39 us (2%)
  other arithmetic  2.39 us (1%)
    ppermute x37, waiting for transfers between devices, swap(): lax.ppermute(value, axis, [(i, i ^ bit) for i in range(lax.axis_size(axis...  54.5 us
    ppermute x35, starting transfers between devices, shifted(): return lax.ppermute(value, name, pairs)  39.1 us
    pallas_call x32, Pallas kernels, run(): pl.pallas_call(body, name=name, out_shape=tuple((jax.ShapeDtypeStruct(*ou...  38.9 us
    ppermute x35, waiting for transfers between devices, shifted(): return lax.ppermute(value, name, pairs)  37.7 us
    ppermute x37, starting transfers between devices, swap(): lax.ppermute(value, axis, [(i, i ^ bit) for i in range(lax.axis_size(axis...  30.8 us
    pallas_call x3, Pallas kernels, put_in_place(): pl.pallas_call(body, name='put_in_place', out_shape=tuple((jax.ShapeDtype...  7.06 us
  transfers between devices with their start and end apart: 72, of which 50 were waited for; matrix products, arithmetic and copies ran while one was open for 2% of the time, Pallas kernels for 9%

profile of v2, /device:TPU:0, one launch (start us, length us, event | category | flops | bytes accessed | tf_op | source)
XLA Modules:
  0.0 216.0 jit_solution(14239946976999150428)
XLA Ops:
  4.2 3.8 %collective-permute-start.3 = (f32[4,512]{1,0:T(4,128)S(1)}, f32[4,512]{1,0:T(4,128)S(1)}, u32[]{:S(2)}, u32[]{:S(2)}) collective-permute-start(f32[4,512]{1,0:T(4,128)S(1)} %add.63), channel_id=1, source_target_pairs={{0,6},{1,7},{2,0},{3,1},{4,2},{5,3},{6,4},{7,5},{8,14},{9,15},{10,... | collective-permute-start | bytes 24584 | tf_op jit(solution)/shard_map/ppermute | solution.py:680
  9.9 1.8 collective-permute-done.2
  13.1 3.6 %collective-permute-start.6 = (f32[4,512]{1,0:T(4,128)S(1)}, f32[4,512]{1,0:T(4,128)S(1)}, u32[]{:S(2)}, u32[]{:S(2)}) collective-permute-start(f32[4,512]{1,0:T(4,128)S(1)} %add_add_fusion.3.stats_0_), channel_id=1, source_target_pairs={{0,24},{8,0},{16,8},{24,16},{1,25},{9,1},{17,9},{25,17},{2,26},{10... | collective-permute-start | bytes 24584 | tf_op jit(solution)/shard_map/ppermute | solution.py:680
  18.7 2.5 %collective-permute-done.5.stats_2_ = f32[4,512]{1,0:T(4,128)S(1)} collective-permute-done((f32[4,512]{1,0:T(4,128)S(1)}, f32[4,512]{1,0:T(4,128)S(1)}, u32[]{:S(2)}, u32[]{:S(2)}) %collective-permute-start.5) | collective-permute-done | bytes 8224 | tf_op jit(solution)/shard_map/ppermute | solution.py:680
  22.1 1.9 enter_layer.2
  25.4 1.5 collective-permute-start.9
  27.0 1.9 collective-permute-start.8
  29.1 2.4 %collective-permute-done.8.ends_1_ = f32[4,768]{1,0:T(4,128)S(1)} collective-permute-done((f32[4,768]{1,0:T(4,128)S(1)}, f32[4,768]{1,0:T(4,128)S(1)}, u32[]{:S(2)}, u32[]{:S(2)}) %collective-permute-start.8) | collective-permute-done | bytes 12320 | tf_op jit(solution)/shard_map/ppermute | solution.py:680
  32.8 3.6 %middle_forward.1 = (f32[528,768]{1,0:T(8,128)S(1)}, bf16[512,768]{1,0:T(8,128)(2,1)S(1)}, bf16[512,512]{1,0:T(8,128)(2,1)S(1)}, f32[512,512]{1,0:T(8,128)S(1)},...) custom-call(s32[10]{0:T(128)S(1)} %pad_add_fusion.place.here.refs_0_, ...), custom_call_target="tpu_custom_call" | custom-call | tf_op jit(solution)/shard_map/middle_forward/pallas_call | solution.py:608
  42.3 2.4 %collective-permute-done.12 = f32[4,512]{1,0:T(4,128)S(1)} collective-permute-done((f32[4,512]{1,0:T(4,128)S(1)}, f32[4,512]{1,0:T(4,128)S(1)}, u32[]{:S(2)}, u32[]{:S(2)}) %collective-permute-start.12) | collective-permute-done | bytes 8224 | tf_op jit(solution)/shard_map/ppermute | solution.py:680
  45.9 2.0 collective-permute-start.15
  49.8 1.5 collective-permute-done.15.stats_1_
  51.4 1.9 enter_layer.3
  55.2 2.8 %collective-permute-start.19 = (f32[4,768]{1,0:T(4,128)S(1)}, f32[4,768]{1,0:T(4,128)S(1)}, u32[]{:S(2)}, u32[]{:S(2)}) collective-permute-start(f32[4,768]{1,0:T(4,128)S(1)} %pad_maximum_fusion.2.ends_0_), channel_id=1, source_target_pairs={{0,6},{1,7},{2,0},{3,1},{4,2},{5,3},{6,4},{7,5},{8,14},{9,15},{10,... | collective-permute-start | bytes 36872 | tf_op jit(solution)/shard_map/ppermute | solution.py:680
  59.7 5.9 %turn_around.1 = (bf16[512,512]{1,0:T(8,128)(2,1)S(1)}, f32[528,768]{1,0:T(8,128)S(1)}, bf16[512,768]{1,0:T(8,128)(2,1)S(1)}, bf16[512,512]{1,0:T(8,128)(2,1)S(1...) custom-call(s32[10]{0:T(128)S(1)} %pad_add_fusion.place.here.refs_0_, ...), custom_call_target="tpu_custom_call" | custom-call | tf_op jit(solution)/shard_map/turn_around/pallas_call | solution.py:608
  66.9 2.9 %collective-permute-start.25 = (f32[4,768]{1,0:T(4,128)S(1)}, f32[4,768]{1,0:T(4,128)S(1)}, u32[]{:S(2)}, u32[]{:S(2)}) collective-permute-start(f32[4,768]{1,0:T(4,128)S(1)} %pad_maximum_fusion.3.ends_0_), channel_id=1, source_target_pairs={{0,6},{1,7},{2,0},{3,1},{4,2},{5,3},{6,4},{7,5},{8,14},{9,15},{10,... | collective-permute-start | bytes 36872 | tf_op jit(solution)/shard_map/ppermute | solution.py:680
  69.8 1.5 collective-permute-start.24
  71.5 2.0 collective-permute-done.24.ends_2_
  73.5 2.4 %collective-permute-done.23.ends_1_ = f32[4,768]{1,0:T(4,128)S(1)} collective-permute-done((f32[4,768]{1,0:T(4,128)S(1)}, f32[4,768]{1,0:T(4,128)S(1)}, u32[]{:S(2)}, u32[]{:S(2)}) %collective-permute-start.23) | collective-permute-done | bytes 12320 | tf_op jit(solution)/shard_map/ppermute | solution.py:680
  75.9 2.8 %backward_finish.2 = (bf16[512,768]{1,0:T(8,128)(2,1)S(1)}, f32[512,512]{1,0:T(8,128)S(1)}, f32[4,512]{1,0:T(4,128)S(1)}, f32[8,512]{1,0:T(8,128)S(1)}) custom-call(s32[10]{0:T(128)S(1)} %pad_add_fusion.place.here.refs_0_, f32[4,768]{1,0:T(4,128)S(1)} %pad_maximum_fusion.3.ends_0_, f32[4,768]{1,0:T(4,128)S(1)} %collective-permute-done.23.ends_1_, ...), custom_call_target="tpu_custom_call" | custom-call | tf_op jit(solution)/shard_map/backward_finish/pallas_call | solution.py:608
  78.8 1.8 all_weights.1
  81.8 2.0 collective-permute-start.27
  88.3 1.5 collective-permute-start.32
  93.5 2.2 %collective-permute-done.34.stats_2_ = f32[4,512]{1,0:T(4,128)S(1)} collective-permute-done((f32[4,512]{1,0:T(4,128)S(1)}, f32[4,512]{1,0:T(4,128)S(1)}, u32[]{:S(2)}, u32[]{:S(2)}) %collective-permute-start.34) | collective-permute-done | bytes 8224 | tf_op jit(solution)/shard_map/ppermute | solution.py:680
  96.9 3.3 %between_layers.1 = (f32[512,512]{1,0:T(8,128)S(1)}, f32[2,512]{1,0:T(2,128)S(1)}, bf16[512,512]{1,0:T(8,128)(2,1)S(1)}, f32[512,512]{1,0:T(8,128)S(1)}, bf16[51...) custom-call(s32[10]{0:T(128)S(1)} %pad_add_fusion.place.here.refs_0_, ...), custom_call_target="tpu_custom_call" | custom-call | tf_op jit(solution)/shard_map/between_layers/pallas_call | solution.py:608
  101.0 1.8 collective-permute-start.36
  106.3 2.5 %collective-permute-start.39 = (f32[4,768]{1,0:T(4,128)S(1)}, f32[4,768]{1,0:T(4,128)S(1)}, u32[]{:S(2)}, u32[]{:S(2)}) collective-permute-start(f32[4,768]{1,0:T(4,128)S(1)} %pad_maximum_fusion.4.refs_1__0_), channel_id=1, source_target_pairs={{0,6},{1,7},{2,0},{3,1},{4,2},{5,3},{6,4},{7,5},{8,14},{9,15},{10,... | collective-permute-start | bytes 36872 | tf_op jit(solution)/shard_map/ppermute | solution.py:680
  112.5 2.8 %backward_finish.3 = (bf16[512,768]{1,0:T(8,128)(2,1)S(1)}, f32[512,512]{1,0:T(8,128)S(1)}, f32[24,512]{1,0:T(8,128)S(1)}) custom-call(s32[10]{0:T(128)S(1)} %pad_add_fusion.place.here.refs_0_, f32[4,768]{1,0:T(4,128)S(1)} %pad_maximum_fusion.4.refs_1__0_, f32[4,768]{1,0:T(4,128)S(1)} %collective-permute-done.39.refs_1__1_, ...), custom_call_target="tpu_custom_call" | custom-call | tf_op jit(solution)/shard_map/backward_finish/pallas_call | solution.py:608
  116.1 4.9 %collective-permute-done.42.found = f32[128,512]{1,0:T(8,128)S(1)} collective-permute-done((f32[128,512]{1,0:T(8,128)S(1)}, f32[128,512]{1,0:T(8,128)S(1)}, u32[]{:S(2)}, u32[]{:S(2)}) %collective-permute-start.42) | collective-permute-done | bytes 262176 | tf_op jit(solution)/shard_map/ppermute | solution.py:709
  122.3 2.9 %collective-permute-start.45 = (f32[320,256]{1,0:T(8,128)S(1)}, f32[320,256]{1,0:T(8,128)S(1)}, u32[]{:S(2)}, u32[]{:S(2)}) collective-permute-start(f32[320,256]{1,0:T(8,128)S(1)} %get-tuple-element.345), channel_id=1, source_target_pairs={{0,2},{1,3},{2,0},{3,1},{4,6},{5,7},{6,4},{7,5},{8,10},{9,11},{10,... | collective-permute-start | bytes 983048 | tf_op jit(solution)/shard_map/ppermute | solution.py:709
  129.0 11.5 %collective-permute-done.44.found = f32[128,512]{1,0:T(8,128)S(1)} collective-permute-done((f32[128,512]{1,0:T(8,128)S(1)}, f32[128,512]{1,0:T(8,128)S(1)}, u32[]{:S(2)}, u32[]{:S(2)}) %collective-permute-start.44) | collective-permute-done | bytes 262176 | tf_op jit(solution)/shard_map/ppermute | solution.py:709
  142.8 6.1 %collective-permute-done.50.found = f32[128,512]{1,0:T(8,128)S(1)} collective-permute-done((f32[128,512]{1,0:T(8,128)S(1)}, f32[128,512]{1,0:T(8,128)S(1)}, u32[]{:S(2)}, u32[]{:S(2)}) %collective-permute-start.50) | collective-permute-done | bytes 262176 | tf_op jit(solution)/shard_map/ppermute | solution.py:709
  152.9 1.8 collective-permute-start.55
  154.7 3.5 %collective-permute-done.53.refs_1_ = f32[256,256]{1,0:T(8,128)S(1)} collective-permute-done((f32[256,256]{1,0:T(8,128)S(1)}, f32[256,256]{1,0:T(8,128)S(1)}, u32[]{:S(2)}, u32[]{:S(2)}) %collective-permute-start.53) | collective-permute-done | bytes 262176 | tf_op jit(solution)/shard_map/ppermute | solution.py:709
  160.1 1.8 collective-permute-start.56
  163.1 1.9 collective-permute-start.58
  165.0 9.7 %collective-permute-done.58.found = f32[128,512]{1,0:T(8,128)S(1)} collective-permute-done((f32[128,512]{1,0:T(8,128)S(1)}, f32[128,512]{1,0:T(8,128)S(1)}, u32[]{:S(2)}, u32[]{:S(2)}) %collective-permute-start.58) | collective-permute-done | bytes 262176 | tf_op jit(solution)/shard_map/ppermute | solution.py:709
  181.0 2.0 collective-permute-done.61
  185.8 2.0 collective-permute-start.66
  187.8 2.1 collective-permute-done.66
  190.0 2.2 %collective-permute-start.67 = (f32[24,512]{1,0:T(8,128)S(1)}, f32[24,512]{1,0:T(8,128)S(1)}, u32[]{:S(2)}, u32[]{:S(2)}) collective-permute-start(f32[24,512]{1,0:T(8,128)S(1)} %add.81), channel_id=1, source_target_pairs={{0,16},{8,24},{16,0},{24,8},{1,17},{9,25},{17,1},{25,9},{2,18},{10... | collective-permute-start | bytes 147464 | tf_op jit(solution)/shard_map/ppermute | solution.py:709
  193.3 1.8 collective-permute-done.67
  195.7 1.6 collective-permute-start.68
  198.5 1.6 last_step.1
  200.8 2.9 %put_in_place.3 = (f32[2,512,512]{2,1,0:T(8,128)}, f32[2,768,512]{2,1,0:T(8,128)}, f32[2,512,768]{2,1,0:T(8,128)}) custom-call(s32[10]{0:T(128)S(1)} %pad_add_fusion.place.here.refs_0_, f32[1024,512]{1,0:T(8,128)S(1)} %unfold_sides.5.refs_0_, f32[1024,512]{1,0:T(8,128)S(1)} %collective-permute-done.70.refs_1_), custom_call_target="tpu_custom_call" | custom-call | tf_op jit(solution)/shard_map/put_in_place/pallas_call | solution.py:654
  203.7 4.0 %collective-permute-done.68.refs_1_ = f32[512,256]{1,0:T(8,128)S(1)} collective-permute-done((f32[512,256]{1,0:T(8,128)S(1)}, f32[512,256]{1,0:T(8,128)S(1)}, u32[]{:S(2)}, u32[]{:S(2)}) %collective-permute-start.68) | collective-permute-done | bytes 524320 | tf_op jit(solution)/shard_map/ppermute | solution.py:709
  211.0 2.1 put_in_place.4
  213.9 2.1 put_in_place.5
  (175 shorter events, 77.2 us)
Async XLA Ops:
  4.2 5.7 %collective-permute-start.3 = (f32[4,512]{1,0:T(4,128)S(1)}, f32[4,512]{1,0:T(4,128)S(1)}, u32[]{:S(2)}, u32[]{:S(2)}) collective-permute-start(f32[4,512]{1,0:T(4,128)S(1)} %add.63), channel_id=1, source_target_pairs={{0,6},{1,7},{2,0},{3,1},{4,2},{5,3},{6,4},{7,5},{8,14},{9,15},{10,... | collective-permute-start | bytes 24584 | tf_op jit(solution)/shard_map/ppermute | solution.py:680
  8.5 4.5 %collective-permute-start.1 = (f32[4,512]{1,0:T(4,128)S(1)}, f32[4,512]{1,0:T(4,128)S(1)}, u32[]{:S(2)}, u32[]{:S(2)}) collective-permute-start(f32[4,512]{1,0:T(4,128)S(1)} %add.63), channel_id=1, source_target_pairs={{0,2},{1,3},{2,4},{3,5},{4,6},{5,7},{6,0},{7,1},{8,10},{9,11},{10,... | collective-permute-start | bytes 24584 | tf_op jit(solution)/shard_map/ppermute | solution.py:680
  13.1 5.7 %collective-permute-start.6 = (f32[4,512]{1,0:T(4,128)S(1)}, f32[4,512]{1,0:T(4,128)S(1)}, u32[]{:S(2)}, u32[]{:S(2)}) collective-permute-start(f32[4,512]{1,0:T(4,128)S(1)} %add_add_fusion.3.stats_0_), channel_id=1, source_target_pairs={{0,24},{8,0},{16,8},{24,16},{1,25},{9,1},{17,9},{25,17},{2,26},{10... | collective-permute-start | bytes 24584 | tf_op jit(solution)/shard_map/ppermute | solution.py:680
  16.7 4.5 %collective-permute-start.5 = (f32[4,512]{1,0:T(4,128)S(1)}, f32[4,512]{1,0:T(4,128)S(1)}, u32[]{:S(2)}, u32[]{:S(2)}) collective-permute-start(f32[4,512]{1,0:T(4,128)S(1)} %add_add_fusion.3.stats_0_), channel_id=1, source_target_pairs={{0,16},{8,24},{16,0},{24,8},{1,17},{9,25},{17,1},{25,9},{2,18},{10... | collective-permute-start | bytes 24584 | tf_op jit(solution)/shard_map/ppermute | solution.py:680
  16.7 5.4 %collective-permute-start.4 = (f32[4,512]{1,0:T(4,128)S(1)}, f32[4,512]{1,0:T(4,128)S(1)}, u32[]{:S(2)}, u32[]{:S(2)}) collective-permute-start(f32[4,512]{1,0:T(4,128)S(1)} %add_add_fusion.3.stats_0_), channel_id=1, source_target_pairs={{0,8},{8,16},{16,24},{24,0},{1,9},{9,17},{17,25},{25,1},{2,10},{10... | collective-permute-start | bytes 24584 | tf_op jit(solution)/shard_map/ppermute | solution.py:680
  27.0 4.6 %collective-permute-start.8 = (f32[4,768]{1,0:T(4,128)S(1)}, f32[4,768]{1,0:T(4,128)S(1)}, u32[]{:S(2)}, u32[]{:S(2)}) collective-permute-start(f32[4,768]{1,0:T(4,128)S(1)} %pad_maximum_fusion.1.ends_0_), channel_id=1, source_target_pairs={{0,2},{1,3},{2,4},{3,5},{4,6},{5,7},{6,0},{7,1},{8,10},{9,11},{10,... | collective-permute-start | bytes 36872 | tf_op jit(solution)/shard_map/ppermute | solution.py:680
  40.1 4.5 %collective-permute-start.12 = (f32[4,512]{1,0:T(4,128)S(1)}, f32[4,512]{1,0:T(4,128)S(1)}, u32[]{:S(2)}, u32[]{:S(2)}) collective-permute-start(f32[4,512]{1,0:T(4,128)S(1)} %add.69), channel_id=1, source_target_pairs={{0,2},{1,3},{2,4},{3,5},{4,6},{5,7},{6,0},{7,1},{8,10},{9,11},{10,... | collective-permute-start | bytes 24584 | tf_op jit(solution)/shard_map/ppermute | solution.py:680
  45.3 4.5 %collective-permute-start.16 = (f32[4,512]{1,0:T(4,128)S(1)}, f32[4,512]{1,0:T(4,128)S(1)}, u32[]{:S(2)}, u32[]{:S(2)}) collective-permute-start(f32[4,512]{1,0:T(4,128)S(1)} %add_add_fusion.2.stats_0_), channel_id=1, source_target_pairs={{0,16},{8,24},{16,0},{24,8},{1,17},{9,25},{17,1},{25,9},{2,18},{10... | collective-permute-start | bytes 24584 | tf_op jit(solution)/shard_map/ppermute | solution.py:680
  45.9 5.4 %collective-permute-start.15 = (f32[4,512]{1,0:T(4,128)S(1)}, f32[4,512]{1,0:T(4,128)S(1)}, u32[]{:S(2)}, u32[]{:S(2)}) collective-permute-start(f32[4,512]{1,0:T(4,128)S(1)} %add_add_fusion.2.stats_0_), channel_id=1, source_target_pairs={{0,8},{8,16},{16,24},{24,0},{1,9},{9,17},{17,25},{25,1},{2,10},{10... | collective-permute-start | bytes 24584 | tf_op jit(solution)/shard_map/ppermute | solution.py:680
  54.5 4.6 %collective-permute-start.21 = (f32[4,768]{1,0:T(4,128)S(1)}, f32[4,768]{1,0:T(4,128)S(1)}, u32[]{:S(2)}, u32[]{:S(2)}) collective-permute-start(f32[4,768]{1,0:T(4,128)S(1)} %pad_maximum_fusion.2.ends_0_), channel_id=1, source_target_pairs={{0,2},{1,3},{2,4},{3,5},{4,6},{5,7},{6,0},{7,1},{8,10},{9,11},{10,... | collective-permute-start | bytes 36872 | tf_op jit(solution)/shard_map/ppermute | solution.py:680
  54.6 4.6 %collective-permute-start.20 = (f32[4,768]{1,0:T(4,128)S(1)}, f32[4,768]{1,0:T(4,128)S(1)}, u32[]{:S(2)}, u32[]{:S(2)}) collective-permute-start(f32[4,768]{1,0:T(4,128)S(1)} %pad_maximum_fusion.2.ends_0_), channel_id=1, source_target_pairs={{0,4},{1,5},{2,6},{3,7},{4,0},{5,1},{6,2},{7,3},{8,12},{9,13},{10,... | collective-permute-start | bytes 36872 | tf_op jit(solution)/shard_map/ppermute | solution.py:680
  55.2 4.5 %collective-permute-start.19 = (f32[4,768]{1,0:T(4,128)S(1)}, f32[4,768]{1,0:T(4,128)S(1)}, u32[]{:S(2)}, u32[]{:S(2)}) collective-permute-start(f32[4,768]{1,0:T(4,128)S(1)} %pad_maximum_fusion.2.ends_0_), channel_id=1, source_target_pairs={{0,6},{1,7},{2,0},{3,1},{4,2},{5,3},{6,4},{7,5},{8,14},{9,15},{10,... | collective-permute-start | bytes 36872 | tf_op jit(solution)/shard_map/ppermute | solution.py:680
  66.9 4.7 %collective-permute-start.25 = (f32[4,768]{1,0:T(4,128)S(1)}, f32[4,768]{1,0:T(4,128)S(1)}, u32[]{:S(2)}, u32[]{:S(2)}) collective-permute-start(f32[4,768]{1,0:T(4,128)S(1)} %pad_maximum_fusion.3.ends_0_), channel_id=1, source_target_pairs={{0,6},{1,7},{2,0},{3,1},{4,2},{5,3},{6,4},{7,5},{8,14},{9,15},{10,... | collective-permute-start | bytes 36872 | tf_op jit(solution)/shard_map/ppermute | solution.py:680
  71.3 4.6 %collective-permute-start.23 = (f32[4,768]{1,0:T(4,128)S(1)}, f32[4,768]{1,0:T(4,128)S(1)}, u32[]{:S(2)}, u32[]{:S(2)}) collective-permute-start(f32[4,768]{1,0:T(4,128)S(1)} %pad_maximum_fusion.3.ends_0_), channel_id=1, source_target_pairs={{0,2},{1,3},{2,4},{3,5},{4,6},{5,7},{6,0},{7,1},{8,10},{9,11},{10,... | collective-permute-start | bytes 36872 | tf_op jit(solution)/shard_map/ppermute | solution.py:680
  80.6 5.7 %collective-permute-start.30 = (f32[1024,512]{1,0:T(8,128)S(1)}, f32[1024,512]{1,0:T(8,128)S(1)}, u32[]{:S(2)}, u32[]{:S(2)}) collective-permute-start(f32[1024,512]{1,0:T(8,128)S(1)} %get-tuple-element.273), channel_id=1, source_target_pairs={{0,1},{1,0},{2,3},{3,2},{4,5},{5,4},{6,7},{7,6},{8,9},{9,8},{10,11... | collective-permute-start | bytes 6291464 | tf_op jit(solution)/shard_map/ppermute | solution.py:709
  81.8 4.6 %collective-permute-start.27 = (f32[4,512]{1,0:T(4,128)S(1)}, f32[4,512]{1,0:T(4,128)S(1)}, u32[]{:S(2)}, u32[]{:S(2)}) collective-permute-start(f32[4,512]{1,0:T(4,128)S(1)} %add.73), channel_id=1, source_target_pairs={{0,2},{1,3},{2,4},{3,5},{4,6},{5,7},{6,0},{7,1},{8,10},{9,11},{10,... | collective-permute-start | bytes 24584 | tf_op jit(solution)/shard_map/ppermute | solution.py:680
  87.2 13.1 %collective-permute-start.31 = (f32[512,256]{1,0:T(8,128)S(1)}, f32[512,256]{1,0:T(8,128)S(1)}, u32[]{:S(2)}, u32[]{:S(2)}) collective-permute-start(f32[512,256]{1,0:T(8,128)S(1)} %get-tuple-element.279), channel_id=1, source_target_pairs={{0,2},{1,3},{2,0},{3,1},{4,6},{5,7},{6,4},{7,5},{8,10},{9,11},{10,... | collective-permute-start | bytes 1572872 | tf_op jit(solution)/shard_map/ppermute | solution.py:709
  88.3 12.0 %collective-permute-start.32 = (f32[512,256]{1,0:T(8,128)S(1)}, f32[512,256]{1,0:T(8,128)S(1)}, u32[]{:S(2)}, u32[]{:S(2)}) collective-permute-start(f32[512,256]{1,0:T(8,128)S(1)} %get-tuple-element.281), channel_id=1, source_target_pairs={{0,4},{1,5},{2,6},{3,7},{4,0},{5,1},{6,2},{7,3},{8,12},{9,13},{10,... | collective-permute-start | bytes 1572872 | tf_op jit(solution)/shard_map/ppermute | solution.py:709
  91.2 4.5 %collective-permute-start.34 = (f32[4,512]{1,0:T(4,128)S(1)}, f32[4,512]{1,0:T(4,128)S(1)}, u32[]{:S(2)}, u32[]{:S(2)}) collective-permute-start(f32[4,512]{1,0:T(4,128)S(1)} %add_add_fusion.1.stats_0_), channel_id=1, source_target_pairs={{0,16},{8,24},{16,0},{24,8},{1,17},{9,25},{17,1},{25,9},{2,18},{10... | collective-permute-start | bytes 24584 | tf_op jit(solution)/shard_map/ppermute | solution.py:680
  91.5 5.4 %collective-permute-start.33 = (f32[4,512]{1,0:T(4,128)S(1)}, f32[4,512]{1,0:T(4,128)S(1)}, u32[]{:S(2)}, u32[]{:S(2)}) collective-permute-start(f32[4,512]{1,0:T(4,128)S(1)} %add_add_fusion.1.stats_0_), channel_id=1, source_target_pairs={{0,8},{8,16},{16,24},{24,0},{1,9},{9,17},{17,25},{25,1},{2,10},{10... | collective-permute-start | bytes 24584 | tf_op jit(solution)/shard_map/ppermute | solution.py:680
  101.0 9.2 %collective-permute-start.36 = (f32[256,256]{1,0:T(8,128)S(1)}, f32[256,256]{1,0:T(8,128)S(1)}, u32[]{:S(2)}, u32[]{:S(2)}) collective-permute-start(f32[256,256]{1,0:T(8,128)S(1)} %get-tuple-element.299), channel_id=1, source_target_pairs={{0,4},{1,5},{2,6},{3,7},{4,0},{5,1},{6,2},{7,3},{8,12},{9,13},{10,... | collective-permute-start | bytes 786440 | tf_op jit(solution)/shard_map/ppermute | solution.py:709
  102.7 7.5 %collective-permute-start.37 = (f32[256,256]{1,0:T(8,128)S(1)}, f32[256,256]{1,0:T(8,128)S(1)}, u32[]{:S(2)}, u32[]{:S(2)}) collective-permute-start(f32[256,256]{1,0:T(8,128)S(1)} %get-tuple-element.301), channel_id=1, source_target_pairs={{0,2},{1,3},{2,0},{3,1},{4,6},{5,7},{6,4},{7,5},{8,10},{9,11},{10,... | collective-permute-start | bytes 786440 | tf_op jit(solution)/shard_map/ppermute | solution.py:709
  104.9 4.6 %collective-permute-start.41 = (f32[4,768]{1,0:T(4,128)S(1)}, f32[4,768]{1,0:T(4,128)S(1)}, u32[]{:S(2)}, u32[]{:S(2)}) collective-permute-start(f32[4,768]{1,0:T(4,128)S(1)} %pad_maximum_fusion.4.refs_1__0_), channel_id=1, source_target_pairs={{0,2},{1,3},{2,4},{3,5},{4,6},{5,7},{6,0},{7,1},{8,10},{9,11},{10,... | collective-permute-start | bytes 36872 | tf_op jit(solution)/shard_map/ppermute | solution.py:680
  112.3 8.7 %collective-permute-start.42 = (f32[128,512]{1,0:T(8,128)S(1)}, f32[128,512]{1,0:T(8,128)S(1)}, u32[]{:S(2)}, u32[]{:S(2)}) collective-permute-start(f32[128,512]{1,0:T(8,128)S(1)} %get-tuple-element.316), channel_id=1, source_target_pairs={{0,8},{8,0},{16,24},{24,16},{1,9},{9,1},{17,25},{25,17},{2,10},{10... | collective-permute-start | bytes 786440 | tf_op jit(solution)/shard_map/ppermute | solution.py:709
  122.2 4.5 %collective-permute-start.47 = (f32[384,512]{1,0:T(8,128)S(1)}, f32[384,512]{1,0:T(8,128)S(1)}, u32[]{:S(2)}, u32[]{:S(2)}) collective-permute-start(f32[384,512]{1,0:T(8,128)S(1)} %get-tuple-element.350), channel_id=1, source_target_pairs={{0,1},{1,0},{2,3},{3,2},{4,5},{5,4},{6,7},{7,6},{8,9},{9,8},{10,11... | collective-permute-start | bytes 2359304 | tf_op jit(solution)/shard_map/ppermute | solution.py:709
  122.3 18.2 %collective-permute-start.45 = (f32[320,256]{1,0:T(8,128)S(1)}, f32[320,256]{1,0:T(8,128)S(1)}, u32[]{:S(2)}, u32[]{:S(2)}) collective-permute-start(f32[320,256]{1,0:T(8,128)S(1)} %get-tuple-element.345), channel_id=1, source_target_pairs={{0,2},{1,3},{2,0},{3,1},{4,6},{5,7},{6,4},{7,5},{8,10},{9,11},{10,... | collective-permute-start | bytes 983048 | tf_op jit(solution)/shard_map/ppermute | solution.py:709
  125.2 15.3 %collective-permute-start.46 = (f32[320,256]{1,0:T(8,128)S(1)}, f32[320,256]{1,0:T(8,128)S(1)}, u32[]{:S(2)}, u32[]{:S(2)}) collective-permute-start(f32[320,256]{1,0:T(8,128)S(1)} %get-tuple-element.347), channel_id=1, source_target_pairs={{0,4},{1,5},{2,6},{3,7},{4,0},{5,1},{6,2},{7,3},{8,12},{9,13},{10,... | collective-permute-start | bytes 983048 | tf_op jit(solution)/shard_map/ppermute | solution.py:709
  126.1 14.4 %collective-permute-start.44 = (f32[128,512]{1,0:T(8,128)S(1)}, f32[128,512]{1,0:T(8,128)S(1)}, u32[]{:S(2)}, u32[]{:S(2)}) collective-permute-start(f32[128,512]{1,0:T(8,128)S(1)} %add_two.4.own), channel_id=1, source_target_pairs={{0,16},{8,24},{16,0},{24,8},{1,17},{9,25},{17,1},{25,9},{2,18},{10... | collective-permute-start | bytes 786440 | tf_op jit(solution)/shard_map/ppermute | solution.py:709
  127.4 13.2 %collective-permute-start.48 = (f32[192,256]{1,0:T(8,128)S(1)}, f32[192,256]{1,0:T(8,128)S(1)}, u32[]{:S(2)}, u32[]{:S(2)}) collective-permute-start(f32[192,256]{1,0:T(8,128)S(1)} %get-tuple-element.352), channel_id=1, source_target_pairs={{0,2},{1,3},{2,0},{3,1},{4,6},{5,7},{6,4},{7,5},{8,10},{9,11},{10,... | collective-permute-start | bytes 589832 | tf_op jit(solution)/shard_map/ppermute | solution.py:709
  128.2 12.4 %collective-permute-start.49 = (f32[192,256]{1,0:T(8,128)S(1)}, f32[192,256]{1,0:T(8,128)S(1)}, u32[]{:S(2)}, u32[]{:S(2)}) collective-permute-start(f32[192,256]{1,0:T(8,128)S(1)} %get-tuple-element.354), channel_id=1, source_target_pairs={{0,4},{1,5},{2,6},{3,7},{4,0},{5,1},{6,2},{7,3},{8,12},{9,13},{10,... | collective-permute-start | bytes 589832 | tf_op jit(solution)/shard_map/ppermute | solution.py:709
  140.6 8.3 %collective-permute-start.50 = (f32[128,512]{1,0:T(8,128)S(1)}, f32[128,512]{1,0:T(8,128)S(1)}, u32[]{:S(2)}, u32[]{:S(2)}) collective-permute-start(f32[128,512]{1,0:T(8,128)S(1)} %add_two.5.own), channel_id=1, source_target_pairs={{0,8},{8,0},{16,24},{24,16},{1,9},{9,1},{17,25},{25,17},{2,10},{10... | collective-permute-start | bytes 786440 | tf_op jit(solution)/shard_map/ppermute | solution.py:709
  141.3 8.3 %collective-permute-start.51 = (f32[256,256]{1,0:T(8,128)S(1)}, f32[256,256]{1,0:T(8,128)S(1)}, u32[]{:S(2)}, u32[]{:S(2)}) collective-permute-start(f32[256,256]{1,0:T(8,128)S(1)} %get-tuple-element.366), channel_id=1, source_target_pairs={{0,4},{1,5},{2,6},{3,7},{4,0},{5,1},{6,2},{7,3},{8,12},{9,13},{10,... | collective-permute-start | bytes 786440 | tf_op jit(solution)/shard_map/ppermute | solution.py:709
  142.5 7.9 %collective-permute-start.52 = (f32[256,256]{1,0:T(8,128)S(1)}, f32[256,256]{1,0:T(8,128)S(1)}, u32[]{:S(2)}, u32[]{:S(2)}) collective-permute-start(f32[256,256]{1,0:T(8,128)S(1)} %get-tuple-element.368), channel_id=1, source_target_pairs={{0,2},{1,3},{2,0},{3,1},{4,6},{5,7},{6,4},{7,5},{8,10},{9,11},{10,... | collective-permute-start | bytes 786440 | tf_op jit(solution)/shard_map/ppermute | solution.py:709
  151.1 7.1 %collective-permute-start.53 = (f32[256,256]{1,0:T(8,128)S(1)}, f32[256,256]{1,0:T(8,128)S(1)}, u32[]{:S(2)}, u32[]{:S(2)}) collective-permute-start(f32[256,256]{1,0:T(8,128)S(1)} %get-tuple-element.379.refs_0_), channel_id=1, source_target_pairs={{0,4},{1,5},{2,6},{3,7},{4,0},{5,1},{6,2},{7,3},{8,12},{9,13},{10,... | collective-permute-start | bytes 786440 | tf_op jit(solution)/shard_map/ppermute | solution.py:709
  152.0 6.8 %collective-permute-start.54 = (f32[256,256]{1,0:T(8,128)S(1)}, f32[256,256]{1,0:T(8,128)S(1)}, u32[]{:S(2)}, u32[]{:S(2)}) collective-permute-start(f32[256,256]{1,0:T(8,128)S(1)} %get-tuple-element.381.refs_2_), channel_id=1, source_target_pairs={{0,2},{1,3},{2,0},{3,1},{4,6},{5,7},{6,4},{7,5},{8,10},{9,11},{10,... | collective-permute-start | bytes 786440 | tf_op jit(solution)/shard_map/ppermute | solution.py:709
  152.9 6.6 %collective-permute-start.55 = (f32[128,512]{1,0:T(8,128)S(1)}, f32[128,512]{1,0:T(8,128)S(1)}, u32[]{:S(2)}, u32[]{:S(2)}) collective-permute-start(f32[128,512]{1,0:T(8,128)S(1)} %get-tuple-element.378), channel_id=1, source_target_pairs={{0,8},{8,0},{16,24},{24,16},{1,9},{9,1},{17,25},{25,17},{2,10},{10... | collective-permute-start | bytes 786440 | tf_op jit(solution)/shard_map/ppermute | solution.py:709
  160.1 14.6 %collective-permute-start.56 = (f32[512,256]{1,0:T(8,128)S(1)}, f32[512,256]{1,0:T(8,128)S(1)}, u32[]{:S(2)}, u32[]{:S(2)}) collective-permute-start(f32[512,256]{1,0:T(8,128)S(1)} %get-tuple-element.410.refs_0_), channel_id=1, source_target_pairs={{0,2},{1,3},{2,0},{3,1},{4,6},{5,7},{6,4},{7,5},{8,10},{9,11},{10,... | collective-permute-start | bytes 1572872 | tf_op jit(solution)/shard_map/ppermute | solution.py:709
  161.9 12.8 %collective-permute-start.57 = (f32[512,256]{1,0:T(8,128)S(1)}, f32[512,256]{1,0:T(8,128)S(1)}, u32[]{:S(2)}, u32[]{:S(2)}) collective-permute-start(f32[512,256]{1,0:T(8,128)S(1)} %get-tuple-element.412.refs_2_), channel_id=1, source_target_pairs={{0,4},{1,5},{2,6},{3,7},{4,0},{5,1},{6,2},{7,3},{8,12},{9,13},{10,... | collective-permute-start | bytes 1572872 | tf_op jit(solution)/shard_map/ppermute | solution.py:709
  163.1 11.6 %collective-permute-start.58 = (f32[128,512]{1,0:T(8,128)S(1)}, f32[128,512]{1,0:T(8,128)S(1)}, u32[]{:S(2)}, u32[]{:S(2)}) collective-permute-start(f32[128,512]{1,0:T(8,128)S(1)} %add_two.6.own), channel_id=1, source_target_pairs={{0,16},{8,24},{16,0},{24,8},{1,17},{9,25},{17,1},{25,9},{2,18},{10... | collective-permute-start | bytes 786440 | tf_op jit(solution)/shard_map/ppermute | solution.py:709
  174.8 8.3 %collective-permute-start.59 = (f32[128,512]{1,0:T(8,128)S(1)}, f32[128,512]{1,0:T(8,128)S(1)}, u32[]{:S(2)}, u32[]{:S(2)}) collective-permute-start(f32[128,512]{1,0:T(8,128)S(1)} %add_two.7.own), channel_id=1, source_target_pairs={{0,8},{8,0},{16,24},{24,16},{1,9},{9,1},{17,25},{25,17},{2,10},{10... | collective-permute-start | bytes 786440 | tf_op jit(solution)/shard_map/ppermute | solution.py:709
  178.0 5.0 %collective-permute-start.61 = (f32[24,512]{1,0:T(8,128)S(1)}, f32[24,512]{1,0:T(8,128)S(1)}, u32[]{:S(2)}, u32[]{:S(2)}) collective-permute-start(f32[24,512]{1,0:T(8,128)S(1)} %add.77), channel_id=1, source_target_pairs={{0,2},{1,3},{2,4},{3,5},{4,6},{5,7},{6,0},{7,1},{8,10},{9,11},{10,... | collective-permute-start | bytes 147464 | tf_op jit(solution)/shard_map/ppermute | solution.py:680
  184.3 16.5 %collective-permute-start.70 = (f32[1024,512]{1,0:T(8,128)S(1)}, f32[1024,512]{1,0:T(8,128)S(1)}, u32[]{:S(2)}, u32[]{:S(2)}) collective-permute-start(f32[1024,512]{1,0:T(8,128)S(1)} %unfold_sides.5.refs_0_), channel_id=1, source_target_pairs={{0,1},{1,0},{2,3},{3,2},{4,5},{5,4},{6,7},{7,6},{8,9},{9,8},{10,11... | collective-permute-start | bytes 6291464 | tf_op jit(solution)/shard_map/ppermute | solution.py:709
  184.4 10.7 %collective-permute-start.64 = (f32[256,256]{1,0:T(8,128)S(1)}, f32[256,256]{1,0:T(8,128)S(1)}, u32[]{:S(2)}, u32[]{:S(2)}) collective-permute-start(f32[256,256]{1,0:T(8,128)S(1)} %get-tuple-element.417.refs_0_), channel_id=1, source_target_pairs={{0,4},{1,5},{2,6},{3,7},{4,0},{5,1},{6,2},{7,3},{8,12},{9,13},{10,... | collective-permute-start | bytes 786440 | tf_op jit(solution)/shard_map/ppermute | solution.py:709
  185.3 9.7 %collective-permute-start.65 = (f32[256,256]{1,0:T(8,128)S(1)}, f32[256,256]{1,0:T(8,128)S(1)}, u32[]{:S(2)}, u32[]{:S(2)}) collective-permute-start(f32[256,256]{1,0:T(8,128)S(1)} %get-tuple-element.419.refs_2_), channel_id=1, source_target_pairs={{0,2},{1,3},{2,0},{3,1},{4,6},{5,7},{6,4},{7,5},{8,10},{9,11},{10,... | collective-permute-start | bytes 786440 | tf_op jit(solution)/shard_map/ppermute | solution.py:709
  190.0 5.1 %collective-permute-start.67 = (f32[24,512]{1,0:T(8,128)S(1)}, f32[24,512]{1,0:T(8,128)S(1)}, u32[]{:S(2)}, u32[]{:S(2)}) collective-permute-start(f32[24,512]{1,0:T(8,128)S(1)} %add.81), channel_id=1, source_target_pairs={{0,16},{8,24},{16,0},{24,8},{1,17},{9,25},{17,1},{25,9},{2,18},{10... | collective-permute-start | bytes 147464 | tf_op jit(solution)/shard_map/ppermute | solution.py:709
  195.7 12.0 %collective-permute-start.68 = (f32[512,256]{1,0:T(8,128)S(1)}, f32[512,256]{1,0:T(8,128)S(1)}, u32[]{:S(2)}, u32[]{:S(2)}) collective-permute-start(f32[512,256]{1,0:T(8,128)S(1)} %get-tuple-element.442.refs_0_), channel_id=1, source_target_pairs={{0,2},{1,3},{2,0},{3,1},{4,6},{5,7},{6,4},{7,5},{8,10},{9,11},{10,... | collective-permute-start | bytes 1572872 | tf_op jit(solution)/shard_map/ppermute | solution.py:709
  197.3 11.6 %collective-permute-start.69 = (f32[512,256]{1,0:T(8,128)S(1)}, f32[512,256]{1,0:T(8,128)S(1)}, u32[]{:S(2)}, u32[]{:S(2)}) collective-permute-start(f32[512,256]{1,0:T(8,128)S(1)} %get-tuple-element.444.refs_2_), channel_id=1, source_target_pairs={{0,4},{1,5},{2,6},{3,7},{4,0},{5,1},{6,2},{7,3},{8,12},{9,13},{10,... | collective-permute-start | bytes 1572872 | tf_op jit(solution)/shard_map/ppermute | solution.py:709
  209.7 4.2 %collective-permute-start.71 = (f32[1024,512]{1,0:T(8,128)S(1)}, f32[1024,512]{1,0:T(8,128)S(1)}, u32[]{:S(2)}, u32[]{:S(2)}) collective-permute-start(f32[1024,512]{1,0:T(8,128)S(1)} %unfold_sides.7.refs_0_), channel_id=1, source_target_pairs={{0,1},{1,0},{2,3},{3,2},{4,5},{5,4},{6,7},{7,6},{8,9},{9,8},{10,11... | collective-permute-start | bytes 6291464 | tf_op jit(solution)/shard_map/ppermute | solution.py:709
  (33 other events, 184.1 us)

commit v3 on v2

--- a/solution.py
+++ b/solution.py
@@ -1,3 +1,4 @@
+import copy
 import functools
 
 import jax
@@ -1132,20 +1133,29 @@
     small_sum = summed[CHUNKS:].reshape(2, CHUNKS, width)
     _, pullback = jax.vjp(discretize, lam_re, lam_im, log_step)
     grad_lr, grad_li, grad_ls = pullback(tuple(small_sum[:, kind, :half] for kind in range(4)))
-    grad_input, grad_lr, grad_li, grad_ls, *placed = wait_for(
-        lower_sum, grad_input, grad_lr, grad_li, grad_ls, *placed
-    )
-
+    both = jnp.stack([shared0, shared1])
+    grad_gain, grad_shift = both[:, 0], both[:, 1]
+    early = [swap(lower_sum.parts[at], "seq", 1) for at in (0, 2)]
+    grad_skip = small_sum[:, 4]
+    grad_input, grad_lr, grad_li, grad_ls, grad_gain, grad_shift, grad_skip, *rest = wait_for(
+        lower_sum, grad_input, grad_lr, grad_li, grad_ls, grad_gain, grad_shift, grad_skip,
+        *early, *placed,
+    )
+    early, placed = rest[:2], rest[2:]
+
+    late = [swap(lower_sum.parts[at], "seq", 1) for at in (1, 3)]
+    other_sum = copy.copy(lower_sum)
+    other_sum.parts = (early[0], late[0], early[1], late[1])
     lower_sum.up_plane(0)
-    own0 = lower_sum.parts[0]
-    other0 = swap(own0, "seq", 1)
-    placed = put_in_place(0, here, ((False, own0),), final, placed, 4)
-    grad_w, grad_c, grad_b = put_in_place(0, here, ((True, other0),), final, placed, 4)
-    both = jnp.stack([shared0, shared1])
+    placed = put_in_place(0, here, ((False, lower_sum.parts[0]),), final, placed, 4)
+    other_sum.up_plane(0)
+    grad_w, grad_c, grad_b = put_in_place(
+        0, here, ((True, other_sum.parts[0]),), final, placed, 4
+    )
     shape = block_in.shape
     return (
-        block_out.reshape(shape), grad_input.reshape(shape), both[:, 0], both[:, 1],
-        grad_ls, grad_lr, grad_li, grad_b, grad_c, small_sum[:, 4], grad_w,
+        block_out.reshape(shape), grad_input.reshape(shape), grad_gain, grad_shift,
+        grad_ls, grad_lr, grad_li, grad_b, grad_c, grad_skip, grad_w,
     )
 
 

time: 216 us -> 215 us (level)
  waiting for transfers between devices: 92.2 us -> 89.7 us
    ppermute x37 -> x40, waiting for transfers between devices: 54.5 us -> 52 us  [swap(): lax.ppermute(value, axis, [(i, i ^ bit) for i in range(lax.axis_size(axis...]
    ppermute x37 -> x40, starting transfers between devices: 30.8 us -> 31.7 us  [swap(): lax.ppermute(value, axis, [(i, i ^ bit) for i in range(lax.axis_size(axis...]
    pallas_call x32 -> x33, Pallas kernels: 38.9 us -> 39.6 us  [run(): pl.pallas_call(body, name=name, out_shape=tuple((jax.ShapeDtypeStruct(*ou...]
  transfers between devices with their start and end apart: 72 -> 75, of which waited for: 50 -> 49; matrix products, arithmetic and copies ran while one was open for 2% -> 2% of each run, Pallas kernels for 9% -> 9%
where the time goes in v3:
time: 215 us
  waiting for transfers between devices  89.7 us (42%)
  starting transfers between devices  70.8 us (33%)
  Pallas kernels  46.6 us (22%)
  local copies, waits for them, and re-layouts  4.39 us (2%)
  other arithmetic  2.39 us (1%)
    ppermute x40, waiting for transfers between devices, swap(): lax.ppermute(value, axis, [(i, i ^ bit) for i in range(lax.axis_size(axis...  52 us
    pallas_call x33, Pallas kernels, run(): pl.pallas_call(body, name=name, out_shape=tuple((jax.ShapeDtypeStruct(*ou...  39.6 us
    ppermute x35, starting transfers between devices, shifted(): return lax.ppermute(value, name, pairs)  39.1 us
    ppermute x35, waiting for transfers between devices, shifted(): return lax.ppermute(value, name, pairs)  37.7 us
    ppermute x40, starting transfers between devices, swap(): lax.ppermute(value, axis, [(i, i ^ bit) for i in range(lax.axis_size(axis...  31.7 us
    pallas_call x3, Pallas kernels, put_in_place(): pl.pallas_call(body, name='put_in_place', out_shape=tuple((jax.ShapeDtype...  7.07 us
  transfers between devices with their start and end apart: 75, of which 49 were waited for; matrix products, arithmetic and copies ran while one was open for 2% of the time, Pallas kernels for 9%

profile of v3, /device:TPU:0, one launch (start us, length us, event | category | flops | bytes accessed | tf_op | source)
XLA Modules:
  0.0 215.1 jit_solution(13343767614733745611)
XLA Ops:
  4.2 3.8 %collective-permute-start.3 = (f32[4,512]{1,0:T(4,128)S(1)}, f32[4,512]{1,0:T(4,128)S(1)}, u32[]{:S(2)}, u32[]{:S(2)}) collective-permute-start(f32[4,512]{1,0:T(4,128)S(1)} %add.63), channel_id=1, source_target_pairs={{0,6},{1,7},{2,0},{3,1},{4,2},{5,3},{6,4},{7,5},{8,14},{9,15},{10,... | collective-permute-start | bytes 24584 | tf_op jit(solution)/shard_map/ppermute | solution.py:681
  9.9 1.8 collective-permute-done.2
  13.1 3.6 %collective-permute-start.6 = (f32[4,512]{1,0:T(4,128)S(1)}, f32[4,512]{1,0:T(4,128)S(1)}, u32[]{:S(2)}, u32[]{:S(2)}) collective-permute-start(f32[4,512]{1,0:T(4,128)S(1)} %add_add_fusion.3.stats_0_), channel_id=1, source_target_pairs={{0,24},{8,0},{16,8},{24,16},{1,25},{9,1},{17,9},{25,17},{2,26},{10... | collective-permute-start | bytes 24584 | tf_op jit(solution)/shard_map/ppermute | solution.py:681
  18.7 2.5 %collective-permute-done.5.stats_2_ = f32[4,512]{1,0:T(4,128)S(1)} collective-permute-done((f32[4,512]{1,0:T(4,128)S(1)}, f32[4,512]{1,0:T(4,128)S(1)}, u32[]{:S(2)}, u32[]{:S(2)}) %collective-permute-start.5) | collective-permute-done | bytes 8224 | tf_op jit(solution)/shard_map/ppermute | solution.py:681
  22.1 1.9 enter_layer.2
  25.4 1.5 collective-permute-start.9
  27.0 1.9 collective-permute-start.8
  29.1 2.4 %collective-permute-done.8.ends_1_ = f32[4,768]{1,0:T(4,128)S(1)} collective-permute-done((f32[4,768]{1,0:T(4,128)S(1)}, f32[4,768]{1,0:T(4,128)S(1)}, u32[]{:S(2)}, u32[]{:S(2)}) %collective-permute-start.8) | collective-permute-done | bytes 12320 | tf_op jit(solution)/shard_map/ppermute | solution.py:681
  32.8 3.6 %middle_forward.1 = (f32[528,768]{1,0:T(8,128)S(1)}, bf16[512,768]{1,0:T(8,128)(2,1)S(1)}, bf16[512,512]{1,0:T(8,128)(2,1)S(1)}, f32[512,512]{1,0:T(8,128)S(1)},...) custom-call(s32[10]{0:T(128)S(1)} %pad_add_fusion.place.here.refs_0_, ...), custom_call_target="tpu_custom_call" | custom-call | tf_op jit(solution)/shard_map/middle_forward/pallas_call | solution.py:609
  42.3 2.4 %collective-permute-done.12 = f32[4,512]{1,0:T(4,128)S(1)} collective-permute-done((f32[4,512]{1,0:T(4,128)S(1)}, f32[4,512]{1,0:T(4,128)S(1)}, u32[]{:S(2)}, u32[]{:S(2)}) %collective-permute-start.12) | collective-permute-done | bytes 8224 | tf_op jit(solution)/shard_map/ppermute | solution.py:681
  45.9 2.0 collective-permute-start.15
  49.8 1.5 collective-permute-done.15.stats_1_
  51.4 1.9 enter_layer.3
  55.2 2.8 %collective-permute-start.19 = (f32[4,768]{1,0:T(4,128)S(1)}, f32[4,768]{1,0:T(4,128)S(1)}, u32[]{:S(2)}, u32[]{:S(2)}) collective-permute-start(f32[4,768]{1,0:T(4,128)S(1)} %pad_maximum_fusion.2.ends_0_), channel_id=1, source_target_pairs={{0,6},{1,7},{2,0},{3,1},{4,2},{5,3},{6,4},{7,5},{8,14},{9,15},{10,... | collective-permute-start | bytes 36872 | tf_op jit(solution)/shard_map/ppermute | solution.py:681
  59.7 5.9 %turn_around.1 = (bf16[512,512]{1,0:T(8,128)(2,1)S(1)}, f32[528,768]{1,0:T(8,128)S(1)}, bf16[512,768]{1,0:T(8,128)(2,1)S(1)}, bf16[512,512]{1,0:T(8,128)(2,1)S(1...) custom-call(s32[10]{0:T(128)S(1)} %pad_add_fusion.place.here.refs_0_, ...), custom_call_target="tpu_custom_call" | custom-call | tf_op jit(solution)/shard_map/turn_around/pallas_call | solution.py:609
  66.9 2.9 %collective-permute-start.25 = (f32[4,768]{1,0:T(4,128)S(1)}, f32[4,768]{1,0:T(4,128)S(1)}, u32[]{:S(2)}, u32[]{:S(2)}) collective-permute-start(f32[4,768]{1,0:T(4,128)S(1)} %pad_maximum_fusion.3.ends_0_), channel_id=1, source_target_pairs={{0,6},{1,7},{2,0},{3,1},{4,2},{5,3},{6,4},{7,5},{8,14},{9,15},{10,... | collective-permute-start | bytes 36872 | tf_op jit(solution)/shard_map/ppermute | solution.py:681
  69.8 1.5 collective-permute-start.24
  71.5 2.0 collective-permute-done.24.ends_2_
  73.5 2.4 %collective-permute-done.23.ends_1_ = f32[4,768]{1,0:T(4,128)S(1)} collective-permute-done((f32[4,768]{1,0:T(4,128)S(1)}, f32[4,768]{1,0:T(4,128)S(1)}, u32[]{:S(2)}, u32[]{:S(2)}) %collective-permute-start.23) | collective-permute-done | bytes 12320 | tf_op jit(solution)/shard_map/ppermute | solution.py:681
  75.9 2.8 %backward_finish.2 = (bf16[512,768]{1,0:T(8,128)(2,1)S(1)}, f32[512,512]{1,0:T(8,128)S(1)}, f32[4,512]{1,0:T(4,128)S(1)}, f32[8,512]{1,0:T(8,128)S(1)}) custom-call(s32[10]{0:T(128)S(1)} %pad_add_fusion.place.here.refs_0_, f32[4,768]{1,0:T(4,128)S(1)} %pad_maximum_fusion.3.ends_0_, f32[4,768]{1,0:T(4,128)S(1)} %collective-permute-done.23.ends_1_, ...), custom_call_target="tpu_custom_call" | custom-call | tf_op jit(solution)/shard_map/backward_finish/pallas_call | solution.py:609
  78.8 1.8 all_weights.1
  81.8 2.0 collective-permute-start.27
  88.3 1.5 collective-permute-start.32
  93.5 2.2 %collective-permute-done.34.stats_2_ = f32[4,512]{1,0:T(4,128)S(1)} collective-permute-done((f32[4,512]{1,0:T(4,128)S(1)}, f32[4,512]{1,0:T(4,128)S(1)}, u32[]{:S(2)}, u32[]{:S(2)}) %collective-permute-start.34) | collective-permute-done | bytes 8224 | tf_op jit(solution)/shard_map/ppermute | solution.py:681
  96.9 3.3 %between_layers.1 = (f32[512,512]{1,0:T(8,128)S(1)}, f32[2,512]{1,0:T(2,128)S(1)}, bf16[512,512]{1,0:T(8,128)(2,1)S(1)}, f32[512,512]{1,0:T(8,128)S(1)}, bf16[51...) custom-call(s32[10]{0:T(128)S(1)} %pad_add_fusion.place.here.refs_0_, ...), custom_call_target="tpu_custom_call" | custom-call | tf_op jit(solution)/shard_map/between_layers/pallas_call | solution.py:609
  101.0 1.8 collective-permute-start.36
  106.3 2.5 %collective-permute-start.39 = (f32[4,768]{1,0:T(4,128)S(1)}, f32[4,768]{1,0:T(4,128)S(1)}, u32[]{:S(2)}, u32[]{:S(2)}) collective-permute-start(f32[4,768]{1,0:T(4,128)S(1)} %pad_maximum_fusion.4.refs_1__0_), channel_id=1, source_target_pairs={{0,6},{1,7},{2,0},{3,1},{4,2},{5,3},{6,4},{7,5},{8,14},{9,15},{10,... | collective-permute-start | bytes 36872 | tf_op jit(solution)/shard_map/ppermute | solution.py:681
  112.5 2.8 %backward_finish.3 = (bf16[512,768]{1,0:T(8,128)(2,1)S(1)}, f32[512,512]{1,0:T(8,128)S(1)}, f32[24,512]{1,0:T(8,128)S(1)}) custom-call(s32[10]{0:T(128)S(1)} %pad_add_fusion.place.here.refs_0_, f32[4,768]{1,0:T(4,128)S(1)} %pad_maximum_fusion.4.refs_1__0_, f32[4,768]{1,0:T(4,128)S(1)} %collective-permute-done.39.refs_1__1_, ...), custom_call_target="tpu_custom_call" | custom-call | tf_op jit(solution)/shard_map/backward_finish/pallas_call | solution.py:609
  116.1 4.9 %collective-permute-done.42.found = f32[128,512]{1,0:T(8,128)S(1)} collective-permute-done((f32[128,512]{1,0:T(8,128)S(1)}, f32[128,512]{1,0:T(8,128)S(1)}, u32[]{:S(2)}, u32[]{:S(2)}) %collective-permute-start.42) | collective-permute-done | bytes 262176 | tf_op jit(solution)/shard_map/ppermute | solution.py:710
  122.3 2.9 %collective-permute-start.45 = (f32[320,256]{1,0:T(8,128)S(1)}, f32[320,256]{1,0:T(8,128)S(1)}, u32[]{:S(2)}, u32[]{:S(2)}) collective-permute-start(f32[320,256]{1,0:T(8,128)S(1)} %get-tuple-element.350), channel_id=1, source_target_pairs={{0,2},{1,3},{2,0},{3,1},{4,6},{5,7},{6,4},{7,5},{8,10},{9,11},{10,... | collective-permute-start | bytes 983048 | tf_op jit(solution)/shard_map/ppermute | solution.py:710
  129.0 11.5 %collective-permute-done.44.found = f32[128,512]{1,0:T(8,128)S(1)} collective-permute-done((f32[128,512]{1,0:T(8,128)S(1)}, f32[128,512]{1,0:T(8,128)S(1)}, u32[]{:S(2)}, u32[]{:S(2)}) %collective-permute-start.44) | collective-permute-done | bytes 262176 | tf_op jit(solution)/shard_map/ppermute | solution.py:710
  142.8 6.1 %collective-permute-done.50.found = f32[128,512]{1,0:T(8,128)S(1)} collective-permute-done((f32[128,512]{1,0:T(8,128)S(1)}, f32[128,512]{1,0:T(8,128)S(1)}, u32[]{:S(2)}, u32[]{:S(2)}) %collective-permute-start.50) | collective-permute-done | bytes 262176 | tf_op jit(solution)/shard_map/ppermute | solution.py:710
  152.9 1.8 collective-permute-start.55
  154.7 3.5 %collective-permute-done.53.refs_1_ = f32[256,256]{1,0:T(8,128)S(1)} collective-permute-done((f32[256,256]{1,0:T(8,128)S(1)}, f32[256,256]{1,0:T(8,128)S(1)}, u32[]{:S(2)}, u32[]{:S(2)}) %collective-permute-start.53) | collective-permute-done | bytes 262176 | tf_op jit(solution)/shard_map/ppermute | solution.py:710
  160.1 1.8 collective-permute-start.56
  163.1 1.9 collective-permute-start.58
  165.0 9.7 %collective-permute-done.58.found = f32[128,512]{1,0:T(8,128)S(1)} collective-permute-done((f32[128,512]{1,0:T(8,128)S(1)}, f32[128,512]{1,0:T(8,128)S(1)}, u32[]{:S(2)}, u32[]{:S(2)}) %collective-permute-start.58) | collective-permute-done | bytes 262176 | tf_op jit(solution)/shard_map/ppermute | solution.py:710
  181.0 2.0 collective-permute-done.61
  185.8 2.0 collective-permute-start.66
  187.8 2.1 collective-permute-done.66
  190.0 2.2 %collective-permute-start.67 = (f32[24,512]{1,0:T(8,128)S(1)}, f32[24,512]{1,0:T(8,128)S(1)}, u32[]{:S(2)}, u32[]{:S(2)}) collective-permute-start(f32[24,512]{1,0:T(8,128)S(1)} %add.81), channel_id=1, source_target_pairs={{0,16},{8,24},{16,0},{24,8},{1,17},{9,25},{17,1},{25,9},{2,18},{10... | collective-permute-start | bytes 147464 | tf_op jit(solution)/shard_map/ppermute | solution.py:710
  193.3 1.8 collective-permute-done.67
  195.7 1.6 collective-permute-start.68
  199.0 1.6 last_step.1
  202.5 2.9 %put_in_place.3 = (f32[2,512,512]{2,1,0:T(8,128)}, f32[2,768,512]{2,1,0:T(8,128)}, f32[2,512,768]{2,1,0:T(8,128)}) custom-call(s32[10]{0:T(128)S(1)} %pad_add_fusion.place.here.refs_0_, f32[1024,512]{1,0:T(8,128)S(1)} %unfold_sides.6.refs_0_, f32[1024,512]{1,0:T(8,128)S(1)} %collective-permute-done.72.refs_1_), custom_call_target="tpu_custom_call" | custom-call | tf_op jit(solution)/shard_map/put_in_place/pallas_call | solution.py:655
  205.4 2.3 %collective-permute-done.68.refs_1_ = f32[512,256]{1,0:T(8,128)S(1)} collective-permute-done((f32[512,256]{1,0:T(8,128)S(1)}, f32[512,256]{1,0:T(8,128)S(1)}, u32[]{:S(2)}, u32[]{:S(2)}) %collective-permute-start.68) | collective-permute-done | bytes 524320 | tf_op jit(solution)/shard_map/ppermute | solution.py:710
  210.2 2.1 put_in_place.4
  213.0 2.1 put_in_place.5
  (182 shorter events, 78.0 us)
Async XLA Ops:
  4.2 5.7 %collective-permute-start.3 = (f32[4,512]{1,0:T(4,128)S(1)}, f32[4,512]{1,0:T(4,128)S(1)}, u32[]{:S(2)}, u32[]{:S(2)}) collective-permute-start(f32[4,512]{1,0:T(4,128)S(1)} %add.63), channel_id=1, source_target_pairs={{0,6},{1,7},{2,0},{3,1},{4,2},{5,3},{6,4},{7,5},{8,14},{9,15},{10,... | collective-permute-start | bytes 24584 | tf_op jit(solution)/shard_map/ppermute | solution.py:681
  8.5 4.5 %collective-permute-start.1 = (f32[4,512]{1,0:T(4,128)S(1)}, f32[4,512]{1,0:T(4,128)S(1)}, u32[]{:S(2)}, u32[]{:S(2)}) collective-permute-start(f32[4,512]{1,0:T(4,128)S(1)} %add.63), channel_id=1, source_target_pairs={{0,2},{1,3},{2,4},{3,5},{4,6},{5,7},{6,0},{7,1},{8,10},{9,11},{10,... | collective-permute-start | bytes 24584 | tf_op jit(solution)/shard_map/ppermute | solution.py:681
  13.1 5.7 %collective-permute-start.6 = (f32[4,512]{1,0:T(4,128)S(1)}, f32[4,512]{1,0:T(4,128)S(1)}, u32[]{:S(2)}, u32[]{:S(2)}) collective-permute-start(f32[4,512]{1,0:T(4,128)S(1)} %add_add_fusion.3.stats_0_), channel_id=1, source_target_pairs={{0,24},{8,0},{16,8},{24,16},{1,25},{9,1},{17,9},{25,17},{2,26},{10... | collective-permute-start | bytes 24584 | tf_op jit(solution)/shard_map/ppermute | solution.py:681
  16.7 4.5 %collective-permute-start.5 = (f32[4,512]{1,0:T(4,128)S(1)}, f32[4,512]{1,0:T(4,128)S(1)}, u32[]{:S(2)}, u32[]{:S(2)}) collective-permute-start(f32[4,512]{1,0:T(4,128)S(1)} %add_add_fusion.3.stats_0_), channel_id=1, source_target_pairs={{0,16},{8,24},{16,0},{24,8},{1,17},{9,25},{17,1},{25,9},{2,18},{10... | collective-permute-start | bytes 24584 | tf_op jit(solution)/shard_map/ppermute | solution.py:681
  16.7 5.4 %collective-permute-start.4 = (f32[4,512]{1,0:T(4,128)S(1)}, f32[4,512]{1,0:T(4,128)S(1)}, u32[]{:S(2)}, u32[]{:S(2)}) collective-permute-start(f32[4,512]{1,0:T(4,128)S(1)} %add_add_fusion.3.stats_0_), channel_id=1, source_target_pairs={{0,8},{8,16},{16,24},{24,0},{1,9},{9,17},{17,25},{25,1},{2,10},{10... | collective-permute-start | bytes 24584 | tf_op jit(solution)/shard_map/ppermute | solution.py:681
  27.0 4.6 %collective-permute-start.8 = (f32[4,768]{1,0:T(4,128)S(1)}, f32[4,768]{1,0:T(4,128)S(1)}, u32[]{:S(2)}, u32[]{:S(2)}) collective-permute-start(f32[4,768]{1,0:T(4,128)S(1)} %pad_maximum_fusion.1.ends_0_), channel_id=1, source_target_pairs={{0,2},{1,3},{2,4},{3,5},{4,6},{5,7},{6,0},{7,1},{8,10},{9,11},{10,... | collective-permute-start | bytes 36872 | tf_op jit(solution)/shard_map/ppermute | solution.py:681
  40.1 4.5 %collective-permute-start.12 = (f32[4,512]{1,0:T(4,128)S(1)}, f32[4,512]{1,0:T(4,128)S(1)}, u32[]{:S(2)}, u32[]{:S(2)}) collective-permute-start(f32[4,512]{1,0:T(4,128)S(1)} %add.69), channel_id=1, source_target_pairs={{0,2},{1,3},{2,4},{3,5},{4,6},{5,7},{6,0},{7,1},{8,10},{9,11},{10,... | collective-permute-start | bytes 24584 | tf_op jit(solution)/shard_map/ppermute | solution.py:681
  45.3 4.5 %collective-permute-start.16 = (f32[4,512]{1,0:T(4,128)S(1)}, f32[4,512]{1,0:T(4,128)S(1)}, u32[]{:S(2)}, u32[]{:S(2)}) collective-permute-start(f32[4,512]{1,0:T(4,128)S(1)} %add_add_fusion.2.stats_0_), channel_id=1, source_target_pairs={{0,16},{8,24},{16,0},{24,8},{1,17},{9,25},{17,1},{25,9},{2,18},{10... | collective-permute-start | bytes 24584 | tf_op jit(solution)/shard_map/ppermute | solution.py:681
  45.9 5.4 %collective-permute-start.15 = (f32[4,512]{1,0:T(4,128)S(1)}, f32[4,512]{1,0:T(4,128)S(1)}, u32[]{:S(2)}, u32[]{:S(2)}) collective-permute-start(f32[4,512]{1,0:T(4,128)S(1)} %add_add_fusion.2.stats_0_), channel_id=1, source_target_pairs={{0,8},{8,16},{16,24},{24,0},{1,9},{9,17},{17,25},{25,1},{2,10},{10... | collective-permute-start | bytes 24584 | tf_op jit(solution)/shard_map/ppermute | solution.py:681
  54.5 4.6 %collective-permute-start.21 = (f32[4,768]{1,0:T(4,128)S(1)}, f32[4,768]{1,0:T(4,128)S(1)}, u32[]{:S(2)}, u32[]{:S(2)}) collective-permute-start(f32[4,768]{1,0:T(4,128)S(1)} %pad_maximum_fusion.2.ends_0_), channel_id=1, source_target_pairs={{0,2},{1,3},{2,4},{3,5},{4,6},{5,7},{6,0},{7,1},{8,10},{9,11},{10,... | collective-permute-start | bytes 36872 | tf_op jit(solution)/shard_map/ppermute | solution.py:681
  54.6 4.6 %collective-permute-start.20 = (f32[4,768]{1,0:T(4,128)S(1)}, f32[4,768]{1,0:T(4,128)S(1)}, u32[]{:S(2)}, u32[]{:S(2)}) collective-permute-start(f32[4,768]{1,0:T(4,128)S(1)} %pad_maximum_fusion.2.ends_0_), channel_id=1, source_target_pairs={{0,4},{1,5},{2,6},{3,7},{4,0},{5,1},{6,2},{7,3},{8,12},{9,13},{10,... | collective-permute-start | bytes 36872 | tf_op jit(solution)/shard_map/ppermute | solution.py:681
  55.2 4.5 %collective-permute-start.19 = (f32[4,768]{1,0:T(4,128)S(1)}, f32[4,768]{1,0:T(4,128)S(1)}, u32[]{:S(2)}, u32[]{:S(2)}) collective-permute-start(f32[4,768]{1,0:T(4,128)S(1)} %pad_maximum_fusion.2.ends_0_), channel_id=1, source_target_pairs={{0,6},{1,7},{2,0},{3,1},{4,2},{5,3},{6,4},{7,5},{8,14},{9,15},{10,... | collective-permute-start | bytes 36872 | tf_op jit(solution)/shard_map/ppermute | solution.py:681
  66.9 4.7 %collective-permute-start.25 = (f32[4,768]{1,0:T(4,128)S(1)}, f32[4,768]{1,0:T(4,128)S(1)}, u32[]{:S(2)}, u32[]{:S(2)}) collective-permute-start(f32[4,768]{1,0:T(4,128)S(1)} %pad_maximum_fusion.3.ends_0_), channel_id=1, source_target_pairs={{0,6},{1,7},{2,0},{3,1},{4,2},{5,3},{6,4},{7,5},{8,14},{9,15},{10,... | collective-permute-start | bytes 36872 | tf_op jit(solution)/shard_map/ppermute | solution.py:681
  71.3 4.6 %collective-permute-start.23 = (f32[4,768]{1,0:T(4,128)S(1)}, f32[4,768]{1,0:T(4,128)S(1)}, u32[]{:S(2)}, u32[]{:S(2)}) collective-permute-start(f32[4,768]{1,0:T(4,128)S(1)} %pad_maximum_fusion.3.ends_0_), channel_id=1, source_target_pairs={{0,2},{1,3},{2,4},{3,5},{4,6},{5,7},{6,0},{7,1},{8,10},{9,11},{10,... | collective-permute-start | bytes 36872 | tf_op jit(solution)/shard_map/ppermute | solution.py:681
  80.6 5.7 %collective-permute-start.30 = (f32[1024,512]{1,0:T(8,128)S(1)}, f32[1024,512]{1,0:T(8,128)S(1)}, u32[]{:S(2)}, u32[]{:S(2)}) collective-permute-start(f32[1024,512]{1,0:T(8,128)S(1)} %get-tuple-element.278), channel_id=1, source_target_pairs={{0,1},{1,0},{2,3},{3,2},{4,5},{5,4},{6,7},{7,6},{8,9},{9,8},{10,11... | collective-permute-start | bytes 6291464 | tf_op jit(solution)/shard_map/ppermute | solution.py:710
  81.8 4.6 %collective-permute-start.27 = (f32[4,512]{1,0:T(4,128)S(1)}, f32[4,512]{1,0:T(4,128)S(1)}, u32[]{:S(2)}, u32[]{:S(2)}) collective-permute-start(f32[4,512]{1,0:T(4,128)S(1)} %add.73), channel_id=1, source_target_pairs={{0,2},{1,3},{2,4},{3,5},{4,6},{5,7},{6,0},{7,1},{8,10},{9,11},{10,... | collective-permute-start | bytes 24584 | tf_op jit(solution)/shard_map/ppermute | solution.py:681
  87.2 13.1 %collective-permute-start.31 = (f32[512,256]{1,0:T(8,128)S(1)}, f32[512,256]{1,0:T(8,128)S(1)}, u32[]{:S(2)}, u32[]{:S(2)}) collective-permute-start(f32[512,256]{1,0:T(8,128)S(1)} %get-tuple-element.284), channel_id=1, source_target_pairs={{0,2},{1,3},{2,0},{3,1},{4,6},{5,7},{6,4},{7,5},{8,10},{9,11},{10,... | collective-permute-start | bytes 1572872 | tf_op jit(solution)/shard_map/ppermute | solution.py:710
  88.3 12.0 %collective-permute-start.32 = (f32[512,256]{1,0:T(8,128)S(1)}, f32[512,256]{1,0:T(8,128)S(1)}, u32[]{:S(2)}, u32[]{:S(2)}) collective-permute-start(f32[512,256]{1,0:T(8,128)S(1)} %get-tuple-element.286), channel_id=1, source_target_pairs={{0,4},{1,5},{2,6},{3,7},{4,0},{5,1},{6,2},{7,3},{8,12},{9,13},{10,... | collective-permute-start | bytes 1572872 | tf_op jit(solution)/shard_map/ppermute | solution.py:710
  91.2 4.5 %collective-permute-start.34 = (f32[4,512]{1,0:T(4,128)S(1)}, f32[4,512]{1,0:T(4,128)S(1)}, u32[]{:S(2)}, u32[]{:S(2)}) collective-permute-start(f32[4,512]{1,0:T(4,128)S(1)} %add_add_fusion.1.stats_0_), channel_id=1, source_target_pairs={{0,16},{8,24},{16,0},{24,8},{1,17},{9,25},{17,1},{25,9},{2,18},{10... | collective-permute-start | bytes 24584 | tf_op jit(solution)/shard_map/ppermute | solution.py:681
  91.5 5.4 %collective-permute-start.33 = (f32[4,512]{1,0:T(4,128)S(1)}, f32[4,512]{1,0:T(4,128)S(1)}, u32[]{:S(2)}, u32[]{:S(2)}) collective-permute-start(f32[4,512]{1,0:T(4,128)S(1)} %add_add_fusion.1.stats_0_), channel_id=1, source_target_pairs={{0,8},{8,16},{16,24},{24,0},{1,9},{9,17},{17,25},{25,1},{2,10},{10... | collective-permute-start | bytes 24584 | tf_op jit(solution)/shard_map/ppermute | solution.py:681
  101.0 9.2 %collective-permute-start.36 = (f32[256,256]{1,0:T(8,128)S(1)}, f32[256,256]{1,0:T(8,128)S(1)}, u32[]{:S(2)}, u32[]{:S(2)}) collective-permute-start(f32[256,256]{1,0:T(8,128)S(1)} %get-tuple-element.304), channel_id=1, source_target_pairs={{0,4},{1,5},{2,6},{3,7},{4,0},{5,1},{6,2},{7,3},{8,12},{9,13},{10,... | collective-permute-start | bytes 786440 | tf_op jit(solution)/shard_map/ppermute | solution.py:710
  102.7 7.5 %collective-permute-start.37 = (f32[256,256]{1,0:T(8,128)S(1)}, f32[256,256]{1,0:T(8,128)S(1)}, u32[]{:S(2)}, u32[]{:S(2)}) collective-permute-start(f32[256,256]{1,0:T(8,128)S(1)} %get-tuple-element.306), channel_id=1, source_target_pairs={{0,2},{1,3},{2,0},{3,1},{4,6},{5,7},{6,4},{7,5},{8,10},{9,11},{10,... | collective-permute-start | bytes 786440 | tf_op jit(solution)/shard_map/ppermute | solution.py:710
  104.9 4.6 %collective-permute-start.41 = (f32[4,768]{1,0:T(4,128)S(1)}, f32[4,768]{1,0:T(4,128)S(1)}, u32[]{:S(2)}, u32[]{:S(2)}) collective-permute-start(f32[4,768]{1,0:T(4,128)S(1)} %pad_maximum_fusion.4.refs_1__0_), channel_id=1, source_target_pairs={{0,2},{1,3},{2,4},{3,5},{4,6},{5,7},{6,0},{7,1},{8,10},{9,11},{10,... | collective-permute-start | bytes 36872 | tf_op jit(solution)/shard_map/ppermute | solution.py:681
  112.3 8.7 %collective-permute-start.42 = (f32[128,512]{1,0:T(8,128)S(1)}, f32[128,512]{1,0:T(8,128)S(1)}, u32[]{:S(2)}, u32[]{:S(2)}) collective-permute-start(f32[128,512]{1,0:T(8,128)S(1)} %get-tuple-element.321), channel_id=1, source_target_pairs={{0,8},{8,0},{16,24},{24,16},{1,9},{9,1},{17,25},{25,17},{2,10},{10... | collective-permute-start | bytes 786440 | tf_op jit(solution)/shard_map/ppermute | solution.py:710
  122.3 18.2 %collective-permute-start.45 = (f32[320,256]{1,0:T(8,128)S(1)}, f32[320,256]{1,0:T(8,128)S(1)}, u32[]{:S(2)}, u32[]{:S(2)}) collective-permute-start(f32[320,256]{1,0:T(8,128)S(1)} %get-tuple-element.350), channel_id=1, source_target_pairs={{0,2},{1,3},{2,0},{3,1},{4,6},{5,7},{6,4},{7,5},{8,10},{9,11},{10,... | collective-permute-start | bytes 983048 | tf_op jit(solution)/shard_map/ppermute | solution.py:710
  125.2 15.3 %collective-permute-start.46 = (f32[320,256]{1,0:T(8,128)S(1)}, f32[320,256]{1,0:T(8,128)S(1)}, u32[]{:S(2)}, u32[]{:S(2)}) collective-permute-start(f32[320,256]{1,0:T(8,128)S(1)} %get-tuple-element.352), channel_id=1, source_target_pairs={{0,4},{1,5},{2,6},{3,7},{4,0},{5,1},{6,2},{7,3},{8,12},{9,13},{10,... | collective-permute-start | bytes 983048 | tf_op jit(solution)/shard_map/ppermute | solution.py:710
  126.1 14.4 %collective-permute-start.44 = (f32[128,512]{1,0:T(8,128)S(1)}, f32[128,512]{1,0:T(8,128)S(1)}, u32[]{:S(2)}, u32[]{:S(2)}) collective-permute-start(f32[128,512]{1,0:T(8,128)S(1)} %add_two.4.own), channel_id=1, source_target_pairs={{0,16},{8,24},{16,0},{24,8},{1,17},{9,25},{17,1},{25,9},{2,18},{10... | collective-permute-start | bytes 786440 | tf_op jit(solution)/shard_map/ppermute | solution.py:710
  127.4 13.2 %collective-permute-start.48 = (f32[192,256]{1,0:T(8,128)S(1)}, f32[192,256]{1,0:T(8,128)S(1)}, u32[]{:S(2)}, u32[]{:S(2)}) collective-permute-start(f32[192,256]{1,0:T(8,128)S(1)} %get-tuple-element.357), channel_id=1, source_target_pairs={{0,2},{1,3},{2,0},{3,1},{4,6},{5,7},{6,4},{7,5},{8,10},{9,11},{10,... | collective-permute-start | bytes 589832 | tf_op jit(solution)/shard_map/ppermute | solution.py:710
  128.2 12.4 %collective-permute-start.49 = (f32[192,256]{1,0:T(8,128)S(1)}, f32[192,256]{1,0:T(8,128)S(1)}, u32[]{:S(2)}, u32[]{:S(2)}) collective-permute-start(f32[192,256]{1,0:T(8,128)S(1)} %get-tuple-element.359), channel_id=1, source_target_pairs={{0,4},{1,5},{2,6},{3,7},{4,0},{5,1},{6,2},{7,3},{8,12},{9,13},{10,... | collective-permute-start | bytes 589832 | tf_op jit(solution)/shard_map/ppermute | solution.py:710
  140.6 8.3 %collective-permute-start.50 = (f32[128,512]{1,0:T(8,128)S(1)}, f32[128,512]{1,0:T(8,128)S(1)}, u32[]{:S(2)}, u32[]{:S(2)}) collective-permute-start(f32[128,512]{1,0:T(8,128)S(1)} %add_two.5.own), channel_id=1, source_target_pairs={{0,8},{8,0},{16,24},{24,16},{1,9},{9,1},{17,25},{25,17},{2,10},{10... | collective-permute-start | bytes 786440 | tf_op jit(solution)/shard_map/ppermute | solution.py:710
  141.3 8.3 %collective-permute-start.51 = (f32[256,256]{1,0:T(8,128)S(1)}, f32[256,256]{1,0:T(8,128)S(1)}, u32[]{:S(2)}, u32[]{:S(2)}) collective-permute-start(f32[256,256]{1,0:T(8,128)S(1)} %get-tuple-element.371), channel_id=1, source_target_pairs={{0,4},{1,5},{2,6},{3,7},{4,0},{5,1},{6,2},{7,3},{8,12},{9,13},{10,... | collective-permute-start | bytes 786440 | tf_op jit(solution)/shard_map/ppermute | solution.py:710
  142.5 7.9 %collective-permute-start.52 = (f32[256,256]{1,0:T(8,128)S(1)}, f32[256,256]{1,0:T(8,128)S(1)}, u32[]{:S(2)}, u32[]{:S(2)}) collective-permute-start(f32[256,256]{1,0:T(8,128)S(1)} %get-tuple-element.373), channel_id=1, source_target_pairs={{0,2},{1,3},{2,0},{3,1},{4,6},{5,7},{6,4},{7,5},{8,10},{9,11},{10,... | collective-permute-start | bytes 786440 | tf_op jit(solution)/shard_map/ppermute | solution.py:710
  151.1 7.1 %collective-permute-start.53 = (f32[256,256]{1,0:T(8,128)S(1)}, f32[256,256]{1,0:T(8,128)S(1)}, u32[]{:S(2)}, u32[]{:S(2)}) collective-permute-start(f32[256,256]{1,0:T(8,128)S(1)} %get-tuple-element.384.refs_0_), channel_id=1, source_target_pairs={{0,4},{1,5},{2,6},{3,7},{4,0},{5,1},{6,2},{7,3},{8,12},{9,13},{10,... | collective-permute-start | bytes 786440 | tf_op jit(solution)/shard_map/ppermute | solution.py:710
  152.0 6.8 %collective-permute-start.54 = (f32[256,256]{1,0:T(8,128)S(1)}, f32[256,256]{1,0:T(8,128)S(1)}, u32[]{:S(2)}, u32[]{:S(2)}) collective-permute-start(f32[256,256]{1,0:T(8,128)S(1)} %get-tuple-element.386.refs_2_), channel_id=1, source_target_pairs={{0,2},{1,3},{2,0},{3,1},{4,6},{5,7},{6,4},{7,5},{8,10},{9,11},{10,... | collective-permute-start | bytes 786440 | tf_op jit(solution)/shard_map/ppermute | solution.py:710
  152.9 6.6 %collective-permute-start.55 = (f32[128,512]{1,0:T(8,128)S(1)}, f32[128,512]{1,0:T(8,128)S(1)}, u32[]{:S(2)}, u32[]{:S(2)}) collective-permute-start(f32[128,512]{1,0:T(8,128)S(1)} %get-tuple-element.383), channel_id=1, source_target_pairs={{0,8},{8,0},{16,24},{24,16},{1,9},{9,1},{17,25},{25,17},{2,10},{10... | collective-permute-start | bytes 786440 | tf_op jit(solution)/shard_map/ppermute | solution.py:710
  160.1 14.6 %collective-permute-start.56 = (f32[512,256]{1,0:T(8,128)S(1)}, f32[512,256]{1,0:T(8,128)S(1)}, u32[]{:S(2)}, u32[]{:S(2)}) collective-permute-start(f32[512,256]{1,0:T(8,128)S(1)} %get-tuple-element.415.refs_0_), channel_id=1, source_target_pairs={{0,2},{1,3},{2,0},{3,1},{4,6},{5,7},{6,4},{7,5},{8,10},{9,11},{10,... | collective-permute-start | bytes 1572872 | tf_op jit(solution)/shard_map/ppermute | solution.py:710
  161.9 12.8 %collective-permute-start.57 = (f32[512,256]{1,0:T(8,128)S(1)}, f32[512,256]{1,0:T(8,128)S(1)}, u32[]{:S(2)}, u32[]{:S(2)}) collective-permute-start(f32[512,256]{1,0:T(8,128)S(1)} %get-tuple-element.417.refs_2_), channel_id=1, source_target_pairs={{0,4},{1,5},{2,6},{3,7},{4,0},{5,1},{6,2},{7,3},{8,12},{9,13},{10,... | collective-permute-start | bytes 1572872 | tf_op jit(solution)/shard_map/ppermute | solution.py:710
  163.1 11.6 %collective-permute-start.58 = (f32[128,512]{1,0:T(8,128)S(1)}, f32[128,512]{1,0:T(8,128)S(1)}, u32[]{:S(2)}, u32[]{:S(2)}) collective-permute-start(f32[128,512]{1,0:T(8,128)S(1)} %add_two.6.own), channel_id=1, source_target_pairs={{0,16},{8,24},{16,0},{24,8},{1,17},{9,25},{17,1},{25,9},{2,18},{10... | collective-permute-start | bytes 786440 | tf_op jit(solution)/shard_map/ppermute | solution.py:710
  174.8 8.3 %collective-permute-start.59 = (f32[128,512]{1,0:T(8,128)S(1)}, f32[128,512]{1,0:T(8,128)S(1)}, u32[]{:S(2)}, u32[]{:S(2)}) collective-permute-start(f32[128,512]{1,0:T(8,128)S(1)} %add_two.7.own), channel_id=1, source_target_pairs={{0,8},{8,0},{16,24},{24,16},{1,9},{9,1},{17,25},{25,17},{2,10},{10... | collective-permute-start | bytes 786440 | tf_op jit(solution)/shard_map/ppermute | solution.py:710
  178.0 5.0 %collective-permute-start.61 = (f32[24,512]{1,0:T(8,128)S(1)}, f32[24,512]{1,0:T(8,128)S(1)}, u32[]{:S(2)}, u32[]{:S(2)}) collective-permute-start(f32[24,512]{1,0:T(8,128)S(1)} %add.77), channel_id=1, source_target_pairs={{0,2},{1,3},{2,4},{3,5},{4,6},{5,7},{6,0},{7,1},{8,10},{9,11},{10,... | collective-permute-start | bytes 147464 | tf_op jit(solution)/shard_map/ppermute | solution.py:681
  184.3 18.2 %collective-permute-start.72 = (f32[1024,512]{1,0:T(8,128)S(1)}, f32[1024,512]{1,0:T(8,128)S(1)}, u32[]{:S(2)}, u32[]{:S(2)}) collective-permute-start(f32[1024,512]{1,0:T(8,128)S(1)} %unfold_sides.6.refs_0_), channel_id=1, source_target_pairs={{0,1},{1,0},{2,3},{3,2},{4,5},{5,4},{6,7},{7,6},{8,9},{9,8},{10,11... | collective-permute-start | bytes 6291464 | tf_op jit(solution)/shard_map/ppermute | solution.py:710
  184.4 10.7 %collective-permute-start.64 = (f32[256,256]{1,0:T(8,128)S(1)}, f32[256,256]{1,0:T(8,128)S(1)}, u32[]{:S(2)}, u32[]{:S(2)}) collective-permute-start(f32[256,256]{1,0:T(8,128)S(1)} %get-tuple-element.422.refs_0_), channel_id=1, source_target_pairs={{0,4},{1,5},{2,6},{3,7},{4,0},{5,1},{6,2},{7,3},{8,12},{9,13},{10,... | collective-permute-start | bytes 786440 | tf_op jit(solution)/shard_map/ppermute | solution.py:710
  185.3 9.7 %collective-permute-start.65 = (f32[256,256]{1,0:T(8,128)S(1)}, f32[256,256]{1,0:T(8,128)S(1)}, u32[]{:S(2)}, u32[]{:S(2)}) collective-permute-start(f32[256,256]{1,0:T(8,128)S(1)} %get-tuple-element.424.refs_2_), channel_id=1, source_target_pairs={{0,2},{1,3},{2,0},{3,1},{4,6},{5,7},{6,4},{7,5},{8,10},{9,11},{10,... | collective-permute-start | bytes 786440 | tf_op jit(solution)/shard_map/ppermute | solution.py:710
  190.0 5.1 %collective-permute-start.67 = (f32[24,512]{1,0:T(8,128)S(1)}, f32[24,512]{1,0:T(8,128)S(1)}, u32[]{:S(2)}, u32[]{:S(2)}) collective-permute-start(f32[24,512]{1,0:T(8,128)S(1)} %add.81), channel_id=1, source_target_pairs={{0,16},{8,24},{16,0},{24,8},{1,17},{9,25},{17,1},{25,9},{2,18},{10... | collective-permute-start | bytes 147464 | tf_op jit(solution)/shard_map/ppermute | solution.py:710
  195.7 12.0 %collective-permute-start.68 = (f32[512,256]{1,0:T(8,128)S(1)}, f32[512,256]{1,0:T(8,128)S(1)}, u32[]{:S(2)}, u32[]{:S(2)}) collective-permute-start(f32[512,256]{1,0:T(8,128)S(1)} %get-tuple-element.453.refs_0_), channel_id=1, source_target_pairs={{0,2},{1,3},{2,0},{3,1},{4,6},{5,7},{6,4},{7,5},{8,10},{9,11},{10,... | collective-permute-start | bytes 1572872 | tf_op jit(solution)/shard_map/ppermute | solution.py:710
  197.3 11.6 %collective-permute-start.69 = (f32[512,256]{1,0:T(8,128)S(1)}, f32[512,256]{1,0:T(8,128)S(1)}, u32[]{:S(2)}, u32[]{:S(2)}) collective-permute-start(f32[512,256]{1,0:T(8,128)S(1)} %get-tuple-element.454.refs_2_), channel_id=1, source_target_pairs={{0,4},{1,5},{2,6},{3,7},{4,0},{5,1},{6,2},{7,3},{8,12},{9,13},{10,... | collective-permute-start | bytes 1572872 | tf_op jit(solution)/shard_map/ppermute | solution.py:710
  198.5 10.5 %collective-permute-start.70 = (f32[512,256]{1,0:T(8,128)S(1)}, f32[512,256]{1,0:T(8,128)S(1)}, u32[]{:S(2)}, u32[]{:S(2)}) collective-permute-start(f32[512,256]{1,0:T(8,128)S(1)} %get-tuple-element.453.refs_0_), channel_id=1, source_target_pairs={{0,1},{1,0},{2,3},{3,2},{4,5},{5,4},{6,7},{7,6},{8,9},{9,8},{10,11... | collective-permute-start | bytes 1572872 | tf_op jit(solution)/shard_map/ppermute | solution.py:710
  198.5 10.5 %collective-permute-start.71 = (f32[512,256]{1,0:T(8,128)S(1)}, f32[512,256]{1,0:T(8,128)S(1)}, u32[]{:S(2)}, u32[]{:S(2)}) collective-permute-start(f32[512,256]{1,0:T(8,128)S(1)} %get-tuple-element.454.refs_2_), channel_id=1, source_target_pairs={{0,1},{1,0},{2,3},{3,2},{4,5},{5,4},{6,7},{7,6},{8,9},{9,8},{10,11... | collective-permute-start | bytes 1572872 | tf_op jit(solution)/shard_map/ppermute | solution.py:710
  (36 other events, 200.4 us)

commit v4 on v3

--- a/solution.py
+++ b/solution.py
@@ -142,7 +142,7 @@
             more = visit(more, batch, None, first, start, keeps, None)
         return tuple(states), more
 
-    return lax.fori_loop(0, steps // 2, pair, (tuple(init), extra), unroll=4)
+    return lax.fori_loop(0, steps // 2, pair, (tuple(init), extra), unroll=8)
 
 
 def zero_states(batches, groups):

time: 215 us -> 215 us (level)
  no operation moved by 1% of the time
where the time goes in v4:
time: 215 us
  waiting for transfers between devices  89.6 us (42%)
  starting transfers between devices  70.9 us (33%)
  Pallas kernels  46.7 us (22%)
  local copies, waits for them, and re-layouts  4.39 us (2%)
  other arithmetic  2.39 us (1%)
    ppermute x40, waiting for transfers between devices, swap(): lax.ppermute(value, axis, [(i, i ^ bit) for i in range(lax.axis_size(axis...  51.9 us
    pallas_call x33, Pallas kernels, run(): pl.pallas_call(body, name=name, out_shape=tuple((jax.ShapeDtypeStruct(*ou...  39.6 us
    ppermute x35, starting transfers between devices, shifted(): return lax.ppermute(value, name, pairs)  39.1 us
    ppermute x35, waiting for transfers between devices, shifted(): return lax.ppermute(value, name, pairs)  37.6 us
    ppermute x40, starting transfers between devices, swap(): lax.ppermute(value, axis, [(i, i ^ bit) for i in range(lax.axis_size(axis...  31.8 us
    pallas_call x3, Pallas kernels, put_in_place(): pl.pallas_call(body, name='put_in_place', out_shape=tuple((jax.ShapeDtype...  7.07 us
  transfers between devices with their start and end apart: 75, of which 49 were waited for; matrix products, arithmetic and copies ran while one was open for 2% of the time, Pallas kernels for 9%

profile of v4, /device:TPU:0, one launch (start us, length us, event | category | flops | bytes accessed | tf_op | source)
XLA Modules:
  0.0 215.2 jit_solution(5787676142296580325)
XLA Ops:
  4.2 3.8 %collective-permute-start.3 = (f32[4,512]{1,0:T(4,128)S(1)}, f32[4,512]{1,0:T(4,128)S(1)}, u32[]{:S(2)}, u32[]{:S(2)}) collective-permute-start(f32[4,512]{1,0:T(4,128)S(1)} %add.63), channel_id=1, source_target_pairs={{0,6},{1,7},{2,0},{3,1},{4,2},{5,3},{6,4},{7,5},{8,14},{9,15},{10,... | collective-permute-start | bytes 24584 | tf_op jit(solution)/shard_map/ppermute | solution.py:681
  9.9 1.8 collective-permute-done.2
  13.1 3.6 %collective-permute-start.6 = (f32[4,512]{1,0:T(4,128)S(1)}, f32[4,512]{1,0:T(4,128)S(1)}, u32[]{:S(2)}, u32[]{:S(2)}) collective-permute-start(f32[4,512]{1,0:T(4,128)S(1)} %add_add_fusion.3.stats_0_), channel_id=1, source_target_pairs={{0,24},{8,0},{16,8},{24,16},{1,25},{9,1},{17,9},{25,17},{2,26},{10... | collective-permute-start | bytes 24584 | tf_op jit(solution)/shard_map/ppermute | solution.py:681
  18.7 2.5 %collective-permute-done.5.stats_2_ = f32[4,512]{1,0:T(4,128)S(1)} collective-permute-done((f32[4,512]{1,0:T(4,128)S(1)}, f32[4,512]{1,0:T(4,128)S(1)}, u32[]{:S(2)}, u32[]{:S(2)}) %collective-permute-start.5) | collective-permute-done | bytes 8224 | tf_op jit(solution)/shard_map/ppermute | solution.py:681
  22.1 1.9 enter_layer.2
  25.4 1.5 collective-permute-start.9
  27.0 1.9 collective-permute-start.8
  29.1 2.4 %collective-permute-done.8.ends_1_ = f32[4,768]{1,0:T(4,128)S(1)} collective-permute-done((f32[4,768]{1,0:T(4,128)S(1)}, f32[4,768]{1,0:T(4,128)S(1)}, u32[]{:S(2)}, u32[]{:S(2)}) %collective-permute-start.8) | collective-permute-done | bytes 12320 | tf_op jit(solution)/shard_map/ppermute | solution.py:681
  32.8 3.6 %middle_forward.1 = (f32[528,768]{1,0:T(8,128)S(1)}, bf16[512,768]{1,0:T(8,128)(2,1)S(1)}, bf16[512,512]{1,0:T(8,128)(2,1)S(1)}, f32[512,512]{1,0:T(8,128)S(1)},...) custom-call(s32[10]{0:T(128)S(1)} %pad_add_fusion.place.here.refs_0_, ...), custom_call_target="tpu_custom_call" | custom-call | tf_op jit(solution)/shard_map/middle_forward/pallas_call | solution.py:609
  38.6 1.5 collective-permute-start.13
  42.3 2.4 %collective-permute-done.12 = f32[4,512]{1,0:T(4,128)S(1)} collective-permute-done((f32[4,512]{1,0:T(4,128)S(1)}, f32[4,512]{1,0:T(4,128)S(1)}, u32[]{:S(2)}, u32[]{:S(2)}) %collective-permute-start.12) | collective-permute-done | bytes 8224 | tf_op jit(solution)/shard_map/ppermute | solution.py:681
  45.9 2.0 collective-permute-start.15
  49.8 1.5 collective-permute-done.15.stats_1_
  51.3 1.9 enter_layer.3
  55.2 2.8 %collective-permute-start.19 = (f32[4,768]{1,0:T(4,128)S(1)}, f32[4,768]{1,0:T(4,128)S(1)}, u32[]{:S(2)}, u32[]{:S(2)}) collective-permute-start(f32[4,768]{1,0:T(4,128)S(1)} %pad_maximum_fusion.2.ends_0_), channel_id=1, source_target_pairs={{0,6},{1,7},{2,0},{3,1},{4,2},{5,3},{6,4},{7,5},{8,14},{9,15},{10,... | collective-permute-start | bytes 36872 | tf_op jit(solution)/shard_map/ppermute | solution.py:681
  59.7 5.8 %turn_around.1 = (bf16[512,512]{1,0:T(8,128)(2,1)S(1)}, f32[528,768]{1,0:T(8,128)S(1)}, bf16[512,768]{1,0:T(8,128)(2,1)S(1)}, bf16[512,512]{1,0:T(8,128)(2,1)S(1...) custom-call(s32[10]{0:T(128)S(1)} %pad_add_fusion.place.here.refs_0_, ...), custom_call_target="tpu_custom_call" | custom-call | tf_op jit(solution)/shard_map/turn_around/pallas_call | solution.py:609
  66.8 2.9 %collective-permute-start.25 = (f32[4,768]{1,0:T(4,128)S(1)}, f32[4,768]{1,0:T(4,128)S(1)}, u32[]{:S(2)}, u32[]{:S(2)}) collective-permute-start(f32[4,768]{1,0:T(4,128)S(1)} %pad_maximum_fusion.3.ends_0_), channel_id=1, source_target_pairs={{0,6},{1,7},{2,0},{3,1},{4,2},{5,3},{6,4},{7,5},{8,14},{9,15},{10,... | collective-permute-start | bytes 36872 | tf_op jit(solution)/shard_map/ppermute | solution.py:681
  69.7 1.5 collective-permute-start.24
  71.5 2.0 collective-permute-done.24.ends_2_
  73.4 2.4 %collective-permute-done.23.ends_1_ = f32[4,768]{1,0:T(4,128)S(1)} collective-permute-done((f32[4,768]{1,0:T(4,128)S(1)}, f32[4,768]{1,0:T(4,128)S(1)}, u32[]{:S(2)}, u32[]{:S(2)}) %collective-permute-start.23) | collective-permute-done | bytes 12320 | tf_op jit(solution)/shard_map/ppermute | solution.py:681
  75.9 2.8 %backward_finish.2 = (bf16[512,768]{1,0:T(8,128)(2,1)S(1)}, f32[512,512]{1,0:T(8,128)S(1)}, f32[4,512]{1,0:T(4,128)S(1)}, f32[8,512]{1,0:T(8,128)S(1)}) custom-call(s32[10]{0:T(128)S(1)} %pad_add_fusion.place.here.refs_0_, f32[4,768]{1,0:T(4,128)S(1)} %pad_maximum_fusion.3.ends_0_, f32[4,768]{1,0:T(4,128)S(1)} %collective-permute-done.23.ends_1_, ...), custom_call_target="tpu_custom_call" | custom-call | tf_op jit(solution)/shard_map/backward_finish/pallas_call | solution.py:609
  78.7 1.8 all_weights.1
  81.7 2.0 collective-permute-start.27
  93.6 2.3 %collective-permute-done.34.stats_2_ = f32[4,512]{1,0:T(4,128)S(1)} collective-permute-done((f32[4,512]{1,0:T(4,128)S(1)}, f32[4,512]{1,0:T(4,128)S(1)}, u32[]{:S(2)}, u32[]{:S(2)}) %collective-permute-start.34) | collective-permute-done | bytes 8224 | tf_op jit(solution)/shard_map/ppermute | solution.py:681
  97.0 3.3 %between_layers.1 = (f32[512,512]{1,0:T(8,128)S(1)}, f32[2,512]{1,0:T(2,128)S(1)}, bf16[512,512]{1,0:T(8,128)(2,1)S(1)}, f32[512,512]{1,0:T(8,128)S(1)}, bf16[51...) custom-call(s32[10]{0:T(128)S(1)} %pad_add_fusion.place.here.refs_0_, ...), custom_call_target="tpu_custom_call" | custom-call | tf_op jit(solution)/shard_map/between_layers/pallas_call | solution.py:609
  101.0 1.8 collective-permute-start.36
  106.4 2.5 %collective-permute-start.39 = (f32[4,768]{1,0:T(4,128)S(1)}, f32[4,768]{1,0:T(4,128)S(1)}, u32[]{:S(2)}, u32[]{:S(2)}) collective-permute-start(f32[4,768]{1,0:T(4,128)S(1)} %pad_maximum_fusion.4.refs_1__0_), channel_id=1, source_target_pairs={{0,6},{1,7},{2,0},{3,1},{4,2},{5,3},{6,4},{7,5},{8,14},{9,15},{10,... | collective-permute-start | bytes 36872 | tf_op jit(solution)/shard_map/ppermute | solution.py:681
  112.6 2.8 %backward_finish.3 = (bf16[512,768]{1,0:T(8,128)(2,1)S(1)}, f32[512,512]{1,0:T(8,128)S(1)}, f32[24,512]{1,0:T(8,128)S(1)}) custom-call(s32[10]{0:T(128)S(1)} %pad_add_fusion.place.here.refs_0_, f32[4,768]{1,0:T(4,128)S(1)} %pad_maximum_fusion.4.refs_1__0_, f32[4,768]{1,0:T(4,128)S(1)} %collective-permute-done.39.refs_1__1_, ...), custom_call_target="tpu_custom_call" | custom-call | tf_op jit(solution)/shard_map/backward_finish/pallas_call | solution.py:609
  116.2 5.0 %collective-permute-done.42.found = f32[128,512]{1,0:T(8,128)S(1)} collective-permute-done((f32[128,512]{1,0:T(8,128)S(1)}, f32[128,512]{1,0:T(8,128)S(1)}, u32[]{:S(2)}, u32[]{:S(2)}) %collective-permute-start.42) | collective-permute-done | bytes 262176 | tf_op jit(solution)/shard_map/ppermute | solution.py:710
  122.4 2.9 %collective-permute-start.45 = (f32[320,256]{1,0:T(8,128)S(1)}, f32[320,256]{1,0:T(8,128)S(1)}, u32[]{:S(2)}, u32[]{:S(2)}) collective-permute-start(f32[320,256]{1,0:T(8,128)S(1)} %get-tuple-element.350), channel_id=1, source_target_pairs={{0,2},{1,3},{2,0},{3,1},{4,6},{5,7},{6,4},{7,5},{8,10},{9,11},{10,... | collective-permute-start | bytes 983048 | tf_op jit(solution)/shard_map/ppermute | solution.py:710
  129.1 11.5 %collective-permute-done.44.found = f32[128,512]{1,0:T(8,128)S(1)} collective-permute-done((f32[128,512]{1,0:T(8,128)S(1)}, f32[128,512]{1,0:T(8,128)S(1)}, u32[]{:S(2)}, u32[]{:S(2)}) %collective-permute-start.44) | collective-permute-done | bytes 262176 | tf_op jit(solution)/shard_map/ppermute | solution.py:710
  142.9 6.1 %collective-permute-done.50.found = f32[128,512]{1,0:T(8,128)S(1)} collective-permute-done((f32[128,512]{1,0:T(8,128)S(1)}, f32[128,512]{1,0:T(8,128)S(1)}, u32[]{:S(2)}, u32[]{:S(2)}) %collective-permute-start.50) | collective-permute-done | bytes 262176 | tf_op jit(solution)/shard_map/ppermute | solution.py:710
  153.0 1.8 collective-permute-start.55
  154.8 3.5 %collective-permute-done.53.refs_1_ = f32[256,256]{1,0:T(8,128)S(1)} collective-permute-done((f32[256,256]{1,0:T(8,128)S(1)}, f32[256,256]{1,0:T(8,128)S(1)}, u32[]{:S(2)}, u32[]{:S(2)}) %collective-permute-start.53) | collective-permute-done | bytes 262176 | tf_op jit(solution)/shard_map/ppermute | solution.py:710
  160.2 1.8 collective-permute-start.56
  163.2 1.9 collective-permute-start.58
  165.1 9.7 %collective-permute-done.58.found = f32[128,512]{1,0:T(8,128)S(1)} collective-permute-done((f32[128,512]{1,0:T(8,128)S(1)}, f32[128,512]{1,0:T(8,128)S(1)}, u32[]{:S(2)}, u32[]{:S(2)}) %collective-permute-start.58) | collective-permute-done | bytes 262176 | tf_op jit(solution)/shard_map/ppermute | solution.py:710
  181.0 2.0 collective-permute-done.61
  185.9 2.0 collective-permute-start.66
  187.9 2.1 collective-permute-done.66
  190.1 2.2 %collective-permute-start.67 = (f32[24,512]{1,0:T(8,128)S(1)}, f32[24,512]{1,0:T(8,128)S(1)}, u32[]{:S(2)}, u32[]{:S(2)}) collective-permute-start(f32[24,512]{1,0:T(8,128)S(1)} %add.81), channel_id=1, source_target_pairs={{0,16},{8,24},{16,0},{24,8},{1,17},{9,25},{17,1},{25,9},{2,18},{10... | collective-permute-start | bytes 147464 | tf_op jit(solution)/shard_map/ppermute | solution.py:710
  193.4 1.7 collective-permute-done.67
  195.8 1.6 collective-permute-start.68
  199.1 1.6 last_step.1
  202.6 2.9 %put_in_place.3 = (f32[2,512,512]{2,1,0:T(8,128)}, f32[2,768,512]{2,1,0:T(8,128)}, f32[2,512,768]{2,1,0:T(8,128)}) custom-call(s32[10]{0:T(128)S(1)} %pad_add_fusion.place.here.refs_0_, f32[1024,512]{1,0:T(8,128)S(1)} %unfold_sides.6.refs_0_, f32[1024,512]{1,0:T(8,128)S(1)} %collective-permute-done.72.refs_1_), custom_call_target="tpu_custom_call" | custom-call | tf_op jit(solution)/shard_map/put_in_place/pallas_call | solution.py:655
  205.5 2.3 %collective-permute-done.68.refs_1_ = f32[512,256]{1,0:T(8,128)S(1)} collective-permute-done((f32[512,256]{1,0:T(8,128)S(1)}, f32[512,256]{1,0:T(8,128)S(1)}, u32[]{:S(2)}, u32[]{:S(2)}) %collective-permute-start.68) | collective-permute-done | bytes 524320 | tf_op jit(solution)/shard_map/ppermute | solution.py:710
  210.3 2.1 put_in_place.4
  213.1 2.1 put_in_place.5
  (182 shorter events, 78.1 us)
Async XLA Ops:
  4.2 5.7 %collective-permute-start.3 = (f32[4,512]{1,0:T(4,128)S(1)}, f32[4,512]{1,0:T(4,128)S(1)}, u32[]{:S(2)}, u32[]{:S(2)}) collective-permute-start(f32[4,512]{1,0:T(4,128)S(1)} %add.63), channel_id=1, source_target_pairs={{0,6},{1,7},{2,0},{3,1},{4,2},{5,3},{6,4},{7,5},{8,14},{9,15},{10,... | collective-permute-start | bytes 24584 | tf_op jit(solution)/shard_map/ppermute | solution.py:681
  8.5 4.5 %collective-permute-start.1 = (f32[4,512]{1,0:T(4,128)S(1)}, f32[4,512]{1,0:T(4,128)S(1)}, u32[]{:S(2)}, u32[]{:S(2)}) collective-permute-start(f32[4,512]{1,0:T(4,128)S(1)} %add.63), channel_id=1, source_target_pairs={{0,2},{1,3},{2,4},{3,5},{4,6},{5,7},{6,0},{7,1},{8,10},{9,11},{10,... | collective-permute-start | bytes 24584 | tf_op jit(solution)/shard_map/ppermute | solution.py:681
  13.1 5.7 %collective-permute-start.6 = (f32[4,512]{1,0:T(4,128)S(1)}, f32[4,512]{1,0:T(4,128)S(1)}, u32[]{:S(2)}, u32[]{:S(2)}) collective-permute-start(f32[4,512]{1,0:T(4,128)S(1)} %add_add_fusion.3.stats_0_), channel_id=1, source_target_pairs={{0,24},{8,0},{16,8},{24,16},{1,25},{9,1},{17,9},{25,17},{2,26},{10... | collective-permute-start | bytes 24584 | tf_op jit(solution)/shard_map/ppermute | solution.py:681
  16.7 4.5 %collective-permute-start.5 = (f32[4,512]{1,0:T(4,128)S(1)}, f32[4,512]{1,0:T(4,128)S(1)}, u32[]{:S(2)}, u32[]{:S(2)}) collective-permute-start(f32[4,512]{1,0:T(4,128)S(1)} %add_add_fusion.3.stats_0_), channel_id=1, source_target_pairs={{0,16},{8,24},{16,0},{24,8},{1,17},{9,25},{17,1},{25,9},{2,18},{10... | collective-permute-start | bytes 24584 | tf_op jit(solution)/shard_map/ppermute | solution.py:681
  16.7 5.4 %collective-permute-start.4 = (f32[4,512]{1,0:T(4,128)S(1)}, f32[4,512]{1,0:T(4,128)S(1)}, u32[]{:S(2)}, u32[]{:S(2)}) collective-permute-start(f32[4,512]{1,0:T(4,128)S(1)} %add_add_fusion.3.stats_0_), channel_id=1, source_target_pairs={{0,8},{8,16},{16,24},{24,0},{1,9},{9,17},{17,25},{25,1},{2,10},{10... | collective-permute-start | bytes 24584 | tf_op jit(solution)/shard_map/ppermute | solution.py:681
  27.0 4.6 %collective-permute-start.8 = (f32[4,768]{1,0:T(4,128)S(1)}, f32[4,768]{1,0:T(4,128)S(1)}, u32[]{:S(2)}, u32[]{:S(2)}) collective-permute-start(f32[4,768]{1,0:T(4,128)S(1)} %pad_maximum_fusion.1.ends_0_), channel_id=1, source_target_pairs={{0,2},{1,3},{2,4},{3,5},{4,6},{5,7},{6,0},{7,1},{8,10},{9,11},{10,... | collective-permute-start | bytes 36872 | tf_op jit(solution)/shard_map/ppermute | solution.py:681
  40.1 4.5 %collective-permute-start.12 = (f32[4,512]{1,0:T(4,128)S(1)}, f32[4,512]{1,0:T(4,128)S(1)}, u32[]{:S(2)}, u32[]{:S(2)}) collective-permute-start(f32[4,512]{1,0:T(4,128)S(1)} %add.69), channel_id=1, source_target_pairs={{0,2},{1,3},{2,4},{3,5},{4,6},{5,7},{6,0},{7,1},{8,10},{9,11},{10,... | collective-permute-start | bytes 24584 | tf_op jit(solution)/shard_map/ppermute | solution.py:681
  45.3 4.5 %collective-permute-start.16 = (f32[4,512]{1,0:T(4,128)S(1)}, f32[4,512]{1,0:T(4,128)S(1)}, u32[]{:S(2)}, u32[]{:S(2)}) collective-permute-start(f32[4,512]{1,0:T(4,128)S(1)} %add_add_fusion.2.stats_0_), channel_id=1, source_target_pairs={{0,16},{8,24},{16,0},{24,8},{1,17},{9,25},{17,1},{25,9},{2,18},{10... | collective-permute-start | bytes 24584 | tf_op jit(solution)/shard_map/ppermute | solution.py:681
  45.9 5.4 %collective-permute-start.15 = (f32[4,512]{1,0:T(4,128)S(1)}, f32[4,512]{1,0:T(4,128)S(1)}, u32[]{:S(2)}, u32[]{:S(2)}) collective-permute-start(f32[4,512]{1,0:T(4,128)S(1)} %add_add_fusion.2.stats_0_), channel_id=1, source_target_pairs={{0,8},{8,16},{16,24},{24,0},{1,9},{9,17},{17,25},{25,1},{2,10},{10... | collective-permute-start | bytes 24584 | tf_op jit(solution)/shard_map/ppermute | solution.py:681
  54.5 4.6 %collective-permute-start.21 = (f32[4,768]{1,0:T(4,128)S(1)}, f32[4,768]{1,0:T(4,128)S(1)}, u32[]{:S(2)}, u32[]{:S(2)}) collective-permute-start(f32[4,768]{1,0:T(4,128)S(1)} %pad_maximum_fusion.2.ends_0_), channel_id=1, source_target_pairs={{0,2},{1,3},{2,4},{3,5},{4,6},{5,7},{6,0},{7,1},{8,10},{9,11},{10,... | collective-permute-start | bytes 36872 | tf_op jit(solution)/shard_map/ppermute | solution.py:681
  54.6 4.6 %collective-permute-start.20 = (f32[4,768]{1,0:T(4,128)S(1)}, f32[4,768]{1,0:T(4,128)S(1)}, u32[]{:S(2)}, u32[]{:S(2)}) collective-permute-start(f32[4,768]{1,0:T(4,128)S(1)} %pad_maximum_fusion.2.ends_0_), channel_id=1, source_target_pairs={{0,4},{1,5},{2,6},{3,7},{4,0},{5,1},{6,2},{7,3},{8,12},{9,13},{10,... | collective-permute-start | bytes 36872 | tf_op jit(solution)/shard_map/ppermute | solution.py:681
  55.2 4.5 %collective-permute-start.19 = (f32[4,768]{1,0:T(4,128)S(1)}, f32[4,768]{1,0:T(4,128)S(1)}, u32[]{:S(2)}, u32[]{:S(2)}) collective-permute-start(f32[4,768]{1,0:T(4,128)S(1)} %pad_maximum_fusion.2.ends_0_), channel_id=1, source_target_pairs={{0,6},{1,7},{2,0},{3,1},{4,2},{5,3},{6,4},{7,5},{8,14},{9,15},{10,... | collective-permute-start | bytes 36872 | tf_op jit(solution)/shard_map/ppermute | solution.py:681
  66.8 4.6 %collective-permute-start.25 = (f32[4,768]{1,0:T(4,128)S(1)}, f32[4,768]{1,0:T(4,128)S(1)}, u32[]{:S(2)}, u32[]{:S(2)}) collective-permute-start(f32[4,768]{1,0:T(4,128)S(1)} %pad_maximum_fusion.3.ends_0_), channel_id=1, source_target_pairs={{0,6},{1,7},{2,0},{3,1},{4,2},{5,3},{6,4},{7,5},{8,14},{9,15},{10,... | collective-permute-start | bytes 36872 | tf_op jit(solution)/shard_map/ppermute | solution.py:681
  71.3 4.6 %collective-permute-start.23 = (f32[4,768]{1,0:T(4,128)S(1)}, f32[4,768]{1,0:T(4,128)S(1)}, u32[]{:S(2)}, u32[]{:S(2)}) collective-permute-start(f32[4,768]{1,0:T(4,128)S(1)} %pad_maximum_fusion.3.ends_0_), channel_id=1, source_target_pairs={{0,2},{1,3},{2,4},{3,5},{4,6},{5,7},{6,0},{7,1},{8,10},{9,11},{10,... | collective-permute-start | bytes 36872 | tf_op jit(solution)/shard_map/ppermute | solution.py:681
  80.6 5.7 %collective-permute-start.30 = (f32[1024,512]{1,0:T(8,128)S(1)}, f32[1024,512]{1,0:T(8,128)S(1)}, u32[]{:S(2)}, u32[]{:S(2)}) collective-permute-start(f32[1024,512]{1,0:T(8,128)S(1)} %get-tuple-element.278), channel_id=1, source_target_pairs={{0,1},{1,0},{2,3},{3,2},{4,5},{5,4},{6,7},{7,6},{8,9},{9,8},{10,11... | collective-permute-start | bytes 6291464 | tf_op jit(solution)/shard_map/ppermute | solution.py:710
  81.7 4.5 %collective-permute-start.27 = (f32[4,512]{1,0:T(4,128)S(1)}, f32[4,512]{1,0:T(4,128)S(1)}, u32[]{:S(2)}, u32[]{:S(2)}) collective-permute-start(f32[4,512]{1,0:T(4,128)S(1)} %add.73), channel_id=1, source_target_pairs={{0,2},{1,3},{2,4},{3,5},{4,6},{5,7},{6,0},{7,1},{8,10},{9,11},{10,... | collective-permute-start | bytes 24584 | tf_op jit(solution)/shard_map/ppermute | solution.py:681
  87.3 13.0 %collective-permute-start.31 = (f32[512,256]{1,0:T(8,128)S(1)}, f32[512,256]{1,0:T(8,128)S(1)}, u32[]{:S(2)}, u32[]{:S(2)}) collective-permute-start(f32[512,256]{1,0:T(8,128)S(1)} %get-tuple-element.284), channel_id=1, source_target_pairs={{0,2},{1,3},{2,0},{3,1},{4,6},{5,7},{6,4},{7,5},{8,10},{9,11},{10,... | collective-permute-start | bytes 1572872 | tf_op jit(solution)/shard_map/ppermute | solution.py:710
  88.4 11.9 %collective-permute-start.32 = (f32[512,256]{1,0:T(8,128)S(1)}, f32[512,256]{1,0:T(8,128)S(1)}, u32[]{:S(2)}, u32[]{:S(2)}) collective-permute-start(f32[512,256]{1,0:T(8,128)S(1)} %get-tuple-element.286), channel_id=1, source_target_pairs={{0,4},{1,5},{2,6},{3,7},{4,0},{5,1},{6,2},{7,3},{8,12},{9,13},{10,... | collective-permute-start | bytes 1572872 | tf_op jit(solution)/shard_map/ppermute | solution.py:710
  91.3 4.6 %collective-permute-start.34 = (f32[4,512]{1,0:T(4,128)S(1)}, f32[4,512]{1,0:T(4,128)S(1)}, u32[]{:S(2)}, u32[]{:S(2)}) collective-permute-start(f32[4,512]{1,0:T(4,128)S(1)} %add_add_fusion.1.stats_0_), channel_id=1, source_target_pairs={{0,16},{8,24},{16,0},{24,8},{1,17},{9,25},{17,1},{25,9},{2,18},{10... | collective-permute-start | bytes 24584 | tf_op jit(solution)/shard_map/ppermute | solution.py:681
  91.6 5.4 %collective-permute-start.33 = (f32[4,512]{1,0:T(4,128)S(1)}, f32[4,512]{1,0:T(4,128)S(1)}, u32[]{:S(2)}, u32[]{:S(2)}) collective-permute-start(f32[4,512]{1,0:T(4,128)S(1)} %add_add_fusion.1.stats_0_), channel_id=1, source_target_pairs={{0,8},{8,16},{16,24},{24,0},{1,9},{9,17},{17,25},{25,1},{2,10},{10... | collective-permute-start | bytes 24584 | tf_op jit(solution)/shard_map/ppermute | solution.py:681
  101.0 9.3 %collective-permute-start.36 = (f32[256,256]{1,0:T(8,128)S(1)}, f32[256,256]{1,0:T(8,128)S(1)}, u32[]{:S(2)}, u32[]{:S(2)}) collective-permute-start(f32[256,256]{1,0:T(8,128)S(1)} %get-tuple-element.304), channel_id=1, source_target_pairs={{0,4},{1,5},{2,6},{3,7},{4,0},{5,1},{6,2},{7,3},{8,12},{9,13},{10,... | collective-permute-start | bytes 786440 | tf_op jit(solution)/shard_map/ppermute | solution.py:710
  102.8 7.5 %collective-permute-start.37 = (f32[256,256]{1,0:T(8,128)S(1)}, f32[256,256]{1,0:T(8,128)S(1)}, u32[]{:S(2)}, u32[]{:S(2)}) collective-permute-start(f32[256,256]{1,0:T(8,128)S(1)} %get-tuple-element.306), channel_id=1, source_target_pairs={{0,2},{1,3},{2,0},{3,1},{4,6},{5,7},{6,4},{7,5},{8,10},{9,11},{10,... | collective-permute-start | bytes 786440 | tf_op jit(solution)/shard_map/ppermute | solution.py:710
  105.0 4.6 %collective-permute-start.41 = (f32[4,768]{1,0:T(4,128)S(1)}, f32[4,768]{1,0:T(4,128)S(1)}, u32[]{:S(2)}, u32[]{:S(2)}) collective-permute-start(f32[4,768]{1,0:T(4,128)S(1)} %pad_maximum_fusion.4.refs_1__0_), channel_id=1, source_target_pairs={{0,2},{1,3},{2,4},{3,5},{4,6},{5,7},{6,0},{7,1},{8,10},{9,11},{10,... | collective-permute-start | bytes 36872 | tf_op jit(solution)/shard_map/ppermute | solution.py:681
  112.4 8.7 %collective-permute-start.42 = (f32[128,512]{1,0:T(8,128)S(1)}, f32[128,512]{1,0:T(8,128)S(1)}, u32[]{:S(2)}, u32[]{:S(2)}) collective-permute-start(f32[128,512]{1,0:T(8,128)S(1)} %get-tuple-element.321), channel_id=1, source_target_pairs={{0,8},{8,0},{16,24},{24,16},{1,9},{9,1},{17,25},{25,17},{2,10},{10... | collective-permute-start | bytes 786440 | tf_op jit(solution)/shard_map/ppermute | solution.py:710
  122.4 18.2 %collective-permute-start.45 = (f32[320,256]{1,0:T(8,128)S(1)}, f32[320,256]{1,0:T(8,128)S(1)}, u32[]{:S(2)}, u32[]{:S(2)}) collective-permute-start(f32[320,256]{1,0:T(8,128)S(1)} %get-tuple-element.350), channel_id=1, source_target_pairs={{0,2},{1,3},{2,0},{3,1},{4,6},{5,7},{6,4},{7,5},{8,10},{9,11},{10,... | collective-permute-start | bytes 983048 | tf_op jit(solution)/shard_map/ppermute | solution.py:710
  125.3 15.3 %collective-permute-start.46 = (f32[320,256]{1,0:T(8,128)S(1)}, f32[320,256]{1,0:T(8,128)S(1)}, u32[]{:S(2)}, u32[]{:S(2)}) collective-permute-start(f32[320,256]{1,0:T(8,128)S(1)} %get-tuple-element.352), channel_id=1, source_target_pairs={{0,4},{1,5},{2,6},{3,7},{4,0},{5,1},{6,2},{7,3},{8,12},{9,13},{10,... | collective-permute-start | bytes 983048 | tf_op jit(solution)/shard_map/ppermute | solution.py:710
  126.2 14.4 %collective-permute-start.44 = (f32[128,512]{1,0:T(8,128)S(1)}, f32[128,512]{1,0:T(8,128)S(1)}, u32[]{:S(2)}, u32[]{:S(2)}) collective-permute-start(f32[128,512]{1,0:T(8,128)S(1)} %add_two.4.own), channel_id=1, source_target_pairs={{0,16},{8,24},{16,0},{24,8},{1,17},{9,25},{17,1},{25,9},{2,18},{10... | collective-permute-start | bytes 786440 | tf_op jit(solution)/shard_map/ppermute | solution.py:710
  127.5 13.2 %collective-permute-start.48 = (f32[192,256]{1,0:T(8,128)S(1)}, f32[192,256]{1,0:T(8,128)S(1)}, u32[]{:S(2)}, u32[]{:S(2)}) collective-permute-start(f32[192,256]{1,0:T(8,128)S(1)} %get-tuple-element.357), channel_id=1, source_target_pairs={{0,2},{1,3},{2,0},{3,1},{4,6},{5,7},{6,4},{7,5},{8,10},{9,11},{10,... | collective-permute-start | bytes 589832 | tf_op jit(solution)/shard_map/ppermute | solution.py:710
  128.2 12.4 %collective-permute-start.49 = (f32[192,256]{1,0:T(8,128)S(1)}, f32[192,256]{1,0:T(8,128)S(1)}, u32[]{:S(2)}, u32[]{:S(2)}) collective-permute-start(f32[192,256]{1,0:T(8,128)S(1)} %get-tuple-element.359), channel_id=1, source_target_pairs={{0,4},{1,5},{2,6},{3,7},{4,0},{5,1},{6,2},{7,3},{8,12},{9,13},{10,... | collective-permute-start | bytes 589832 | tf_op jit(solution)/shard_map/ppermute | solution.py:710
  140.7 8.3 %collective-permute-start.50 = (f32[128,512]{1,0:T(8,128)S(1)}, f32[128,512]{1,0:T(8,128)S(1)}, u32[]{:S(2)}, u32[]{:S(2)}) collective-permute-start(f32[128,512]{1,0:T(8,128)S(1)} %add_two.5.own), channel_id=1, source_target_pairs={{0,8},{8,0},{16,24},{24,16},{1,9},{9,1},{17,25},{25,17},{2,10},{10... | collective-permute-start | bytes 786440 | tf_op jit(solution)/shard_map/ppermute | solution.py:710
  141.4 8.3 %collective-permute-start.51 = (f32[256,256]{1,0:T(8,128)S(1)}, f32[256,256]{1,0:T(8,128)S(1)}, u32[]{:S(2)}, u32[]{:S(2)}) collective-permute-start(f32[256,256]{1,0:T(8,128)S(1)} %get-tuple-element.371), channel_id=1, source_target_pairs={{0,4},{1,5},{2,6},{3,7},{4,0},{5,1},{6,2},{7,3},{8,12},{9,13},{10,... | collective-permute-start | bytes 786440 | tf_op jit(solution)/shard_map/ppermute | solution.py:710
  142.6 7.9 %collective-permute-start.52 = (f32[256,256]{1,0:T(8,128)S(1)}, f32[256,256]{1,0:T(8,128)S(1)}, u32[]{:S(2)}, u32[]{:S(2)}) collective-permute-start(f32[256,256]{1,0:T(8,128)S(1)} %get-tuple-element.373), channel_id=1, source_target_pairs={{0,2},{1,3},{2,0},{3,1},{4,6},{5,7},{6,4},{7,5},{8,10},{9,11},{10,... | collective-permute-start | bytes 786440 | tf_op jit(solution)/shard_map/ppermute | solution.py:710
  151.2 7.1 %collective-permute-start.53 = (f32[256,256]{1,0:T(8,128)S(1)}, f32[256,256]{1,0:T(8,128)S(1)}, u32[]{:S(2)}, u32[]{:S(2)}) collective-permute-start(f32[256,256]{1,0:T(8,128)S(1)} %get-tuple-element.384.refs_0_), channel_id=1, source_target_pairs={{0,4},{1,5},{2,6},{3,7},{4,0},{5,1},{6,2},{7,3},{8,12},{9,13},{10,... | collective-permute-start | bytes 786440 | tf_op jit(solution)/shard_map/ppermute | solution.py:710
  152.1 6.8 %collective-permute-start.54 = (f32[256,256]{1,0:T(8,128)S(1)}, f32[256,256]{1,0:T(8,128)S(1)}, u32[]{:S(2)}, u32[]{:S(2)}) collective-permute-start(f32[256,256]{1,0:T(8,128)S(1)} %get-tuple-element.386.refs_2_), channel_id=1, source_target_pairs={{0,2},{1,3},{2,0},{3,1},{4,6},{5,7},{6,4},{7,5},{8,10},{9,11},{10,... | collective-permute-start | bytes 786440 | tf_op jit(solution)/shard_map/ppermute | solution.py:710
  153.0 6.6 %collective-permute-start.55 = (f32[128,512]{1,0:T(8,128)S(1)}, f32[128,512]{1,0:T(8,128)S(1)}, u32[]{:S(2)}, u32[]{:S(2)}) collective-permute-start(f32[128,512]{1,0:T(8,128)S(1)} %get-tuple-element.383), channel_id=1, source_target_pairs={{0,8},{8,0},{16,24},{24,16},{1,9},{9,1},{17,25},{25,17},{2,10},{10... | collective-permute-start | bytes 786440 | tf_op jit(solution)/shard_map/ppermute | solution.py:710
  160.2 14.6 %collective-permute-start.56 = (f32[512,256]{1,0:T(8,128)S(1)}, f32[512,256]{1,0:T(8,128)S(1)}, u32[]{:S(2)}, u32[]{:S(2)}) collective-permute-start(f32[512,256]{1,0:T(8,128)S(1)} %get-tuple-element.415.refs_0_), channel_id=1, source_target_pairs={{0,2},{1,3},{2,0},{3,1},{4,6},{5,7},{6,4},{7,5},{8,10},{9,11},{10,... | collective-permute-start | bytes 1572872 | tf_op jit(solution)/shard_map/ppermute | solution.py:710
  162.0 12.8 %collective-permute-start.57 = (f32[512,256]{1,0:T(8,128)S(1)}, f32[512,256]{1,0:T(8,128)S(1)}, u32[]{:S(2)}, u32[]{:S(2)}) collective-permute-start(f32[512,256]{1,0:T(8,128)S(1)} %get-tuple-element.417.refs_2_), channel_id=1, source_target_pairs={{0,4},{1,5},{2,6},{3,7},{4,0},{5,1},{6,2},{7,3},{8,12},{9,13},{10,... | collective-permute-start | bytes 1572872 | tf_op jit(solution)/shard_map/ppermute | solution.py:710
  163.2 11.6 %collective-permute-start.58 = (f32[128,512]{1,0:T(8,128)S(1)}, f32[128,512]{1,0:T(8,128)S(1)}, u32[]{:S(2)}, u32[]{:S(2)}) collective-permute-start(f32[128,512]{1,0:T(8,128)S(1)} %add_two.6.own), channel_id=1, source_target_pairs={{0,16},{8,24},{16,0},{24,8},{1,17},{9,25},{17,1},{25,9},{2,18},{10... | collective-permute-start | bytes 786440 | tf_op jit(solution)/shard_map/ppermute | solution.py:710
  174.8 8.3 %collective-permute-start.59 = (f32[128,512]{1,0:T(8,128)S(1)}, f32[128,512]{1,0:T(8,128)S(1)}, u32[]{:S(2)}, u32[]{:S(2)}) collective-permute-start(f32[128,512]{1,0:T(8,128)S(1)} %add_two.7.own), channel_id=1, source_target_pairs={{0,8},{8,0},{16,24},{24,16},{1,9},{9,1},{17,25},{25,17},{2,10},{10... | collective-permute-start | bytes 786440 | tf_op jit(solution)/shard_map/ppermute | solution.py:710
  178.1 5.0 %collective-permute-start.61 = (f32[24,512]{1,0:T(8,128)S(1)}, f32[24,512]{1,0:T(8,128)S(1)}, u32[]{:S(2)}, u32[]{:S(2)}) collective-permute-start(f32[24,512]{1,0:T(8,128)S(1)} %add.77), channel_id=1, source_target_pairs={{0,2},{1,3},{2,4},{3,5},{4,6},{5,7},{6,0},{7,1},{8,10},{9,11},{10,... | collective-permute-start | bytes 147464 | tf_op jit(solution)/shard_map/ppermute | solution.py:681
  184.4 18.2 %collective-permute-start.72 = (f32[1024,512]{1,0:T(8,128)S(1)}, f32[1024,512]{1,0:T(8,128)S(1)}, u32[]{:S(2)}, u32[]{:S(2)}) collective-permute-start(f32[1024,512]{1,0:T(8,128)S(1)} %unfold_sides.6.refs_0_), channel_id=1, source_target_pairs={{0,1},{1,0},{2,3},{3,2},{4,5},{5,4},{6,7},{7,6},{8,9},{9,8},{10,11... | collective-permute-start | bytes 6291464 | tf_op jit(solution)/shard_map/ppermute | solution.py:710
  184.5 10.7 %collective-permute-start.64 = (f32[256,256]{1,0:T(8,128)S(1)}, f32[256,256]{1,0:T(8,128)S(1)}, u32[]{:S(2)}, u32[]{:S(2)}) collective-permute-start(f32[256,256]{1,0:T(8,128)S(1)} %get-tuple-element.422.refs_0_), channel_id=1, source_target_pairs={{0,4},{1,5},{2,6},{3,7},{4,0},{5,1},{6,2},{7,3},{8,12},{9,13},{10,... | collective-permute-start | bytes 786440 | tf_op jit(solution)/shard_map/ppermute | solution.py:710
  185.4 9.7 %collective-permute-start.65 = (f32[256,256]{1,0:T(8,128)S(1)}, f32[256,256]{1,0:T(8,128)S(1)}, u32[]{:S(2)}, u32[]{:S(2)}) collective-permute-start(f32[256,256]{1,0:T(8,128)S(1)} %get-tuple-element.424.refs_2_), channel_id=1, source_target_pairs={{0,2},{1,3},{2,0},{3,1},{4,6},{5,7},{6,4},{7,5},{8,10},{9,11},{10,... | collective-permute-start | bytes 786440 | tf_op jit(solution)/shard_map/ppermute | solution.py:710
  190.1 5.1 %collective-permute-start.67 = (f32[24,512]{1,0:T(8,128)S(1)}, f32[24,512]{1,0:T(8,128)S(1)}, u32[]{:S(2)}, u32[]{:S(2)}) collective-permute-start(f32[24,512]{1,0:T(8,128)S(1)} %add.81), channel_id=1, source_target_pairs={{0,16},{8,24},{16,0},{24,8},{1,17},{9,25},{17,1},{25,9},{2,18},{10... | collective-permute-start | bytes 147464 | tf_op jit(solution)/shard_map/ppermute | solution.py:710
  195.8 12.0 %collective-permute-start.68 = (f32[512,256]{1,0:T(8,128)S(1)}, f32[512,256]{1,0:T(8,128)S(1)}, u32[]{:S(2)}, u32[]{:S(2)}) collective-permute-start(f32[512,256]{1,0:T(8,128)S(1)} %get-tuple-element.453.refs_0_), channel_id=1, source_target_pairs={{0,2},{1,3},{2,0},{3,1},{4,6},{5,7},{6,4},{7,5},{8,10},{9,11},{10,... | collective-permute-start | bytes 1572872 | tf_op jit(solution)/shard_map/ppermute | solution.py:710
  197.4 11.6 %collective-permute-start.69 = (f32[512,256]{1,0:T(8,128)S(1)}, f32[512,256]{1,0:T(8,128)S(1)}, u32[]{:S(2)}, u32[]{:S(2)}) collective-permute-start(f32[512,256]{1,0:T(8,128)S(1)} %get-tuple-element.454.refs_2_), channel_id=1, source_target_pairs={{0,4},{1,5},{2,6},{3,7},{4,0},{5,1},{6,2},{7,3},{8,12},{9,13},{10,... | collective-permute-start | bytes 1572872 | tf_op jit(solution)/shard_map/ppermute | solution.py:710
  198.6 10.5 %collective-permute-start.70 = (f32[512,256]{1,0:T(8,128)S(1)}, f32[512,256]{1,0:T(8,128)S(1)}, u32[]{:S(2)}, u32[]{:S(2)}) collective-permute-start(f32[512,256]{1,0:T(8,128)S(1)} %get-tuple-element.453.refs_0_), channel_id=1, source_target_pairs={{0,1},{1,0},{2,3},{3,2},{4,5},{5,4},{6,7},{7,6},{8,9},{9,8},{10,11... | collective-permute-start | bytes 1572872 | tf_op jit(solution)/shard_map/ppermute | solution.py:710
  198.6 10.5 %collective-permute-start.71 = (f32[512,256]{1,0:T(8,128)S(1)}, f32[512,256]{1,0:T(8,128)S(1)}, u32[]{:S(2)}, u32[]{:S(2)}) collective-permute-start(f32[512,256]{1,0:T(8,128)S(1)} %get-tuple-element.454.refs_2_), channel_id=1, source_target_pairs={{0,1},{1,0},{2,3},{3,2},{4,5},{5,4},{6,7},{7,6},{8,9},{9,8},{10,11... | collective-permute-start | bytes 1572872 | tf_op jit(solution)/shard_map/ppermute | solution.py:710
  (36 other events, 200.3 us)

commit v5 on v3

--- a/solution.py
+++ b/solution.py
@@ -37,7 +37,7 @@
     def one(index, carry):
         return body(pl.multiple_of(index * step, step), carry)
 
-    return lax.fori_loop(0, count // step, one, init, unroll=2)
+    return lax.fori_loop(0, count // step, one, init, unroll=4)
 
 
 def documents(here, batches, span, count):

time: 215 us -> 215 us (level)
  no operation moved by 1% of the time
where the time goes in v5:
time: 215 us
  waiting for transfers between devices  89.7 us (42%)
  starting transfers between devices  70.7 us (33%)
  Pallas kernels  46.7 us (22%)
  local copies, waits for them, and re-layouts  4.39 us (2%)
  other arithmetic  2.39 us (1%)
    ppermute x40, waiting for transfers between devices, swap(): lax.ppermute(value, axis, [(i, i ^ bit) for i in range(lax.axis_size(axis...  52 us
    pallas_call x33, Pallas kernels, run(): pl.pallas_call(body, name=name, out_shape=tuple((jax.ShapeDtypeStruct(*ou...  39.6 us
    ppermute x35, starting transfers between devices, shifted(): return lax.ppermute(value, name, pairs)  39.2 us
    ppermute x35, waiting for transfers between devices, shifted(): return lax.ppermute(value, name, pairs)  37.7 us
    ppermute x40, starting transfers between devices, swap(): lax.ppermute(value, axis, [(i, i ^ bit) for i in range(lax.axis_size(axis...  31.6 us
    pallas_call x3, Pallas kernels, put_in_place(): pl.pallas_call(body, name='put_in_place', out_shape=tuple((jax.ShapeDtype...  7.07 us
  transfers between devices with their start and end apart: 75, of which 49 were waited for; matrix products, arithmetic and copies ran while one was open for 2% of the time, Pallas kernels for 9%

profile of v5, /device:TPU:0, one launch (start us, length us, event | category | flops | bytes accessed | tf_op | source)
XLA Modules:
  0.0 215.1 jit_solution(13871403182639758088)
XLA Ops:
  4.2 3.8 %collective-permute-start.3 = (f32[4,512]{1,0:T(4,128)S(1)}, f32[4,512]{1,0:T(4,128)S(1)}, u32[]{:S(2)}, u32[]{:S(2)}) collective-permute-start(f32[4,512]{1,0:T(4,128)S(1)} %add.63), channel_id=1, source_target_pairs={{0,6},{1,7},{2,0},{3,1},{4,2},{5,3},{6,4},{7,5},{8,14},{9,15},{10,... | collective-permute-start | bytes 24584 | tf_op jit(solution)/shard_map/ppermute | solution.py:681
  9.9 1.8 collective-permute-done.2
  13.0 3.6 %collective-permute-start.6 = (f32[4,512]{1,0:T(4,128)S(1)}, f32[4,512]{1,0:T(4,128)S(1)}, u32[]{:S(2)}, u32[]{:S(2)}) collective-permute-start(f32[4,512]{1,0:T(4,128)S(1)} %add_add_fusion.3.stats_0_), channel_id=1, source_target_pairs={{0,24},{8,0},{16,8},{24,16},{1,25},{9,1},{17,9},{25,17},{2,26},{10... | collective-permute-start | bytes 24584 | tf_op jit(solution)/shard_map/ppermute | solution.py:681
  18.7 2.5 %collective-permute-done.5.stats_2_ = f32[4,512]{1,0:T(4,128)S(1)} collective-permute-done((f32[4,512]{1,0:T(4,128)S(1)}, f32[4,512]{1,0:T(4,128)S(1)}, u32[]{:S(2)}, u32[]{:S(2)}) %collective-permute-start.5) | collective-permute-done | bytes 8224 | tf_op jit(solution)/shard_map/ppermute | solution.py:681
  22.1 1.9 enter_layer.2
  25.4 1.5 collective-permute-start.9
  26.9 1.9 collective-permute-start.8
  29.1 2.4 %collective-permute-done.8.ends_1_ = f32[4,768]{1,0:T(4,128)S(1)} collective-permute-done((f32[4,768]{1,0:T(4,128)S(1)}, f32[4,768]{1,0:T(4,128)S(1)}, u32[]{:S(2)}, u32[]{:S(2)}) %collective-permute-start.8) | collective-permute-done | bytes 12320 | tf_op jit(solution)/shard_map/ppermute | solution.py:681
  32.7 3.6 %middle_forward.1 = (f32[528,768]{1,0:T(8,128)S(1)}, bf16[512,768]{1,0:T(8,128)(2,1)S(1)}, bf16[512,512]{1,0:T(8,128)(2,1)S(1)}, f32[512,512]{1,0:T(8,128)S(1)},...) custom-call(s32[10]{0:T(128)S(1)} %pad_add_fusion.place.here.refs_0_, ...), custom_call_target="tpu_custom_call" | custom-call | tf_op jit(solution)/shard_map/middle_forward/pallas_call | solution.py:609
  42.2 2.4 %collective-permute-done.12 = f32[4,512]{1,0:T(4,128)S(1)} collective-permute-done((f32[4,512]{1,0:T(4,128)S(1)}, f32[4,512]{1,0:T(4,128)S(1)}, u32[]{:S(2)}, u32[]{:S(2)}) %collective-permute-start.12) | collective-permute-done | bytes 8224 | tf_op jit(solution)/shard_map/ppermute | solution.py:681
  45.9 2.0 collective-permute-start.15
  49.8 1.5 collective-permute-done.15.stats_1_
  51.3 1.9 enter_layer.3
  55.2 2.8 %collective-permute-start.19 = (f32[4,768]{1,0:T(4,128)S(1)}, f32[4,768]{1,0:T(4,128)S(1)}, u32[]{:S(2)}, u32[]{:S(2)}) collective-permute-start(f32[4,768]{1,0:T(4,128)S(1)} %pad_maximum_fusion.2.ends_0_), channel_id=1, source_target_pairs={{0,6},{1,7},{2,0},{3,1},{4,2},{5,3},{6,4},{7,5},{8,14},{9,15},{10,... | collective-permute-start | bytes 36872 | tf_op jit(solution)/shard_map/ppermute | solution.py:681
  59.7 5.9 %turn_around.1 = (bf16[512,512]{1,0:T(8,128)(2,1)S(1)}, f32[528,768]{1,0:T(8,128)S(1)}, bf16[512,768]{1,0:T(8,128)(2,1)S(1)}, bf16[512,512]{1,0:T(8,128)(2,1)S(1...) custom-call(s32[10]{0:T(128)S(1)} %pad_add_fusion.place.here.refs_0_, ...), custom_call_target="tpu_custom_call" | custom-call | tf_op jit(solution)/shard_map/turn_around/pallas_call | solution.py:609
  66.8 2.9 %collective-permute-start.25 = (f32[4,768]{1,0:T(4,128)S(1)}, f32[4,768]{1,0:T(4,128)S(1)}, u32[]{:S(2)}, u32[]{:S(2)}) collective-permute-start(f32[4,768]{1,0:T(4,128)S(1)} %pad_maximum_fusion.3.ends_0_), channel_id=1, source_target_pairs={{0,6},{1,7},{2,0},{3,1},{4,2},{5,3},{6,4},{7,5},{8,14},{9,15},{10,... | collective-permute-start | bytes 36872 | tf_op jit(solution)/shard_map/ppermute | solution.py:681
  69.8 1.5 collective-permute-start.24
  71.5 2.0 collective-permute-done.24.ends_2_
  73.5 2.4 %collective-permute-done.23.ends_1_ = f32[4,768]{1,0:T(4,128)S(1)} collective-permute-done((f32[4,768]{1,0:T(4,128)S(1)}, f32[4,768]{1,0:T(4,128)S(1)}, u32[]{:S(2)}, u32[]{:S(2)}) %collective-permute-start.23) | collective-permute-done | bytes 12320 | tf_op jit(solution)/shard_map/ppermute | solution.py:681
  75.9 2.8 %backward_finish.2 = (bf16[512,768]{1,0:T(8,128)(2,1)S(1)}, f32[512,512]{1,0:T(8,128)S(1)}, f32[4,512]{1,0:T(4,128)S(1)}, f32[8,512]{1,0:T(8,128)S(1)}) custom-call(s32[10]{0:T(128)S(1)} %pad_add_fusion.place.here.refs_0_, f32[4,768]{1,0:T(4,128)S(1)} %pad_maximum_fusion.3.ends_0_, f32[4,768]{1,0:T(4,128)S(1)} %collective-permute-done.23.ends_1_, ...), custom_call_target="tpu_custom_call" | custom-call | tf_op jit(solution)/shard_map/backward_finish/pallas_call | solution.py:609
  78.7 1.8 all_weights.1
  81.7 2.0 collective-permute-start.27
  88.3 1.5 collective-permute-start.32
  93.5 2.2 %collective-permute-done.34.stats_2_ = f32[4,512]{1,0:T(4,128)S(1)} collective-permute-done((f32[4,512]{1,0:T(4,128)S(1)}, f32[4,512]{1,0:T(4,128)S(1)}, u32[]{:S(2)}, u32[]{:S(2)}) %collective-permute-start.34) | collective-permute-done | bytes 8224 | tf_op jit(solution)/shard_map/ppermute | solution.py:681
  96.9 3.5 %between_layers.1 = (f32[512,512]{1,0:T(8,128)S(1)}, f32[2,512]{1,0:T(2,128)S(1)}, bf16[512,512]{1,0:T(8,128)(2,1)S(1)}, f32[512,512]{1,0:T(8,128)S(1)}, bf16[51...) custom-call(s32[10]{0:T(128)S(1)} %pad_add_fusion.place.here.refs_0_, ...), custom_call_target="tpu_custom_call" | custom-call | tf_op jit(solution)/shard_map/between_layers/pallas_call | solution.py:609
  101.1 1.6 collective-permute-start.36
  106.4 2.3 %collective-permute-start.39 = (f32[4,768]{1,0:T(4,128)S(1)}, f32[4,768]{1,0:T(4,128)S(1)}, u32[]{:S(2)}, u32[]{:S(2)}) collective-permute-start(f32[4,768]{1,0:T(4,128)S(1)} %pad_maximum_fusion.4.refs_1__0_), channel_id=1, source_target_pairs={{0,6},{1,7},{2,0},{3,1},{4,2},{5,3},{6,4},{7,5},{8,14},{9,15},{10,... | collective-permute-start | bytes 36872 | tf_op jit(solution)/shard_map/ppermute | solution.py:681
  112.5 2.8 %backward_finish.3 = (bf16[512,768]{1,0:T(8,128)(2,1)S(1)}, f32[512,512]{1,0:T(8,128)S(1)}, f32[24,512]{1,0:T(8,128)S(1)}) custom-call(s32[10]{0:T(128)S(1)} %pad_add_fusion.place.here.refs_0_, f32[4,768]{1,0:T(4,128)S(1)} %pad_maximum_fusion.4.refs_1__0_, f32[4,768]{1,0:T(4,128)S(1)} %collective-permute-done.39.refs_1__1_, ...), custom_call_target="tpu_custom_call" | custom-call | tf_op jit(solution)/shard_map/backward_finish/pallas_call | solution.py:609
  116.0 5.0 %collective-permute-done.42.found = f32[128,512]{1,0:T(8,128)S(1)} collective-permute-done((f32[128,512]{1,0:T(8,128)S(1)}, f32[128,512]{1,0:T(8,128)S(1)}, u32[]{:S(2)}, u32[]{:S(2)}) %collective-permute-start.42) | collective-permute-done | bytes 262176 | tf_op jit(solution)/shard_map/ppermute | solution.py:710
  122.2 2.9 %collective-permute-start.45 = (f32[320,256]{1,0:T(8,128)S(1)}, f32[320,256]{1,0:T(8,128)S(1)}, u32[]{:S(2)}, u32[]{:S(2)}) collective-permute-start(f32[320,256]{1,0:T(8,128)S(1)} %get-tuple-element.350), channel_id=1, source_target_pairs={{0,2},{1,3},{2,0},{3,1},{4,6},{5,7},{6,4},{7,5},{8,10},{9,11},{10,... | collective-permute-start | bytes 983048 | tf_op jit(solution)/shard_map/ppermute | solution.py:710
  129.0 11.5 %collective-permute-done.44.found = f32[128,512]{1,0:T(8,128)S(1)} collective-permute-done((f32[128,512]{1,0:T(8,128)S(1)}, f32[128,512]{1,0:T(8,128)S(1)}, u32[]{:S(2)}, u32[]{:S(2)}) %collective-permute-start.44) | collective-permute-done | bytes 262176 | tf_op jit(solution)/shard_map/ppermute | solution.py:710
  142.8 6.1 %collective-permute-done.50.found = f32[128,512]{1,0:T(8,128)S(1)} collective-permute-done((f32[128,512]{1,0:T(8,128)S(1)}, f32[128,512]{1,0:T(8,128)S(1)}, u32[]{:S(2)}, u32[]{:S(2)}) %collective-permute-start.50) | collective-permute-done | bytes 262176 | tf_op jit(solution)/shard_map/ppermute | solution.py:710
  152.9 1.8 collective-permute-start.55
  154.7 3.5 %collective-permute-done.53.refs_1_ = f32[256,256]{1,0:T(8,128)S(1)} collective-permute-done((f32[256,256]{1,0:T(8,128)S(1)}, f32[256,256]{1,0:T(8,128)S(1)}, u32[]{:S(2)}, u32[]{:S(2)}) %collective-permute-start.53) | collective-permute-done | bytes 262176 | tf_op jit(solution)/shard_map/ppermute | solution.py:710
  160.1 1.8 collective-permute-start.56
  163.1 1.9 collective-permute-start.58
  164.9 9.7 %collective-permute-done.58.found = f32[128,512]{1,0:T(8,128)S(1)} collective-permute-done((f32[128,512]{1,0:T(8,128)S(1)}, f32[128,512]{1,0:T(8,128)S(1)}, u32[]{:S(2)}, u32[]{:S(2)}) %collective-permute-start.58) | collective-permute-done | bytes 262176 | tf_op jit(solution)/shard_map/ppermute | solution.py:710
  180.9 2.0 collective-permute-done.61
  185.8 2.0 collective-permute-start.66
  187.8 2.1 collective-permute-done.66
  189.9 2.2 %collective-permute-start.67 = (f32[24,512]{1,0:T(8,128)S(1)}, f32[24,512]{1,0:T(8,128)S(1)}, u32[]{:S(2)}, u32[]{:S(2)}) collective-permute-start(f32[24,512]{1,0:T(8,128)S(1)} %add.81), channel_id=1, source_target_pairs={{0,16},{8,24},{16,0},{24,8},{1,17},{9,25},{17,1},{25,9},{2,18},{10... | collective-permute-start | bytes 147464 | tf_op jit(solution)/shard_map/ppermute | solution.py:710
  193.2 1.7 collective-permute-done.67
  195.7 1.6 collective-permute-start.68
  199.0 1.5 last_step.1
  202.4 2.9 %put_in_place.3 = (f32[2,512,512]{2,1,0:T(8,128)}, f32[2,768,512]{2,1,0:T(8,128)}, f32[2,512,768]{2,1,0:T(8,128)}) custom-call(s32[10]{0:T(128)S(1)} %pad_add_fusion.place.here.refs_0_, f32[1024,512]{1,0:T(8,128)S(1)} %unfold_sides.6.refs_0_, f32[1024,512]{1,0:T(8,128)S(1)} %collective-permute-done.72.refs_1_), custom_call_target="tpu_custom_call" | custom-call | tf_op jit(solution)/shard_map/put_in_place/pallas_call | solution.py:655
  205.3 2.3 %collective-permute-done.68.refs_1_ = f32[512,256]{1,0:T(8,128)S(1)} collective-permute-done((f32[512,256]{1,0:T(8,128)S(1)}, f32[512,256]{1,0:T(8,128)S(1)}, u32[]{:S(2)}, u32[]{:S(2)}) %collective-permute-start.68) | collective-permute-done | bytes 524320 | tf_op jit(solution)/shard_map/ppermute | solution.py:710
  210.2 2.1 put_in_place.4
  213.0 2.1 put_in_place.5
  (182 shorter events, 78.1 us)
Async XLA Ops:
  4.2 5.7 %collective-permute-start.3 = (f32[4,512]{1,0:T(4,128)S(1)}, f32[4,512]{1,0:T(4,128)S(1)}, u32[]{:S(2)}, u32[]{:S(2)}) collective-permute-start(f32[4,512]{1,0:T(4,128)S(1)} %add.63), channel_id=1, source_target_pairs={{0,6},{1,7},{2,0},{3,1},{4,2},{5,3},{6,4},{7,5},{8,14},{9,15},{10,... | collective-permute-start | bytes 24584 | tf_op jit(solution)/shard_map/ppermute | solution.py:681
  8.5 4.5 %collective-permute-start.1 = (f32[4,512]{1,0:T(4,128)S(1)}, f32[4,512]{1,0:T(4,128)S(1)}, u32[]{:S(2)}, u32[]{:S(2)}) collective-permute-start(f32[4,512]{1,0:T(4,128)S(1)} %add.63), channel_id=1, source_target_pairs={{0,2},{1,3},{2,4},{3,5},{4,6},{5,7},{6,0},{7,1},{8,10},{9,11},{10,... | collective-permute-start | bytes 24584 | tf_op jit(solution)/shard_map/ppermute | solution.py:681
  13.0 5.7 %collective-permute-start.6 = (f32[4,512]{1,0:T(4,128)S(1)}, f32[4,512]{1,0:T(4,128)S(1)}, u32[]{:S(2)}, u32[]{:S(2)}) collective-permute-start(f32[4,512]{1,0:T(4,128)S(1)} %add_add_fusion.3.stats_0_), channel_id=1, source_target_pairs={{0,24},{8,0},{16,8},{24,16},{1,25},{9,1},{17,9},{25,17},{2,26},{10... | collective-permute-start | bytes 24584 | tf_op jit(solution)/shard_map/ppermute | solution.py:681
  16.6 4.5 %collective-permute-start.5 = (f32[4,512]{1,0:T(4,128)S(1)}, f32[4,512]{1,0:T(4,128)S(1)}, u32[]{:S(2)}, u32[]{:S(2)}) collective-permute-start(f32[4,512]{1,0:T(4,128)S(1)} %add_add_fusion.3.stats_0_), channel_id=1, source_target_pairs={{0,16},{8,24},{16,0},{24,8},{1,17},{9,25},{17,1},{25,9},{2,18},{10... | collective-permute-start | bytes 24584 | tf_op jit(solution)/shard_map/ppermute | solution.py:681
  16.6 5.4 %collective-permute-start.4 = (f32[4,512]{1,0:T(4,128)S(1)}, f32[4,512]{1,0:T(4,128)S(1)}, u32[]{:S(2)}, u32[]{:S(2)}) collective-permute-start(f32[4,512]{1,0:T(4,128)S(1)} %add_add_fusion.3.stats_0_), channel_id=1, source_target_pairs={{0,8},{8,16},{16,24},{24,0},{1,9},{9,17},{17,25},{25,1},{2,10},{10... | collective-permute-start | bytes 24584 | tf_op jit(solution)/shard_map/ppermute | solution.py:681
  26.9 4.6 %collective-permute-start.8 = (f32[4,768]{1,0:T(4,128)S(1)}, f32[4,768]{1,0:T(4,128)S(1)}, u32[]{:S(2)}, u32[]{:S(2)}) collective-permute-start(f32[4,768]{1,0:T(4,128)S(1)} %pad_maximum_fusion.1.ends_0_), channel_id=1, source_target_pairs={{0,2},{1,3},{2,4},{3,5},{4,6},{5,7},{6,0},{7,1},{8,10},{9,11},{10,... | collective-permute-start | bytes 36872 | tf_op jit(solution)/shard_map/ppermute | solution.py:681
  40.1 4.5 %collective-permute-start.12 = (f32[4,512]{1,0:T(4,128)S(1)}, f32[4,512]{1,0:T(4,128)S(1)}, u32[]{:S(2)}, u32[]{:S(2)}) collective-permute-start(f32[4,512]{1,0:T(4,128)S(1)} %add.69), channel_id=1, source_target_pairs={{0,2},{1,3},{2,4},{3,5},{4,6},{5,7},{6,0},{7,1},{8,10},{9,11},{10,... | collective-permute-start | bytes 24584 | tf_op jit(solution)/shard_map/ppermute | solution.py:681
  45.2 4.5 %collective-permute-start.16 = (f32[4,512]{1,0:T(4,128)S(1)}, f32[4,512]{1,0:T(4,128)S(1)}, u32[]{:S(2)}, u32[]{:S(2)}) collective-permute-start(f32[4,512]{1,0:T(4,128)S(1)} %add_add_fusion.2.stats_0_), channel_id=1, source_target_pairs={{0,16},{8,24},{16,0},{24,8},{1,17},{9,25},{17,1},{25,9},{2,18},{10... | collective-permute-start | bytes 24584 | tf_op jit(solution)/shard_map/ppermute | solution.py:681
  45.9 5.4 %collective-permute-start.15 = (f32[4,512]{1,0:T(4,128)S(1)}, f32[4,512]{1,0:T(4,128)S(1)}, u32[]{:S(2)}, u32[]{:S(2)}) collective-permute-start(f32[4,512]{1,0:T(4,128)S(1)} %add_add_fusion.2.stats_0_), channel_id=1, source_target_pairs={{0,8},{8,16},{16,24},{24,0},{1,9},{9,17},{17,25},{25,1},{2,10},{10... | collective-permute-start | bytes 24584 | tf_op jit(solution)/shard_map/ppermute | solution.py:681
  54.5 4.6 %collective-permute-start.21 = (f32[4,768]{1,0:T(4,128)S(1)}, f32[4,768]{1,0:T(4,128)S(1)}, u32[]{:S(2)}, u32[]{:S(2)}) collective-permute-start(f32[4,768]{1,0:T(4,128)S(1)} %pad_maximum_fusion.2.ends_0_), channel_id=1, source_target_pairs={{0,2},{1,3},{2,4},{3,5},{4,6},{5,7},{6,0},{7,1},{8,10},{9,11},{10,... | collective-permute-start | bytes 36872 | tf_op jit(solution)/shard_map/ppermute | solution.py:681
  54.5 4.6 %collective-permute-start.20 = (f32[4,768]{1,0:T(4,128)S(1)}, f32[4,768]{1,0:T(4,128)S(1)}, u32[]{:S(2)}, u32[]{:S(2)}) collective-permute-start(f32[4,768]{1,0:T(4,128)S(1)} %pad_maximum_fusion.2.ends_0_), channel_id=1, source_target_pairs={{0,4},{1,5},{2,6},{3,7},{4,0},{5,1},{6,2},{7,3},{8,12},{9,13},{10,... | collective-permute-start | bytes 36872 | tf_op jit(solution)/shard_map/ppermute | solution.py:681
  55.2 4.5 %collective-permute-start.19 = (f32[4,768]{1,0:T(4,128)S(1)}, f32[4,768]{1,0:T(4,128)S(1)}, u32[]{:S(2)}, u32[]{:S(2)}) collective-permute-start(f32[4,768]{1,0:T(4,128)S(1)} %pad_maximum_fusion.2.ends_0_), channel_id=1, source_target_pairs={{0,6},{1,7},{2,0},{3,1},{4,2},{5,3},{6,4},{7,5},{8,14},{9,15},{10,... | collective-permute-start | bytes 36872 | tf_op jit(solution)/shard_map/ppermute | solution.py:681
  66.8 4.7 %collective-permute-start.25 = (f32[4,768]{1,0:T(4,128)S(1)}, f32[4,768]{1,0:T(4,128)S(1)}, u32[]{:S(2)}, u32[]{:S(2)}) collective-permute-start(f32[4,768]{1,0:T(4,128)S(1)} %pad_maximum_fusion.3.ends_0_), channel_id=1, source_target_pairs={{0,6},{1,7},{2,0},{3,1},{4,2},{5,3},{6,4},{7,5},{8,14},{9,15},{10,... | collective-permute-start | bytes 36872 | tf_op jit(solution)/shard_map/ppermute | solution.py:681
  71.3 4.6 %collective-permute-start.23 = (f32[4,768]{1,0:T(4,128)S(1)}, f32[4,768]{1,0:T(4,128)S(1)}, u32[]{:S(2)}, u32[]{:S(2)}) collective-permute-start(f32[4,768]{1,0:T(4,128)S(1)} %pad_maximum_fusion.3.ends_0_), channel_id=1, source_target_pairs={{0,2},{1,3},{2,4},{3,5},{4,6},{5,7},{6,0},{7,1},{8,10},{9,11},{10,... | collective-permute-start | bytes 36872 | tf_op jit(solution)/shard_map/ppermute | solution.py:681
  80.6 5.7 %collective-permute-start.30 = (f32[1024,512]{1,0:T(8,128)S(1)}, f32[1024,512]{1,0:T(8,128)S(1)}, u32[]{:S(2)}, u32[]{:S(2)}) collective-permute-start(f32[1024,512]{1,0:T(8,128)S(1)} %get-tuple-element.278), channel_id=1, source_target_pairs={{0,1},{1,0},{2,3},{3,2},{4,5},{5,4},{6,7},{7,6},{8,9},{9,8},{10,11... | collective-permute-start | bytes 6291464 | tf_op jit(solution)/shard_map/ppermute | solution.py:710
  81.7 4.5 %collective-permute-start.27 = (f32[4,512]{1,0:T(4,128)S(1)}, f32[4,512]{1,0:T(4,128)S(1)}, u32[]{:S(2)}, u32[]{:S(2)}) collective-permute-start(f32[4,512]{1,0:T(4,128)S(1)} %add.73), channel_id=1, source_target_pairs={{0,2},{1,3},{2,4},{3,5},{4,6},{5,7},{6,0},{7,1},{8,10},{9,11},{10,... | collective-permute-start | bytes 24584 | tf_op jit(solution)/shard_map/ppermute | solution.py:681
  87.2 13.2 %collective-permute-start.31 = (f32[512,256]{1,0:T(8,128)S(1)}, f32[512,256]{1,0:T(8,128)S(1)}, u32[]{:S(2)}, u32[]{:S(2)}) collective-permute-start(f32[512,256]{1,0:T(8,128)S(1)} %get-tuple-element.284), channel_id=1, source_target_pairs={{0,2},{1,3},{2,0},{3,1},{4,6},{5,7},{6,4},{7,5},{8,10},{9,11},{10,... | collective-permute-start | bytes 1572872 | tf_op jit(solution)/shard_map/ppermute | solution.py:710
  88.3 12.1 %collective-permute-start.32 = (f32[512,256]{1,0:T(8,128)S(1)}, f32[512,256]{1,0:T(8,128)S(1)}, u32[]{:S(2)}, u32[]{:S(2)}) collective-permute-start(f32[512,256]{1,0:T(8,128)S(1)} %get-tuple-element.286), channel_id=1, source_target_pairs={{0,4},{1,5},{2,6},{3,7},{4,0},{5,1},{6,2},{7,3},{8,12},{9,13},{10,... | collective-permute-start | bytes 1572872 | tf_op jit(solution)/shard_map/ppermute | solution.py:710
  91.2 4.6 %collective-permute-start.34 = (f32[4,512]{1,0:T(4,128)S(1)}, f32[4,512]{1,0:T(4,128)S(1)}, u32[]{:S(2)}, u32[]{:S(2)}) collective-permute-start(f32[4,512]{1,0:T(4,128)S(1)} %add_add_fusion.1.stats_0_), channel_id=1, source_target_pairs={{0,16},{8,24},{16,0},{24,8},{1,17},{9,25},{17,1},{25,9},{2,18},{10... | collective-permute-start | bytes 24584 | tf_op jit(solution)/shard_map/ppermute | solution.py:681
  91.4 5.4 %collective-permute-start.33 = (f32[4,512]{1,0:T(4,128)S(1)}, f32[4,512]{1,0:T(4,128)S(1)}, u32[]{:S(2)}, u32[]{:S(2)}) collective-permute-start(f32[4,512]{1,0:T(4,128)S(1)} %add_add_fusion.1.stats_0_), channel_id=1, source_target_pairs={{0,8},{8,16},{16,24},{24,0},{1,9},{9,17},{17,25},{25,1},{2,10},{10... | collective-permute-start | bytes 24584 | tf_op jit(solution)/shard_map/ppermute | solution.py:681
  101.1 9.1 %collective-permute-start.36 = (f32[256,256]{1,0:T(8,128)S(1)}, f32[256,256]{1,0:T(8,128)S(1)}, u32[]{:S(2)}, u32[]{:S(2)}) collective-permute-start(f32[256,256]{1,0:T(8,128)S(1)} %get-tuple-element.304), channel_id=1, source_target_pairs={{0,4},{1,5},{2,6},{3,7},{4,0},{5,1},{6,2},{7,3},{8,12},{9,13},{10,... | collective-permute-start | bytes 786440 | tf_op jit(solution)/shard_map/ppermute | solution.py:710
  102.7 7.5 %collective-permute-start.37 = (f32[256,256]{1,0:T(8,128)S(1)}, f32[256,256]{1,0:T(8,128)S(1)}, u32[]{:S(2)}, u32[]{:S(2)}) collective-permute-start(f32[256,256]{1,0:T(8,128)S(1)} %get-tuple-element.306), channel_id=1, source_target_pairs={{0,2},{1,3},{2,0},{3,1},{4,6},{5,7},{6,4},{7,5},{8,10},{9,11},{10,... | collective-permute-start | bytes 786440 | tf_op jit(solution)/shard_map/ppermute | solution.py:710
  104.9 4.6 %collective-permute-start.41 = (f32[4,768]{1,0:T(4,128)S(1)}, f32[4,768]{1,0:T(4,128)S(1)}, u32[]{:S(2)}, u32[]{:S(2)}) collective-permute-start(f32[4,768]{1,0:T(4,128)S(1)} %pad_maximum_fusion.4.refs_1__0_), channel_id=1, source_target_pairs={{0,2},{1,3},{2,4},{3,5},{4,6},{5,7},{6,0},{7,1},{8,10},{9,11},{10,... | collective-permute-start | bytes 36872 | tf_op jit(solution)/shard_map/ppermute | solution.py:681
  112.3 8.7 %collective-permute-start.42 = (f32[128,512]{1,0:T(8,128)S(1)}, f32[128,512]{1,0:T(8,128)S(1)}, u32[]{:S(2)}, u32[]{:S(2)}) collective-permute-start(f32[128,512]{1,0:T(8,128)S(1)} %get-tuple-element.321), channel_id=1, source_target_pairs={{0,8},{8,0},{16,24},{24,16},{1,9},{9,1},{17,25},{25,17},{2,10},{10... | collective-permute-start | bytes 786440 | tf_op jit(solution)/shard_map/ppermute | solution.py:710
  122.2 18.2 %collective-permute-start.45 = (f32[320,256]{1,0:T(8,128)S(1)}, f32[320,256]{1,0:T(8,128)S(1)}, u32[]{:S(2)}, u32[]{:S(2)}) collective-permute-start(f32[320,256]{1,0:T(8,128)S(1)} %get-tuple-element.350), channel_id=1, source_target_pairs={{0,2},{1,3},{2,0},{3,1},{4,6},{5,7},{6,4},{7,5},{8,10},{9,11},{10,... | collective-permute-start | bytes 983048 | tf_op jit(solution)/shard_map/ppermute | solution.py:710
  125.2 15.3 %collective-permute-start.46 = (f32[320,256]{1,0:T(8,128)S(1)}, f32[320,256]{1,0:T(8,128)S(1)}, u32[]{:S(2)}, u32[]{:S(2)}) collective-permute-start(f32[320,256]{1,0:T(8,128)S(1)} %get-tuple-element.352), channel_id=1, source_target_pairs={{0,4},{1,5},{2,6},{3,7},{4,0},{5,1},{6,2},{7,3},{8,12},{9,13},{10,... | collective-permute-start | bytes 983048 | tf_op jit(solution)/shard_map/ppermute | solution.py:710
  126.1 14.4 %collective-permute-start.44 = (f32[128,512]{1,0:T(8,128)S(1)}, f32[128,512]{1,0:T(8,128)S(1)}, u32[]{:S(2)}, u32[]{:S(2)}) collective-permute-start(f32[128,512]{1,0:T(8,128)S(1)} %add_two.4.own), channel_id=1, source_target_pairs={{0,16},{8,24},{16,0},{24,8},{1,17},{9,25},{17,1},{25,9},{2,18},{10... | collective-permute-start | bytes 786440 | tf_op jit(solution)/shard_map/ppermute | solution.py:710
  127.3 13.1 %collective-permute-start.48 = (f32[192,256]{1,0:T(8,128)S(1)}, f32[192,256]{1,0:T(8,128)S(1)}, u32[]{:S(2)}, u32[]{:S(2)}) collective-permute-start(f32[192,256]{1,0:T(8,128)S(1)} %get-tuple-element.357), channel_id=1, source_target_pairs={{0,2},{1,3},{2,0},{3,1},{4,6},{5,7},{6,4},{7,5},{8,10},{9,11},{10,... | collective-permute-start | bytes 589832 | tf_op jit(solution)/shard_map/ppermute | solution.py:710
  128.1 12.4 %collective-permute-start.49 = (f32[192,256]{1,0:T(8,128)S(1)}, f32[192,256]{1,0:T(8,128)S(1)}, u32[]{:S(2)}, u32[]{:S(2)}) collective-permute-start(f32[192,256]{1,0:T(8,128)S(1)} %get-tuple-element.359), channel_id=1, source_target_pairs={{0,4},{1,5},{2,6},{3,7},{4,0},{5,1},{6,2},{7,3},{8,12},{9,13},{10,... | collective-permute-start | bytes 589832 | tf_op jit(solution)/shard_map/ppermute | solution.py:710
  140.5 8.3 %collective-permute-start.50 = (f32[128,512]{1,0:T(8,128)S(1)}, f32[128,512]{1,0:T(8,128)S(1)}, u32[]{:S(2)}, u32[]{:S(2)}) collective-permute-start(f32[128,512]{1,0:T(8,128)S(1)} %add_two.5.own), channel_id=1, source_target_pairs={{0,8},{8,0},{16,24},{24,16},{1,9},{9,1},{17,25},{25,17},{2,10},{10... | collective-permute-start | bytes 786440 | tf_op jit(solution)/shard_map/ppermute | solution.py:710
  141.3 8.3 %collective-permute-start.51 = (f32[256,256]{1,0:T(8,128)S(1)}, f32[256,256]{1,0:T(8,128)S(1)}, u32[]{:S(2)}, u32[]{:S(2)}) collective-permute-start(f32[256,256]{1,0:T(8,128)S(1)} %get-tuple-element.371), channel_id=1, source_target_pairs={{0,4},{1,5},{2,6},{3,7},{4,0},{5,1},{6,2},{7,3},{8,12},{9,13},{10,... | collective-permute-start | bytes 786440 | tf_op jit(solution)/shard_map/ppermute | solution.py:710
  142.5 7.9 %collective-permute-start.52 = (f32[256,256]{1,0:T(8,128)S(1)}, f32[256,256]{1,0:T(8,128)S(1)}, u32[]{:S(2)}, u32[]{:S(2)}) collective-permute-start(f32[256,256]{1,0:T(8,128)S(1)} %get-tuple-element.373), channel_id=1, source_target_pairs={{0,2},{1,3},{2,0},{3,1},{4,6},{5,7},{6,4},{7,5},{8,10},{9,11},{10,... | collective-permute-start | bytes 786440 | tf_op jit(solution)/shard_map/ppermute | solution.py:710
  151.0 7.1 %collective-permute-start.53 = (f32[256,256]{1,0:T(8,128)S(1)}, f32[256,256]{1,0:T(8,128)S(1)}, u32[]{:S(2)}, u32[]{:S(2)}) collective-permute-start(f32[256,256]{1,0:T(8,128)S(1)} %get-tuple-element.384.refs_0_), channel_id=1, source_target_pairs={{0,4},{1,5},{2,6},{3,7},{4,0},{5,1},{6,2},{7,3},{8,12},{9,13},{10,... | collective-permute-start | bytes 786440 | tf_op jit(solution)/shard_map/ppermute | solution.py:710
  152.0 6.8 %collective-permute-start.54 = (f32[256,256]{1,0:T(8,128)S(1)}, f32[256,256]{1,0:T(8,128)S(1)}, u32[]{:S(2)}, u32[]{:S(2)}) collective-permute-start(f32[256,256]{1,0:T(8,128)S(1)} %get-tuple-element.386.refs_2_), channel_id=1, source_target_pairs={{0,2},{1,3},{2,0},{3,1},{4,6},{5,7},{6,4},{7,5},{8,10},{9,11},{10,... | collective-permute-start | bytes 786440 | tf_op jit(solution)/shard_map/ppermute | solution.py:710
  152.9 6.6 %collective-permute-start.55 = (f32[128,512]{1,0:T(8,128)S(1)}, f32[128,512]{1,0:T(8,128)S(1)}, u32[]{:S(2)}, u32[]{:S(2)}) collective-permute-start(f32[128,512]{1,0:T(8,128)S(1)} %get-tuple-element.383), channel_id=1, source_target_pairs={{0,8},{8,0},{16,24},{24,16},{1,9},{9,1},{17,25},{25,17},{2,10},{10... | collective-permute-start | bytes 786440 | tf_op jit(solution)/shard_map/ppermute | solution.py:710
  160.1 14.6 %collective-permute-start.56 = (f32[512,256]{1,0:T(8,128)S(1)}, f32[512,256]{1,0:T(8,128)S(1)}, u32[]{:S(2)}, u32[]{:S(2)}) collective-permute-start(f32[512,256]{1,0:T(8,128)S(1)} %get-tuple-element.415.refs_0_), channel_id=1, source_target_pairs={{0,2},{1,3},{2,0},{3,1},{4,6},{5,7},{6,4},{7,5},{8,10},{9,11},{10,... | collective-permute-start | bytes 1572872 | tf_op jit(solution)/shard_map/ppermute | solution.py:710
  161.9 12.8 %collective-permute-start.57 = (f32[512,256]{1,0:T(8,128)S(1)}, f32[512,256]{1,0:T(8,128)S(1)}, u32[]{:S(2)}, u32[]{:S(2)}) collective-permute-start(f32[512,256]{1,0:T(8,128)S(1)} %get-tuple-element.417.refs_2_), channel_id=1, source_target_pairs={{0,4},{1,5},{2,6},{3,7},{4,0},{5,1},{6,2},{7,3},{8,12},{9,13},{10,... | collective-permute-start | bytes 1572872 | tf_op jit(solution)/shard_map/ppermute | solution.py:710
  163.1 11.6 %collective-permute-start.58 = (f32[128,512]{1,0:T(8,128)S(1)}, f32[128,512]{1,0:T(8,128)S(1)}, u32[]{:S(2)}, u32[]{:S(2)}) collective-permute-start(f32[128,512]{1,0:T(8,128)S(1)} %add_two.6.own), channel_id=1, source_target_pairs={{0,16},{8,24},{16,0},{24,8},{1,17},{9,25},{17,1},{25,9},{2,18},{10... | collective-permute-start | bytes 786440 | tf_op jit(solution)/shard_map/ppermute | solution.py:710
  174.7 8.3 %collective-permute-start.59 = (f32[128,512]{1,0:T(8,128)S(1)}, f32[128,512]{1,0:T(8,128)S(1)}, u32[]{:S(2)}, u32[]{:S(2)}) collective-permute-start(f32[128,512]{1,0:T(8,128)S(1)} %add_two.7.own), channel_id=1, source_target_pairs={{0,8},{8,0},{16,24},{24,16},{1,9},{9,1},{17,25},{25,17},{2,10},{10... | collective-permute-start | bytes 786440 | tf_op jit(solution)/shard_map/ppermute | solution.py:710
  178.0 5.0 %collective-permute-start.61 = (f32[24,512]{1,0:T(8,128)S(1)}, f32[24,512]{1,0:T(8,128)S(1)}, u32[]{:S(2)}, u32[]{:S(2)}) collective-permute-start(f32[24,512]{1,0:T(8,128)S(1)} %add.77), channel_id=1, source_target_pairs={{0,2},{1,3},{2,4},{3,5},{4,6},{5,7},{6,0},{7,1},{8,10},{9,11},{10,... | collective-permute-start | bytes 147464 | tf_op jit(solution)/shard_map/ppermute | solution.py:681
  184.3 18.2 %collective-permute-start.72 = (f32[1024,512]{1,0:T(8,128)S(1)}, f32[1024,512]{1,0:T(8,128)S(1)}, u32[]{:S(2)}, u32[]{:S(2)}) collective-permute-start(f32[1024,512]{1,0:T(8,128)S(1)} %unfold_sides.6.refs_0_), channel_id=1, source_target_pairs={{0,1},{1,0},{2,3},{3,2},{4,5},{5,4},{6,7},{7,6},{8,9},{9,8},{10,11... | collective-permute-start | bytes 6291464 | tf_op jit(solution)/shard_map/ppermute | solution.py:710
  184.3 10.7 %collective-permute-start.64 = (f32[256,256]{1,0:T(8,128)S(1)}, f32[256,256]{1,0:T(8,128)S(1)}, u32[]{:S(2)}, u32[]{:S(2)}) collective-permute-start(f32[256,256]{1,0:T(8,128)S(1)} %get-tuple-element.422.refs_0_), channel_id=1, source_target_pairs={{0,4},{1,5},{2,6},{3,7},{4,0},{5,1},{6,2},{7,3},{8,12},{9,13},{10,... | collective-permute-start | bytes 786440 | tf_op jit(solution)/shard_map/ppermute | solution.py:710
  185.3 9.7 %collective-permute-start.65 = (f32[256,256]{1,0:T(8,128)S(1)}, f32[256,256]{1,0:T(8,128)S(1)}, u32[]{:S(2)}, u32[]{:S(2)}) collective-permute-start(f32[256,256]{1,0:T(8,128)S(1)} %get-tuple-element.424.refs_2_), channel_id=1, source_target_pairs={{0,2},{1,3},{2,0},{3,1},{4,6},{5,7},{6,4},{7,5},{8,10},{9,11},{10,... | collective-permute-start | bytes 786440 | tf_op jit(solution)/shard_map/ppermute | solution.py:710
  189.9 5.1 %collective-permute-start.67 = (f32[24,512]{1,0:T(8,128)S(1)}, f32[24,512]{1,0:T(8,128)S(1)}, u32[]{:S(2)}, u32[]{:S(2)}) collective-permute-start(f32[24,512]{1,0:T(8,128)S(1)} %add.81), channel_id=1, source_target_pairs={{0,16},{8,24},{16,0},{24,8},{1,17},{9,25},{17,1},{25,9},{2,18},{10... | collective-permute-start | bytes 147464 | tf_op jit(solution)/shard_map/ppermute | solution.py:710
  195.7 12.0 %collective-permute-start.68 = (f32[512,256]{1,0:T(8,128)S(1)}, f32[512,256]{1,0:T(8,128)S(1)}, u32[]{:S(2)}, u32[]{:S(2)}) collective-permute-start(f32[512,256]{1,0:T(8,128)S(1)} %get-tuple-element.453.refs_0_), channel_id=1, source_target_pairs={{0,2},{1,3},{2,0},{3,1},{4,6},{5,7},{6,4},{7,5},{8,10},{9,11},{10,... | collective-permute-start | bytes 1572872 | tf_op jit(solution)/shard_map/ppermute | solution.py:710
  197.3 11.6 %collective-permute-start.69 = (f32[512,256]{1,0:T(8,128)S(1)}, f32[512,256]{1,0:T(8,128)S(1)}, u32[]{:S(2)}, u32[]{:S(2)}) collective-permute-start(f32[512,256]{1,0:T(8,128)S(1)} %get-tuple-element.454.refs_2_), channel_id=1, source_target_pairs={{0,4},{1,5},{2,6},{3,7},{4,0},{5,1},{6,2},{7,3},{8,12},{9,13},{10,... | collective-permute-start | bytes 1572872 | tf_op jit(solution)/shard_map/ppermute | solution.py:710
  198.4 10.5 %collective-permute-start.70 = (f32[512,256]{1,0:T(8,128)S(1)}, f32[512,256]{1,0:T(8,128)S(1)}, u32[]{:S(2)}, u32[]{:S(2)}) collective-permute-start(f32[512,256]{1,0:T(8,128)S(1)} %get-tuple-element.453.refs_0_), channel_id=1, source_target_pairs={{0,1},{1,0},{2,3},{3,2},{4,5},{5,4},{6,7},{7,6},{8,9},{9,8},{10,11... | collective-permute-start | bytes 1572872 | tf_op jit(solution)/shard_map/ppermute | solution.py:710
  198.4 10.5 %collective-permute-start.71 = (f32[512,256]{1,0:T(8,128)S(1)}, f32[512,256]{1,0:T(8,128)S(1)}, u32[]{:S(2)}, u32[]{:S(2)}) collective-permute-start(f32[512,256]{1,0:T(8,128)S(1)} %get-tuple-element.454.refs_2_), channel_id=1, source_target_pairs={{0,1},{1,0},{2,3},{3,2},{4,5},{5,4},{6,7},{7,6},{8,9},{9,8},{10,11... | collective-permute-start | bytes 1572872 | tf_op jit(solution)/shard_map/ppermute | solution.py:710
  (36 other events, 200.0 us)
